TPU v7x, 128 devices: a whole 4x4x4 slice. The times are simulated.
128 devices in a mesh: ctx: 8 (over x, core), tp: 16 (over z, y).
Axes of the slice: x: 4, y: 4, z: 4, core: 2. Of those that a mesh axis runs over, the one named last changes fastest.
Arguments:
- tokens: bfloat16 [8192, 4096], P('ctx', 'tp')
- modality: int32 [8192], P('ctx'), may hold values from 0 to 2, as said below
- w_query: bfloat16 [3, 4096, 4096], P(None, None, 'tp')
- w_key: bfloat16 [3, 4096, 4096], P(None, None, 'tp'), may hold values from -0.09375 to 0.09375
- w_value: bfloat16 [3, 4096, 4096], P(None, None, 'tp'), may hold values from -0.09375 to 0.09375
- w_out: bfloat16 [3, 4096, 4096], P(None, 'tp'), may hold values from -0.5 to 0.5
Outputs:
- mixed: bfloat16 [8192, 4096], P('ctx', 'tp')
Inputs may be any that keep to these rules, and one draw needn't show every extreme that they name: In each aligned block of 1024 tokens (one index of ctx) the tokens of each modality form one contiguous run of at most 512 tokens; in every draw some block has a modality with exactly 512 tokens.
All inputs are finite; a program needn't handle non-finite values.
Results may differ from a plain program's by a relative error of at most 0.013.
Values may be sent and summed in bfloat16 or wider, within the bound.
No kernel may reach another device: no remote copies, remote signals or barrier semaphores. Data moves between devices by JAX's collectives and lax.ppermute only.
A program may use at most 128 MiB of HBM per device.

v0:
```python
import functools
import math

import jax
import jax.numpy as jnp
import numpy as np
from jax import lax
from jax.experimental import pallas as pl
from jax.experimental.pallas import tpu as pltpu
from jax.sharding import PartitionSpec as P

HD = 128
MODALITIES = 3
EPS = 1e-05
WINDOW = 528
ALIGN = 16
Q_TILE = 512
K_TILE = 1024
STATE_ROWS = HD + 16
AXES = ("ctx", "tp")
BF = jnp.bfloat16
F32 = jnp.float32
VMEM_PROJECT = 50 * 1024 * 1024
VMEM_BYTES = 24 * 1024 * 1024
FEATURES = 4096
SPAN = 256
HEADROOM = 2.0**-13


def plane_perm(first, step):
    pairs = []
    for ctx in range(8):
        for z in range(4):
            for y in range(4):
                along_y = (ctx % 2 == 0) == first
                to_z = z if along_y else (z + step) % 4
                to_y = (y + step) % 4 if along_y else y
                pairs.append((ctx * 16 + z * 4 + y, ctx * 16 + to_z * 4 + to_y))
    return pairs


def move(array, first, step):
    return lax.ppermute(array, AXES, plane_perm(first, step))


def move_x(array, step):
    pairs = [(x * 2 + c, ((x + step) % 4) * 2 + c) for x in range(4) for c in range(2)]
    return lax.ppermute(array, "ctx", pairs)


def swap_core(array):
    return lax.ppermute(array, "ctx", [(i, i ^ 1) for i in range(8)])


def shard_table(first_offsets, second_offsets):
    core = lax.axis_index("ctx") % 2
    tp = lax.axis_index("tp")
    z, y = tp // 4, tp % 4
    first_offsets = jnp.asarray(first_offsets, jnp.int32)
    second_offsets = jnp.asarray(second_offsets, jnp.int32)
    first = (jnp.where(core == 0, y, z) + first_offsets) % 4
    second = (jnp.where(core == 0, z, y) + second_offsets) % 4
    return jnp.where(core == 0, second * 4 + first, first * 4 + second).astype(jnp.int32)


def segment_scalars(modality):
    rows = modality.shape[0]
    kinds = jnp.arange(MODALITIES, dtype=jnp.int32)[:, None]
    member = modality[None, :] == kinds
    positions = jnp.arange(rows, dtype=jnp.int32)[None, :]
    begin = jnp.min(jnp.where(member, positions, rows), axis=1)
    end = jnp.max(jnp.where(member, positions + 1, 0), axis=1)
    end = jnp.maximum(end, begin)
    core = lax.axis_index("ctx") % 2
    return jnp.concatenate([begin, end, core[None]]).astype(jnp.int32)


def for_runs(seg_ref, rows, body):
    for kind in range(MODALITIES):
        begin = seg_ref[kind]
        end = seg_ref[MODALITIES + kind]
        first = jnp.minimum(begin // ALIGN * ALIGN, rows - WINDOW)
        first = pl.multiple_of(first, ALIGN)
        positions = first + lax.broadcasted_iota(jnp.int32, (WINDOW, 1), 0)
        body(kind, pl.ds(first, WINDOW), (positions >= begin) & (positions < end))


def constant_spec(shape):
    return pl.BlockSpec(shape, lambda k, *scalars: (0,) * len(shape))


def project(pieces, weights, table, seg, before=None, last=False):
    count = len(pieces)
    counts = [piece.shape[0] for piece in pieces]
    firsts = [sum(counts[:i]) for i in range(count)]
    depth = sum(counts)
    rows, width = pieces[0].shape[1:]
    out_width = 3 * width
    has_before = before is not None

    def kernel(table_ref, seg_ref, *refs):
        piece_refs = refs[:count]
        weight_refs = refs[count : count + 3]
        refs = refs[count + 3 :]
        if has_before:
            squares_before_ref, before_ref, *refs = refs
        if last:
            query_ref, kv_ref, query_send_ref, kv_send_ref, *refs = refs
        else:
            squares_ref, out_ref, *refs = refs
        held, normed, left, right, total, shrink, piece_sem, weight_sem, total_sem = refs

        spans = [pl.ds(row, SPAN) for row in range(0, rows, SPAN)]
        piece_copies = [
            pltpu.make_async_copy(
                piece_refs[i].at[:, span, :],
                held.at[pl.ds(firsts[i], counts[i]), span, :],
                piece_sem.at[k, i],
            )
            for k, span in enumerate(spans)
            for i in range(count)
        ]
        groups = ((0, 2 * width), (2 * width, out_width))
        weight_copies = ([], [])
        before_copies = ([], [])
        out_copies = []
        for g, (low, high) in enumerate(groups):
            columns = pl.ds(low, high - low)
            for j in range(depth):
                first = pl.multiple_of(table_ref[j] * width, width)
                for i in range(low // width, high // width):
                    weight_copies[g].append(
                        pltpu.make_async_copy(
                            weight_refs[i].at[:, pl.ds(first, width), :],
                            right.at[:, pl.ds(j * width, width), pl.ds(i * width, width)],
                            weight_sem.at[i, j],
                        )
                    )
            for k, span in enumerate(spans):
                if has_before:
                    before_copies[g].append(
                        pltpu.make_async_copy(
                            before_ref.at[span, columns],
                            total.at[span, columns],
                            total_sem.at[0, g, k],
                        )
                    )
                if not last:
                    out_copies.append(
                        pltpu.make_async_copy(
                            total.at[span, columns],
                            out_ref.at[span, columns],
                            total_sem.at[1, g, k],
                        )
                    )
        for copy in piece_copies:
            copy.start()
        for g in range(2):
            for copy in weight_copies[g] + before_copies[g]:
                copy.start()

        for row in range(0, rows, HD):
            at = slice(row, row + HD)
            if row % SPAN == 0:
                k = row // SPAN
                for copy in piece_copies[k * count : (k + 1) * count]:
                    copy.wait()
            by_lane = jnp.zeros((HD, HD), F32)
            for j in range(depth):
                for column in range(0, width, HD):
                    by_lane += jnp.square(held[j, at, column : column + HD].astype(F32))
            squares = jnp.sum(by_lane, axis=1, keepdims=True)
            if has_before:
                squares_before = squares_before_ref[at, :]
                scale_before = lax.rsqrt(squares_before / FEATURES + EPS)
                squares += squares_before
            scale = lax.rsqrt(squares / FEATURES + EPS)
            if has_before:
                shrink[at, :] = jnp.where(scale_before > 0.0, scale / scale_before, 0.0)
            if not last:
                squares_ref[at, :] = squares
            for j in range(depth):
                piece = held[j, at, :].astype(F32)
                normed[at, j * width : (j + 1) * width] = (piece * (scale * HEADROOM)).astype(BF)

        def mask(kind, at, keep):
            left[kind] = normed[at, :] * keep.astype(BF)

        for_runs(seg_ref, rows, mask)
        for g, (low, high) in enumerate(groups):
            for copy in weight_copies[g] + before_copies[g]:
                copy.wait()
            if has_before:
                total[:, low:high] *= shrink[...]
            else:
                total[:, low:high] = jnp.zeros((rows, high - low), F32)

            def run(kind, at, keep, low=low, high=high):
                total[at, low:high] += jnp.dot(
                    left[kind], right[kind, :, low:high], preferred_element_type=F32
                )

            for_runs(seg_ref, rows, run)
            if not last:
                for copy in out_copies[g * len(spans) : (g + 1) * len(spans)]:
                    copy.start()
        for copy in out_copies:
            copy.wait()

        if last:
            query_scale = math.log2(math.e) / math.sqrt(HD) / HEADROOM
            core = seg_ref[2 * MODALITIES]
            for mine in range(2):

                @pl.when(core == mine)
                def _(mine=mine):
                    for head, q_out, kv_out in (
                        (mine, query_ref, kv_ref),
                        (1 - mine, query_send_ref, kv_send_ref),
                    ):
                        at = head * HD
                        kv_out[:, :HD] = (total[:, at : at + HD] / HEADROOM).astype(BF)
                        at += width
                        for row in range(0, rows, HD):
                            block = total[row : row + HD, at : at + HD] / HEADROOM
                            kv_out[row : row + HD, HD:] = block.T.astype(BF)
                        at += width
                        q_out[...] = (total[:, at : at + HD] * query_scale).astype(BF)

    vmem = pl.BlockSpec(memory_space=pltpu.VMEM)
    operands = [table, seg, *pieces, *weights]
    in_specs = [pl.BlockSpec(memory_space=pltpu.SMEM)] * 2
    in_specs += [pl.BlockSpec(memory_space=pl.ANY)] * count
    in_specs += [pl.BlockSpec(memory_space=pl.ANY)] * 3
    if has_before:
        operands += before
        in_specs += [vmem, pl.BlockSpec(memory_space=pl.ANY)]
    if last:
        shapes = [(rows, HD), (rows, 2 * HD)] * 2
        out_shape = tuple(jax.ShapeDtypeStruct(shape, BF) for shape in shapes)
        out_specs = (vmem,) * 4
    else:
        out_shape = (
            jax.ShapeDtypeStruct((rows, 1), F32),
            jax.ShapeDtypeStruct((rows, 3 * width), F32),
        )
        out_specs = (vmem, pl.BlockSpec(memory_space=pl.ANY))
    return pl.pallas_call(
        kernel,
        in_specs=in_specs,
        out_specs=out_specs,
        scratch_shapes=[
            pltpu.VMEM((depth, rows, width), BF),
            pltpu.VMEM((rows, depth * width), BF),
            pltpu.VMEM((MODALITIES, WINDOW, depth * width), BF),
            pltpu.VMEM((MODALITIES, depth * width, 3 * width), BF),
            pltpu.VMEM((rows, out_width), F32),
            pltpu.VMEM((rows, 1), F32),
            pltpu.SemaphoreType.DMA((rows // SPAN, count)),
            pltpu.SemaphoreType.DMA((3, depth)),
            pltpu.SemaphoreType.DMA((2, 2, rows // SPAN)),
        ],
        out_shape=out_shape,
        compiler_params=pltpu.CompilerParams(vmem_limit_bytes=VMEM_PROJECT),
        cost_estimate=pl.CostEstimate(
            flops=2 * depth * 3 * WINDOW * width * 3 * width,
            bytes_accessed=depth * (rows * width * 2 + 9 * width * width * 2),
            transcendentals=0,
        ),
    )(*operands)


def score(query, key, keep=None):
    scores = lax.dot_general(key, query, (((1,), (1,)), ((), ())), preferred_element_type=F32)
    return scores if keep is None else jnp.where(keep, scores, -1e30)


def fold(state, scores, value_t):
    top, total, summed = state
    new_top = jnp.maximum(top, jnp.max(scores, axis=0, keepdims=True))
    factor = jnp.exp2(top - new_top)
    weights = jnp.exp2(scores - new_top)
    total = total * factor + jnp.sum(weights, axis=0, keepdims=True)
    summed = summed * factor + jnp.dot(value_t, weights.astype(BF), preferred_element_type=F32)
    return new_top, total, summed


def empty_state():
    return (
        jnp.full((1, Q_TILE), -1e30, F32),
        jnp.zeros((1, Q_TILE), F32),
        jnp.zeros((HD, Q_TILE), F32),
    )


def store_state(state, state_ref):
    top, total, summed = state
    state_ref[0, :HD, :] = summed
    state_ref[0, HD : HD + 8, :] = jnp.broadcast_to(top, (8, Q_TILE))
    state_ref[0, HD + 8 :, :] = jnp.broadcast_to(total, (8, Q_TILE))


def load_state(state_ref):
    return (
        state_ref[0, HD : HD + 1, :],
        state_ref[0, HD + 8 : HD + 9, :],
        state_ref[0, :HD, :],
    )


def read_keys(ref, first, count):
    key = ref[pl.ds(first, count), :HD]
    blocks = [ref[pl.ds(first + i, HD), HD:] for i in range(0, count, HD)]
    return key, jnp.concatenate(blocks, axis=1)


def attend_own(query, query_other, kv, kv_other, core):
    rows = query.shape[0]
    per_block = rows // Q_TILE
    tiles = 2 * per_block

    def kernel(core_ref, query_ref, query_other_ref, kv_ref, kv_other_ref, state_ref, keys, both):
        place = pl.program_id(0)

        @pl.when(place == 0)
        def _():
            for mine in range(2):

                @pl.when(core_ref[0] == mine)
                def _(mine=mine):
                    at, other = mine * rows, (1 - mine) * rows
                    keys[at : at + rows, :] = kv_ref[...]
                    keys[other : other + rows, :] = kv_other_ref[...]
                    both[at : at + rows, :] = query_ref[...]
                    both[other : other + rows, :] = query_other_ref[...]

        at = pl.multiple_of(place * Q_TILE, Q_TILE)
        q = both[pl.ds(at, Q_TILE), :]
        causal = lax.broadcasted_iota(
            jnp.int32, (Q_TILE, Q_TILE), 0
        ) <= lax.broadcasted_iota(jnp.int32, (Q_TILE, Q_TILE), 1)
        key, value_t = read_keys(keys, at, Q_TILE)
        state = fold(empty_state(), score(q, key, causal), value_t)

        def earlier(tile, state):
            key, value_t = read_keys(keys, pl.multiple_of(tile * Q_TILE, Q_TILE), Q_TILE)
            return fold(state, score(q, key), value_t)

        store_state(lax.fori_loop(0, place, earlier, state), state_ref)

    whole = constant_spec((rows, HD))
    whole_kv = constant_spec((rows, 2 * HD))
    return pl.pallas_call(
        kernel,
        grid_spec=pltpu.PrefetchScalarGridSpec(
            num_scalar_prefetch=1,
            grid=(tiles,),
            in_specs=[whole, whole, whole_kv, whole_kv],
            out_specs=pl.BlockSpec(
                (1, STATE_ROWS, Q_TILE),
                lambda i, core: ((i + core[0] * per_block) % tiles, 0, 0),
            ),
            scratch_shapes=[
                pltpu.VMEM((2 * rows, 2 * HD), BF),
                pltpu.VMEM((2 * rows, HD), BF),
            ],
        ),
        out_shape=jax.ShapeDtypeStruct((tiles, STATE_ROWS, Q_TILE), F32),
        compiler_params=pltpu.CompilerParams(vmem_limit_bytes=VMEM_BYTES),
        cost_estimate=pl.CostEstimate(
            flops=10 * Q_TILE * Q_TILE * HD * 4,
            bytes_accessed=4 << 20,
            transcendentals=10 * Q_TILE * Q_TILE,
        ),
    )(core, query, query_other, kv, kv_other)


def attend_other(query, query_other, state, sources, use, last=False):
    rows = query.shape[0]
    per_block = rows // Q_TILE
    tiles = 2 * per_block
    count = len(sources)

    def kernel(use_ref, query_ref, query_other_ref, before_ref, *refs):
        source_refs = refs[:count]
        *out_refs, after, q_ref = refs[count:]
        tile = pl.program_id(0)

        @pl.when(tile < per_block)
        def _():
            q_ref[...] = query_ref[...]

        @pl.when(tile >= per_block)
        def _():
            q_ref[...] = query_other_ref[...]

        q = q_ref[...]
        after[...] = before_ref[...]

        def fold_in(refs):
            parts = [(ref, at) for ref in refs for at in range(0, rows, K_TILE)]
            state = load_state(after)
            scores = None
            for i, (ref, at) in enumerate(parts):
                key, value_t = read_keys(ref, at, K_TILE)
                if scores is None:
                    scores = score(q, key)
                later = None
                if i + 1 < len(parts):
                    next_ref, next_at = parts[i + 1]
                    later = score(q, next_ref[next_at : next_at + K_TILE, :HD])
                state = fold(state, scores, value_t)
                scores = later
            store_state(state, after)

        all_used = use_ref[0]
        for i in range(1, count):
            all_used = all_used & use_ref[i]

        @pl.when(all_used != 0)
        def _():
            fold_in(source_refs)

        for i, source_ref in enumerate(source_refs):

            @pl.when((all_used == 0) & (use_ref[i] != 0))
            def _(source_ref=source_ref):
                fold_in([source_ref])

        if last:
            _, total, summed = load_state(after)
            attended = (summed / total).T.astype(BF)
            for part, out_ref in enumerate(out_refs):

                @pl.when(tile // per_block == part)
                def _(out_ref=out_ref):
                    at = pl.multiple_of(tile % per_block * Q_TILE, Q_TILE)
                    out_ref[pl.ds(at, Q_TILE), :] = attended

        else:
            out_refs[0][...] = after[...]

    state_spec = pl.BlockSpec((1, STATE_ROWS, Q_TILE), lambda i, use: (i, 0, 0))
    if last:
        out_shape = (jax.ShapeDtypeStruct((rows, HD), BF),) * 2
        out_specs = (constant_spec((rows, HD)),) * 2
    else:
        out_shape = jax.ShapeDtypeStruct((tiles, STATE_ROWS, Q_TILE), F32)
        out_specs = state_spec
    return pl.pallas_call(
        kernel,
        grid_spec=pltpu.PrefetchScalarGridSpec(
            num_scalar_prefetch=1,
            grid=(tiles,),
            in_specs=[
                pl.BlockSpec((Q_TILE, HD), lambda i, use: (jnp.minimum(i, per_block - 1), 0)),
                pl.BlockSpec((Q_TILE, HD), lambda i, use: (jnp.maximum(i - per_block, 0), 0)),
                state_spec,
            ]
            + [constant_spec(source.shape) for source in sources],
            out_specs=out_specs,
            scratch_shapes=[
                pltpu.VMEM((1, STATE_ROWS, Q_TILE), F32),
                pltpu.VMEM((Q_TILE, HD), BF),
            ],
        ),
        out_shape=out_shape,
        compiler_params=pltpu.CompilerParams(vmem_limit_bytes=VMEM_BYTES),
        cost_estimate=pl.CostEstimate(
            flops=2 * rows * count * rows * HD * 4,
            bytes_accessed=6 << 20,
            transcendentals=2 * rows * count * rows,
        ),
    )(use, query, query_other, state, *sources)


def pick_weights(w_out, table):
    depth, width = w_out.shape[1], 2 * HD

    def kernel(table_ref, weight_ref, out_ref):
        out_ref[0] = weight_ref[...]

    return pl.pallas_call(
        kernel,
        grid_spec=pltpu.PrefetchScalarGridSpec(
            num_scalar_prefetch=1,
            grid=(4,),
            in_specs=[pl.BlockSpec((MODALITIES, depth, width), lambda k, t: (0, 0, t[k]))],
            out_specs=pl.BlockSpec((1, MODALITIES, depth, width), lambda k, t: (k, 0, 0, 0)),
        ),
        out_shape=jax.ShapeDtypeStruct((4, MODALITIES, depth, width), BF),
        compiler_params=pltpu.CompilerParams(vmem_limit_bytes=VMEM_BYTES),
        cost_estimate=pl.CostEstimate(flops=0, bytes_accessed=3 << 20, transcendentals=0),
    )(table, w_out)


def output_part(own, other, weights, table, seg, sizes):
    blocks = table.shape[0]
    rows = own.shape[0]
    width = 2 * HD
    picked = weights.ndim == 4

    def kernel(table_ref, seg_ref, own_ref, other_ref, weight_ref, *refs):
        *out_refs, attended, left, right, total, result, weight_sem, out_sem = refs
        weight_copies = []
        for i in range(blocks):
            first = pl.multiple_of(table_ref[i] * width, width)
            weight_copies.append(
                pltpu.make_async_copy(
                    weight_ref.at[i] if picked else weight_ref.at[:, :, pl.ds(first, width)],
                    right.at[i // 2, :, :, pl.ds(i % 2 * width, width)],
                    weight_sem.at[i],
                )
            )
            weight_copies[i].start()
        core = seg_ref[2 * MODALITIES]
        for mine in range(2):

            @pl.when(core == mine)
            def _(mine=mine):
                attended[:, mine * HD : (mine + 1) * HD] = own_ref[...]
                attended[:, (1 - mine) * HD : (2 - mine) * HD] = other_ref[...]

        def mask(kind, at, keep):
            left[kind] = attended[at, :] * keep.astype(BF)

        for_runs(seg_ref, rows, mask)
        out_copies = []
        for pair in range(blocks // 2):
            weight_copies[2 * pair].wait()
            weight_copies[2 * pair + 1].wait()
            total[...] = jnp.zeros_like(total)

            def run(kind, at, keep, pair=pair):
                total[at, :] += jnp.dot(left[kind], right[pair, kind], preferred_element_type=F32)

            for_runs(seg_ref, rows, run)
            for i in range(2):
                result[2 * pair + i] = total[:, i * width : (i + 1) * width].astype(BF)
            done = 0
            for size, out_ref in zip(sizes, out_refs):
                if done // 2 == pair:
                    source = result.at[pl.ds(done, 2)] if size else result.at[done]
                    out_copies.append(
                        pltpu.make_async_copy(source, out_ref, out_sem.at[len(out_copies)])
                    )
                    out_copies[-1].start()
                done += max(size, 1)
        for copy in out_copies:
            copy.wait()

    vmem = pl.BlockSpec(memory_space=pltpu.VMEM)
    shapes = [(size, rows, width) if size else (rows, width) for size in sizes]
    return pl.pallas_call(
        kernel,
        in_specs=[pl.BlockSpec(memory_space=pltpu.SMEM)] * 2
        + [vmem, vmem, pl.BlockSpec(memory_space=pl.ANY)],
        out_specs=(pl.BlockSpec(memory_space=pl.ANY),) * len(shapes),
        scratch_shapes=[
            pltpu.VMEM((rows, width), BF),
            pltpu.VMEM((MODALITIES, WINDOW, width), BF),
            pltpu.VMEM((blocks // 2, MODALITIES, width, 2 * width), BF),
            pltpu.VMEM((rows, 2 * width), F32),
            pltpu.VMEM((blocks, rows, width), BF),
            pltpu.SemaphoreType.DMA((blocks,)),
            pltpu.SemaphoreType.DMA((len(shapes),)),
        ],
        out_shape=tuple(jax.ShapeDtypeStruct(shape, BF) for shape in shapes),
        compiler_params=pltpu.CompilerParams(vmem_limit_bytes=VMEM_BYTES),
        cost_estimate=pl.CostEstimate(flops=0, bytes_accessed=rows, transcendentals=0),
    )(table, seg, own, other, weights)


def add(*arrays):
    return sum(array.astype(F32) for array in arrays).astype(BF)


def local(tokens, modality, w_query, w_key, w_value, w_out):
    seg = segment_scalars(modality)
    core = seg[2 * MODALITIES :]
    weights = (w_key, w_value, w_query)

    before, after = move(tokens, True, 1), move(tokens, True, -1)
    opposite = move(tokens, True, 2)
    plus_first = jnp.stack([tokens, before])
    minus_first = jnp.stack([tokens, after])
    before_first = move(plus_first, False, 1)
    after_first = move(minus_first, False, -1)
    before, after, opposite, _ = lax.optimization_barrier((before, after, opposite, plus_first))
    plus_second = jnp.stack([after, opposite])
    minus_second = jnp.stack([before, opposite])
    before_second = move(plus_second, False, 1)
    after_second = move(minus_second, False, -1)
    names = dict(self=0, before=3, after=1, opposite=2)

    def shards(second, *firsts):
        return [(names[first], second) for first in firsts]

    lists = [
        shards(0, "self", "before", "after", "opposite"),
        shards(3, "self", "before") + shards(1, "self", "after"),
        shards(3, "after", "opposite") + shards(1, "before", "opposite") + shards(2, "after"),
        shards(2, "self", "before", "opposite"),
    ]
    tables = [shard_table(*zip(*chosen)) for chosen in lists]
    partial = project([plus_first, plus_second], weights, tables[0], seg)
    before_first, after_first, partial = lax.optimization_barrier(
        (before_first, after_first, partial)
    )
    far_first = move(before_first, False, 1)
    far_after = move(after_first[1:], False, -1)
    partial = project([before_first, after_first], weights, tables[1], seg, before=partial)
    after_second, partial = lax.optimization_barrier((after_second, partial))
    far_opposite = move(after_second[1:], False, -1)
    partial = project(
        [before_second, after_second, far_after], weights, tables[2], seg, before=partial
    )
    query, kv, query_send, kv_send = project(
        [far_first, far_opposite], weights, tables[3], seg, before=partial, last=True
    )

    kv_other = swap_core(kv_send)
    query_other = swap_core(query_send)
    kv_before = move_x(kv, 1)
    kv_other_after = move_x(kv_other, -1)
    kv_other_before = move_x(kv_other, 1)
    kv_after = move_x(kv, -1)
    chip = lax.axis_index("ctx") // 2
    near_use = jnp.stack([chip >= 1, chip == 3]).astype(jnp.int32)
    far_use = jnp.stack([chip >= 2, chip >= 2]).astype(jnp.int32)
    queries = (query, query_other)
    state = attend_own(*queries, kv, kv_other, core)
    here, plus, two, minus = (shard_table(np.full(4, offset), np.arange(4)) for offset in range(4))
    kv_before, kv_other_after, state, w_two = lax.optimization_barrier(
        (kv_before, kv_other_after, state, pick_weights(w_out, two))
    )
    kv_far = move_x(kv_before, 1)
    kv_other_far = move_x(kv_other_after, -1)
    state = attend_other(*queries, state, [kv_before, kv_other_after], near_use)
    state = attend_other(*queries, state, [kv_other_before, kv_after], near_use)
    own, own_send = attend_other(*queries, state, [kv_far, kv_other_far], far_use, last=True)
    other = swap_core(own_send)

    part = functools.partial(output_part, own, other)
    two_low, two_high = part(w_two, two, seg, (2, 2))
    two_low = move(two_low, True, 1)
    two_high = move(two_high, True, -1)
    first = jnp.concatenate([plus[2:], minus[:2]])
    plus_high, minus_low = part(w_out, first, seg, (2, 2))
    plus_high = move(plus_high, True, 1)
    minus_low = move(minus_low, True, -1)
    later = jnp.concatenate([plus[:2], minus[2:]])
    plus_low, minus_high = part(w_out, later, seg, (2, 2))
    plus_low = add(plus_low, two_low)
    minus_high = add(minus_high, two_high)
    plus_low, minus_high, own, other = lax.optimization_barrier((plus_low, minus_high, own, other))
    here = output_part(own, other, w_out, here, seg, (0, 0, 0, 0))
    plus_low = move(plus_low, True, 1)
    minus_high = move(minus_high, True, -1)
    plus_low, plus_high, minus_low, minus_high = lax.optimization_barrier(
        (plus_low, plus_high, minus_low, minus_high)
    )
    mine, plus, two, minus = (
        add(here[i], (plus_low, plus_high)[i // 2][i % 2], (minus_low, minus_high)[i // 2][i % 2])
        for i in range(4)
    )
    return add(
        tokens, mine, move(plus, False, 1), move(two, False, 2), move(minus, False, -1)
    )


def solution(mesh):
    in_specs = (
        P("ctx", "tp"),
        P("ctx"),
        P(None, None, "tp"),
        P(None, None, "tp"),
        P(None, None, "tp"),
        P(None, "tp", None),
    )
    return jax.shard_map(
        local, mesh=mesh, in_specs=in_specs, out_specs=P("ctx", "tp"), check_vma=False
    )
```

profile of v0, /device:TPU:6, one launch (start us, length us, event | category | flops | bytes accessed | tf_op | source)
XLA Modules:
  0.0 202.1 jit_solution(13711100871880926088)
XLA Ops:
  0.0 1.6 collective-permute-start
  1.6 1.7 collective-permute-start.2
  3.2 2.0 collective-permute-start.4
  5.2 5.4 %collective-permute-done = bf16[1024,256]{1,0:T(8,128)(2,1)S(1)} collective-permute-done((bf16[1024,256]{1,0:T(8,128)(2,1)}, bf16[1024,256]{1,0:T(8,128)(2,1)S(1)}, u32[]{:S(2)}, u32[]{:S(2)}) %collective-permute-start) | collective-permute-done | bytes 524320 | tf_op jit(solution)/shard_map/ppermute | solution.py:43
  10.6 0.4 collective-permute-done.2
  11.0 2.4 %pad_maximum_fusion = (bf16[2,1024,256]{2,1,0:T(8,128)(2,1)}, bf16[2,1024,256]{2,1,0:T(8,128)(2,1)S(1)}) fusion(bf16[1,1024,256]{2,1,0:T(8,128)(2,1)} %bitcast.38, bf16[1,1024,256]{2,1,0:T(8,128)(2,1)S(1)} %bitcast.36, bf16[1,1024,256]{2,1,0:T(8,128)(2,1)S(1)} %bitcast.34), kind=kLoop, calls=%fused_computation.2 | loop fusion | flops 1048576 | bytes 3670016 | tf_op jit(solution)/shard_map/stack | solution.py:586
  13.4 2.0 collective-permute-start.1
  15.4 2.2 %collective-permute-start.3 = (bf16[2,1024,256]{2,1,0:T(8,128)(2,1)}, bf16[2,1024,256]{2,1,0:T(8,128)(2,1)S(1)}, u32[]{:S(2)}, u32[]{:S(2)}) collective-permute-start(bf16[2,1024,256]{2,1,0:T(8,128)(2,1)} %get-tuple-element.99), channel_id=1, source_target_pairs={{0,12},{1,13},{2,14},{3,15},{4,0},{5,1},{6,2},{7,3},{8,4},{9,5},{1... | collective-permute-start | bytes 3145736 | tf_op jit(solution)/shard_map/ppermute | solution.py:43
  17.6 2.6 %pad_maximum_fusion.2 = (bf16[2,1024,256]{2,1,0:T(8,128)(2,1)}, bf16[2,1024,256]{2,1,0:T(8,128)(2,1)S(1)}) fusion(bf16[1,1024,256]{2,1,0:T(8,128)(2,1)} %bitcast.6, bf16[1,1024,256]{2,1,0:T(8,128)(2,1)} %bitcast.35, bf16[1,1024,256]{2,1,0:T(8,128)(2,1)} %bitcast.37), kind=kLoop, calls=%fused_computation.4 | loop fusion | flops 1048576 | bytes 3670016 | tf_op jit(solution)/shard_map/stack | solution.py:591
  20.1 4.0 %collective-permute-start.6 = (bf16[2,1024,256]{2,1,0:T(8,128)(2,1)}, bf16[2,1024,256]{2,1,0:T(8,128)(2,1)}, u32[]{:S(2)}, u32[]{:S(2)}) collective-permute-start(bf16[2,1024,256]{2,1,0:T(8,128)(2,1)} %get-tuple-element.97), channel_id=1, source_target_pairs={{0,12},{1,13},{2,14},{3,15},{4,0},{5,1},{6,2},{7,3},{8,4},{9,5},{1... | collective-permute-start | bytes 3145736 | tf_op jit(solution)/shard_map/ppermute | solution.py:43
  24.2 0.2 select_reduce_fusion.1
  24.5 0.1 pad_add_fusion.seg_ref
  24.6 7.7 %shard_map.208 = (f32[1024,1]{1,0:T(8,128)S(1)}, f32[1024,768]{1,0:T(8,128)}) custom-call(s32[4]{0:T(128)S(1)} %get-tuple-element.106.table_ref, s32[7]{0:T(128)S(1)} %pad_add_fusion.seg_ref, bf16[2,1024,256]{2,1,0:T(8,128)(2,1)S(1)} %get-tuple-element.100.refs_0_, bf16[2,1024,256]{2,1,0:T(8,128)(2,1)S(1)} %get-tuple-element.98.refs_1_, ...), custom_call_target="tpu_custom_call" | custom-call | flops 2491416576 | bytes 6815744 | tf_op jit(solution)/shard_map/pallas_call | solution.py:248
  32.3 0.8 copy-done.3
  33.2 15.2 %collective-permute-start.9 = (bf16[1,1024,256]{2,1,0:T(8,128)(2,1)S(1)}, bf16[1,1024,256]{2,1,0:T(8,128)(2,1)S(1)}, u32[]{:S(2)}, u32[]{:S(2)}) collective-permute-start(bf16[1,1024,256]{2,1,0:T(8,128)(2,1)S(1)} %slice.45), channel_id=1, source_target_pairs={{0,12},{1,13},{2,14},{3,15},{4,0},{5,1},{6,2},{7,3},{8,4},{9,5},{1... | collective-permute-start | bytes 1572872 | tf_op jit(solution)/shard_map/ppermute | solution.py:43
  48.3 1.0 copy-done.4
  49.4 8.3 %shard_map.209 = (f32[1024,1]{1,0:T(8,128)S(1)}, f32[1024,768]{1,0:T(8,128)}) custom-call(s32[4]{0:T(128)S(1)} %get-tuple-element.105.table_ref, s32[7]{0:T(128)S(1)} %pad_add_fusion.seg_ref, bf16[2,1024,256]{2,1,0:T(8,128)(2,1)} %collective-permute-done.1.refs_0_, bf16[2,1024,256]{2,1,0:T(8,128)(2,1)S(1)} %collective-permute-done.3.refs_1_, ...), custom_call_target="tpu_custom_call" | custom-call | flops 2491416576 | bytes 6815744 | tf_op jit(solution)/shard_map/pallas_call | solution.py:248
  57.7 1.1 slice.44
  58.8 2.1 %collective-permute-start.7 = (bf16[1,1024,256]{2,1,0:T(8,128)(2,1)S(1)}, bf16[1,1024,256]{2,1,0:T(8,128)(2,1)S(1)}, u32[]{:S(2)}, u32[]{:S(2)}) collective-permute-start(bf16[1,1024,256]{2,1,0:T(8,128)(2,1)S(1)} %slice.44), channel_id=1, source_target_pairs={{0,12},{1,13},{2,14},{3,15},{4,0},{5,1},{6,2},{7,3},{8,4},{9,5},{1... | collective-permute-start | bytes 1572872 | tf_op jit(solution)/shard_map/ppermute | solution.py:43
  60.9 9.9 %shard_map.210 = (f32[1024,1]{1,0:T(8,128)S(1)}, f32[1024,768]{1,0:T(8,128)}) custom-call(s32[5]{0:T(128)S(1)} %broadcast_select_fusion.table_ref, s32[7]{0:T(128)S(1)} %pad_add_fusion.seg_ref, bf16[2,1024,256]{2,1,0:T(8,128)(2,1)} %collective-permute-done.8.refs_0_, bf16[2,1024,256]{2,1,0:T(8,128)(2,1)} %collective-permute-done.6.refs_1_, ...), custom_call_target="tpu_custom_call" | custom-call | flops 3114270720 | bytes 8519680 | tf_op jit(solution)/shard_map/pallas_call | solution.py:248
  70.9 7.8 %shard_map.211 = (bf16[1024,128]{1,0:T(8,128)(2,1)S(1)}, bf16[1024,256]{1,0:T(8,128)(2,1)S(1)}, bf16[1024,128]{1,0:T(8,128)(2,1)}, bf16[1024,256]{1,0:T(8,128)(2,1)S(1)}) custom-call(s32[3]{0:T(128)S(1)} %broadcast_select_fusion.1.table_ref, s32[7]{0:T(128)S(1)} %pad_add_fusion.seg_ref, bf16[2,1024,256]{2,1,0:T(8,128)(2,1)S(1)} %collective-permute-done.5.refs_0_, ...), custom_call_target="tpu_custom_call" | custom-call | flops 1868562432 | bytes 5111808 | tf_op jit(solution)/shard_map/pallas_call | solution.py:248
  78.7 0.1 collective-permute-start.12
  78.7 0.5 collective-permute-start.11
  79.3 1.5 collective-permute-done.12.kv_other_ref
  80.8 0.8 collective-permute-start.13
  81.6 2.8 %copy-done = bf16[3,256,4096]{2,1,0:T(8,128)(2,1)S(1)} copy-done((bf16[3,256,4096]{2,1,0:T(8,128)(2,1)S(1)}, bf16[3,256,4096]{2,1,0:T(8,128)(2,1)}, u32[]{:S(2)}) %copy-start) | copy-done | bytes 6291480
  84.4 1.0 shard_map.213.weight_ref
  85.4 0.6 collective-permute-start.15
  86.0 3.1 %collective-permute-start.14 = (bf16[1024,256]{1,0:T(8,128)(2,1)}, bf16[1024,256]{1,0:T(8,128)(2,1)}, u32[]{:S(2)}, u32[]{:S(2)}) collective-permute-start(bf16[1024,256]{1,0:T(8,128)(2,1)} %collective-permute-done.12.kv_other_ref), channel_id=1, source_target_pairs={{0,32},{16,48},{32,64},{48,80},{64,96},{80,112},{96,0},{112,16},{1... | collective-permute-start | bytes 1572872 | tf_op jit(solution)/shard_map/ppermute | solution.py:48
  89.1 7.7 %shard_map.212.before_ref = f32[4,144,512]{2,1,0:T(8,128)S(1)} custom-call(s32[1]{0:T(128)} %bitcast.core_ref, bf16[1024,128]{1,0:T(8,128)(2,1)S(1)} %get-tuple-element.65.query_ref, bf16[1024,128]{1,0:T(8,128)(2,1)S(1)} %collective-permute-done.10.query_other_ref, bf16[1024,256]{1,0:T(8,128)(2,1)S(1)} %get-tuple-element.67.kv_ref, ...), custom_call_target="tpu_custom_call" | custom-call | flops 1342177280 | bytes 4194304 | tf_op jit(solution)/shard_map/pallas_call | solution.py:353
  96.8 1.1 copy-done.6
  97.8 1.2 collective-permute-start.16
  99.0 0.8 collective-permute-start.17
  100.0 1.3 copy-done.7
  101.3 8.1 %shard_map.214.before_ref = f32[4,144,512]{2,1,0:T(8,128)S(1)} custom-call(s32[2]{0:T(128)S(1)} %add_convert_fusion.4.use_ref, bf16[1024,128]{1,0:T(8,128)(2,1)S(1)} %get-tuple-element.65.query_ref, bf16[1024,128]{1,0:T(8,128)(2,1)S(1)} %collective-permute-done.10.query_other_ref, f32[4,144,512]{2,1,0:T(8,128)S(1)} %copy-done.7, ...), custom_call_target="tpu_custom_call" | custom-call | flops 2147483648 | bytes 6291456 | tf_op jit(solution)/shard_map/pallas_call | solution.py:450
  109.4 8.2 %shard_map.215.before_ref = f32[4,144,512]{2,1,0:T(8,128)S(1)} custom-call(s32[2]{0:T(128)S(1)} %add_convert_fusion.4.use_ref, bf16[1024,128]{1,0:T(8,128)(2,1)S(1)} %get-tuple-element.65.query_ref, bf16[1024,128]{1,0:T(8,128)(2,1)S(1)} %collective-permute-done.10.query_other_ref, f32[4,144,512]{2,1,0:T(8,128)S(1)} %shard_map.214.before_ref, ...), custom_call_target="tpu_custom_call" | custom-call | flops 2147483648 | bytes 6291456 | tf_op jit(solution)/shard_map/pallas_call | solution.py:450
  117.5 1.2 collective-permute-done.17.refs_1_
  118.7 8.5 %shard_map.216 = (bf16[1024,128]{1,0:T(8,128)(2,1)S(1)}, bf16[1024,128]{1,0:T(8,128)(2,1)S(1)}) custom-call(s32[2]{0:T(128)S(1)} %add_convert_fusion.3.use_ref, bf16[1024,128]{1,0:T(8,128)(2,1)S(1)} %get-tuple-element.65.query_ref, bf16[1024,128]{1,0:T(8,128)(2,1)S(1)} %collective-permute-done.10.query_other_ref, f32[4,144,512]{2,1,0:T(8,128)S(1)} %shard_map.215.before_ref, ...), custom_call_target="tpu_custom_call" | custom-call | flops 2147483648 | bytes 6291456 | tf_op jit(solution)/shard_map/pallas_call | solution.py:450
  127.3 0.1 collective-permute-start.18
  127.4 1.5 collective-permute-done.18.other_ref
  128.9 3.9 %shard_map.218 = (bf16[2,1024,256]{2,1,0:T(8,128)(2,1)S(1)}, bf16[2,1024,256]{2,1,0:T(8,128)(2,1)}) custom-call(s32[4]{0:T(128)S(1)} %broadcast_select_fusion.2.table_ref, s32[7]{0:T(128)S(1)} %pad_add_fusion.seg_ref, bf16[1024,128]{1,0:T(8,128)(2,1)S(1)} %get-tuple-element.79.own_ref, bf16[1024,128]{1,0:T(8,128)(2,1)S(1)} %collective-permute-done.18.other_ref, ...), custom_call_target="tpu_custom_call" | custom-call | bytes 1024 | tf_op jit(solution)/shard_map/pallas_call | solution.py:554
  132.9 1.0 copy-done.5
  133.8 6.4 %collective-permute-start.20 = (bf16[2,1024,256]{2,1,0:T(8,128)(2,1)}, bf16[2,1024,256]{2,1,0:T(8,128)(2,1)}, u32[]{:S(2)}, u32[]{:S(2)}) collective-permute-start(bf16[2,1024,256]{2,1,0:T(8,128)(2,1)} %get-tuple-element.78), channel_id=1, source_target_pairs={{0,3},{1,0},{2,1},{3,2},{4,7},{5,4},{6,5},{7,6},{8,11},{9,8},{10,9... | collective-permute-start | bytes 3145736 | tf_op jit(solution)/shard_map/ppermute | solution.py:43
  140.5 2.8 %copy-done.1 = bf16[3,256,4096]{2,1,0:T(8,128)(2,1)S(1)} copy-done((bf16[3,256,4096]{2,1,0:T(8,128)(2,1)S(1)}, bf16[3,256,4096]{2,1,0:T(8,128)(2,1)}, u32[]{:S(2)}) %copy-start.1) | copy-done | bytes 6291480
  143.3 3.0 %shard_map.220 = (bf16[2,1024,256]{2,1,0:T(8,128)(2,1)S(1)}, bf16[2,1024,256]{2,1,0:T(8,128)(2,1)S(1)}) custom-call(s32[4]{0:T(128)S(1)} %pad_add_fusion.2.table_ref, s32[7]{0:T(128)S(1)} %pad_add_fusion.seg_ref, bf16[1024,128]{1,0:T(8,128)(2,1)S(1)} %get-tuple-element.79.own_ref, bf16[1024,128]{1,0:T(8,128)(2,1)S(1)} %collective-permute-done.18.other_ref, ...), custom_call_target="tpu_custom_call" | custom-call | bytes 1024 | tf_op jit(solution)/shard_map/pallas_call | solution.py:554
  146.4 3.3 %collective-permute-start.23 = (bf16[2,1024,256]{2,1,0:T(8,128)(2,1)S(1)}, bf16[2,1024,256]{2,1,0:T(8,128)(2,1)}, u32[]{:S(2)}, u32[]{:S(2)}) collective-permute-start(bf16[2,1024,256]{2,1,0:T(8,128)(2,1)S(1)} %get-tuple-element.84), channel_id=1, source_target_pairs={{0,3},{1,0},{2,1},{3,2},{4,7},{5,4},{6,5},{7,6},{8,11},{9,8},{10,9... | collective-permute-start | bytes 3145736 | tf_op jit(solution)/shard_map/ppermute | solution.py:43
  149.7 3.0 %shard_map.217 = (bf16[2,1024,256]{2,1,0:T(8,128)(2,1)S(1)}, bf16[2,1024,256]{2,1,0:T(8,128)(2,1)S(1)}) custom-call(s32[4]{0:T(128)S(1)} %pad_add_fusion.1.table_ref, s32[7]{0:T(128)S(1)} %pad_add_fusion.seg_ref, bf16[1024,128]{1,0:T(8,128)(2,1)S(1)} %get-tuple-element.79.own_ref, bf16[1024,128]{1,0:T(8,128)(2,1)S(1)} %collective-permute-done.18.other_ref, ...), custom_call_target="tpu_custom_call" | custom-call | bytes 1024 | tf_op jit(solution)/shard_map/pallas_call | solution.py:554
  152.7 0.2 collective-permute-done.20
  152.8 2.5 %add_convert_fusion = bf16[2,1024,256]{2,1,0:T(8,128)(2,1)} fusion(bf16[2,1024,256]{2,1,0:T(8,128)(2,1)} %collective-permute-done.20, bf16[2,1024,256]{2,1,0:T(8,128)(2,1)S(1)} %get-tuple-element.77), kind=kLoop, calls=%fused_computation | loop fusion | flops 2097152 | bytes 3145728 | tf_op jit(solution)/shard_map/convert_element_type | solution.py:575
  155.3 1.1 collective-permute-done.19
  156.4 1.3 add_convert_fusion.1
  157.8 3.2 %collective-permute-start.24 = (bf16[2,1024,256]{2,1,0:T(8,128)(2,1)}, bf16[2,1024,256]{2,1,0:T(8,128)(2,1)}, u32[]{:S(2)}, u32[]{:S(2)}) collective-permute-start(bf16[2,1024,256]{2,1,0:T(8,128)(2,1)} %add_convert_fusion), channel_id=1, source_target_pairs={{0,3},{1,0},{2,1},{3,2},{4,7},{5,4},{6,5},{7,6},{8,11},{9,8},{10,9... | collective-permute-start | bytes 3145736 | tf_op jit(solution)/shard_map/ppermute | solution.py:43
  161.0 2.8 %copy-done.2 = bf16[3,256,4096]{2,1,0:T(8,128)(2,1)S(1)} copy-done((bf16[3,256,4096]{2,1,0:T(8,128)(2,1)S(1)}, bf16[3,256,4096]{2,1,0:T(8,128)(2,1)}, u32[]{:S(2)}) %copy-start.2) | copy-done | bytes 6291480
  163.8 3.0 %shard_map.219 = (bf16[1024,256]{1,0:T(8,128)(2,1)S(1)}, bf16[1024,256]{1,0:T(8,128)(2,1)S(1)}, bf16[1024,256]{1,0:T(8,128)(2,1)S(1)}, bf16[1024,256]{1,0:T(8,128)(2,1)S(1)}) custom-call(s32[4]{0:T(128)S(1)} %broadcast_select_fusion.7.table_ref, s32[7]{0:T(128)S(1)} %pad_add_fusion.seg_ref, bf16[1024,128]{1,0:T(8,128)(2,1)S(1)} %get-tuple-element.79.own_ref, ...), custom_call_target="tpu_custom_call" | custom-call | bytes 1024 | tf_op jit(solution)/shard_map/pallas_call | solution.py:554
  166.8 1.0 collective-permute-done.22
  167.8 11.2 %collective-permute-done.21 = bf16[2,1024,256]{2,1,0:T(8,128)(2,1)} collective-permute-done((bf16[2,1024,256]{2,1,0:T(8,128)(2,1)}, bf16[2,1024,256]{2,1,0:T(8,128)(2,1)}, u32[]{:S(2)}, u32[]{:S(2)}) %collective-permute-start.21) | collective-permute-done | bytes 1048608 | tf_op jit(solution)/shard_map/ppermute | solution.py:43
  179.0 1.4 fusion.2
  180.4 0.2 collective-permute-start.25
  180.6 2.0 fusion.1
  182.6 1.8 collective-permute-start.26
  184.4 1.5 collective-permute-start.27
  185.9 10.6 %collective-permute-done.25 = bf16[1024,256]{1,0:T(8,128)(2,1)S(1)} collective-permute-done((bf16[1024,256]{1,0:T(8,128)(2,1)S(1)}, bf16[1024,256]{1,0:T(8,128)(2,1)S(1)}, u32[]{:S(2)}, u32[]{:S(2)}) %collective-permute-start.25) | collective-permute-done | bytes 524320 | tf_op jit(solution)/shard_map/ppermute | solution.py:43
  196.5 3.0 %collective-permute-done.27 = bf16[1024,256]{1,0:T(8,128)(2,1)S(1)} collective-permute-done((bf16[1024,256]{1,0:T(8,128)(2,1)S(1)}, bf16[1024,256]{1,0:T(8,128)(2,1)S(1)}, u32[]{:S(2)}, u32[]{:S(2)}) %collective-permute-start.27) | collective-permute-done | bytes 524320 | tf_op jit(solution)/shard_map/ppermute | solution.py:43
  199.5 2.5 %add_convert_fusion.2 = bf16[1024,256]{1,0:T(8,128)(2,1)} fusion(bf16[1024,256]{1,0:T(8,128)(2,1)S(1)} %collective-permute-done.27, bf16[1024,256]{1,0:T(8,128)(2,1)S(1)} %collective-permute-done.26, bf16[1024,256]{1,0:T(8,128)(2,1)S(1)} %collective-permute-done.25, bf16[1024,256]{1,0:T(8,128)(2,1)S(1)} %copy-done.10, ...), kind=kLoop, calls=%fused_computation.18 | loop fusion | flops 4194304 | bytes 4194304 | tf_op jit(solution)/shard_map/convert_element_type | solution.py:575
  (66 shorter events, 0.8 us)
Async XLA Ops:
  0.0 10.6 %collective-permute-start = (bf16[1024,256]{1,0:T(8,128)(2,1)}, bf16[1024,256]{1,0:T(8,128)(2,1)S(1)}, u32[]{:S(2)}, u32[]{:S(2)}) collective-permute-start(bf16[1024,256]{1,0:T(8,128)(2,1)} %param.22), channel_id=1, source_target_pairs={{0,1},{1,2},{2,3},{3,0},{4,5},{5,6},{6,7},{7,4},{8,9},{9,10},{10,1... | collective-permute-start | bytes 1572872 | tf_op jit(solution)/shard_map/ppermute | solution.py:43
  1.6 9.4 %collective-permute-start.2 = (bf16[1024,256]{1,0:T(8,128)(2,1)}, bf16[1024,256]{1,0:T(8,128)(2,1)S(1)}, u32[]{:S(2)}, u32[]{:S(2)}) collective-permute-start(bf16[1024,256]{1,0:T(8,128)(2,1)} %param.22), channel_id=1, source_target_pairs={{0,3},{1,0},{2,1},{3,2},{4,7},{5,4},{6,5},{7,6},{8,11},{9,8},{10,9... | collective-permute-start | bytes 1572872 | tf_op jit(solution)/shard_map/ppermute | solution.py:43
  3.2 14.3 %collective-permute-start.4 = (bf16[1024,256]{1,0:T(8,128)(2,1)}, bf16[1024,256]{1,0:T(8,128)(2,1)}, u32[]{:S(2)}, u32[]{:S(2)}) collective-permute-start(bf16[1024,256]{1,0:T(8,128)(2,1)} %param.22), channel_id=1, source_target_pairs={{0,2},{1,3},{2,0},{3,1},{4,6},{5,7},{6,4},{7,5},{8,10},{9,11},{10,... | collective-permute-start | bytes 1572872 | tf_op jit(solution)/shard_map/ppermute | solution.py:43
  10.6 7.0 %copy-start.8 = (bf16[1024,256]{1,0:T(8,128)(2,1)}, bf16[1024,256]{1,0:T(8,128)(2,1)S(1)}, u32[]{:S(2)}) copy-start(bf16[1024,256]{1,0:T(8,128)(2,1)S(1)} %collective-permute-done) | copy-start | bytes 1572868
  11.0 6.6 %copy-start.9 = (bf16[1024,256]{1,0:T(8,128)(2,1)}, bf16[1024,256]{1,0:T(8,128)(2,1)S(1)}, u32[]{:S(2)}) copy-start(bf16[1024,256]{1,0:T(8,128)(2,1)S(1)} %collective-permute-done.2) | copy-start | bytes 1572868
  13.4 10.8 %copy-start.11 = (s32[1024]{0:T(1024)S(1)}, s32[1024]{0:T(1024)}, u32[]{:S(2)}) copy-start(s32[1024]{0:T(1024)} %param.23) | copy-start | bytes 12292
  13.4 11.0 %copy-start.12 = (s32[4]{0:T(128)S(1)}, s32[4]{0:T(128)}, u32[]{:S(2)}) copy-start(s32[4]{0:T(128)} %constant.221.clone) | copy-start | bytes 52
  13.4 11.0 %copy-start.13 = (s32[4]{0:T(128)S(1)}, s32[4]{0:T(128)}, u32[]{:S(2)}) copy-start(s32[4]{0:T(128)} %constant.223.clone) | copy-start | bytes 52
  13.4 11.0 %copy-start.14 = (s32[4]{0:T(128)S(1)}, s32[4]{0:T(128)}, u32[]{:S(2)}) copy-start(s32[4]{0:T(128)} %constant.224.clone) | copy-start | bytes 52
  13.4 19.7 %collective-permute-start.1 = (bf16[2,1024,256]{2,1,0:T(8,128)(2,1)S(1)}, bf16[2,1024,256]{2,1,0:T(8,128)(2,1)}, u32[]{:S(2)}, u32[]{:S(2)}) collective-permute-start(bf16[2,1024,256]{2,1,0:T(8,128)(2,1)S(1)} %get-tuple-element.100.refs_0_), channel_id=1, source_target_pairs={{0,4},{1,5},{2,6},{3,7},{4,8},{5,9},{6,10},{7,11},{8,12},{9,13},{1... | collective-permute-start | bytes 3145736 | tf_op jit(solution)/shard_map/ppermute | solution.py:43
  15.4 17.7 %collective-permute-start.3 = (bf16[2,1024,256]{2,1,0:T(8,128)(2,1)}, bf16[2,1024,256]{2,1,0:T(8,128)(2,1)S(1)}, u32[]{:S(2)}, u32[]{:S(2)}) collective-permute-start(bf16[2,1024,256]{2,1,0:T(8,128)(2,1)} %get-tuple-element.99), channel_id=1, source_target_pairs={{0,12},{1,13},{2,14},{3,15},{4,0},{5,1},{6,2},{7,3},{8,4},{9,5},{1... | collective-permute-start | bytes 3145736 | tf_op jit(solution)/shard_map/ppermute | solution.py:43
  20.1 37.5 %collective-permute-start.6 = (bf16[2,1024,256]{2,1,0:T(8,128)(2,1)}, bf16[2,1024,256]{2,1,0:T(8,128)(2,1)}, u32[]{:S(2)}, u32[]{:S(2)}) collective-permute-start(bf16[2,1024,256]{2,1,0:T(8,128)(2,1)} %get-tuple-element.97), channel_id=1, source_target_pairs={{0,12},{1,13},{2,14},{3,15},{4,0},{5,1},{6,2},{7,3},{8,4},{9,5},{1... | collective-permute-start | bytes 3145736 | tf_op jit(solution)/shard_map/ppermute | solution.py:43
  24.4 36.5 %collective-permute-start.8 = (bf16[2,1024,256]{2,1,0:T(8,128)(2,1)S(1)}, bf16[2,1024,256]{2,1,0:T(8,128)(2,1)}, u32[]{:S(2)}, u32[]{:S(2)}) collective-permute-start(bf16[2,1024,256]{2,1,0:T(8,128)(2,1)S(1)} %get-tuple-element.98.refs_1_), channel_id=1, source_target_pairs={{0,4},{1,5},{2,6},{3,7},{4,8},{5,9},{6,10},{7,11},{8,12},{9,13},{1... | collective-permute-start | bytes 3145736 | tf_op jit(solution)/shard_map/ppermute | solution.py:43
  32.3 0.8 copy-start.3
  33.1 37.8 %collective-permute-start.5 = (bf16[2,1024,256]{2,1,0:T(8,128)(2,1)}, bf16[2,1024,256]{2,1,0:T(8,128)(2,1)S(1)}, u32[]{:S(2)}, u32[]{:S(2)}) collective-permute-start(bf16[2,1024,256]{2,1,0:T(8,128)(2,1)} %collective-permute-done.1.refs_0_), channel_id=1, source_target_pairs={{0,4},{1,5},{2,6},{3,7},{4,8},{5,9},{6,10},{7,11},{8,12},{9,13},{1... | collective-permute-start | bytes 3145736 | tf_op jit(solution)/shard_map/ppermute | solution.py:43
  33.2 27.8 %collective-permute-start.9 = (bf16[1,1024,256]{2,1,0:T(8,128)(2,1)S(1)}, bf16[1,1024,256]{2,1,0:T(8,128)(2,1)S(1)}, u32[]{:S(2)}, u32[]{:S(2)}) collective-permute-start(bf16[1,1024,256]{2,1,0:T(8,128)(2,1)S(1)} %slice.45), channel_id=1, source_target_pairs={{0,12},{1,13},{2,14},{3,15},{4,0},{5,1},{6,2},{7,3},{8,4},{9,5},{1... | collective-permute-start | bytes 1572872 | tf_op jit(solution)/shard_map/ppermute | solution.py:43
  48.3 1.0 copy-start.4
  49.4 11.5 %copy-start.17 = (s32[3]{0:T(128)S(1)}, s32[3]{0:T(128)}, u32[]{:S(2)}) copy-start(s32[3]{0:T(128)} %constant.227.clone) | copy-start | bytes 40
  49.4 11.5 %copy-start.15 = (s32[5]{0:T(128)S(1)}, s32[5]{0:T(128)}, u32[]{:S(2)}) copy-start(s32[5]{0:T(128)} %constant.225.clone) | copy-start | bytes 64
  49.4 11.5 %copy-start.16 = (s32[5]{0:T(128)S(1)}, s32[5]{0:T(128)}, u32[]{:S(2)}) copy-start(s32[5]{0:T(128)} %constant.226.clone) | copy-start | bytes 64
  58.8 12.1 %collective-permute-start.7 = (bf16[1,1024,256]{2,1,0:T(8,128)(2,1)S(1)}, bf16[1,1024,256]{2,1,0:T(8,128)(2,1)S(1)}, u32[]{:S(2)}, u32[]{:S(2)}) collective-permute-start(bf16[1,1024,256]{2,1,0:T(8,128)(2,1)S(1)} %slice.44), channel_id=1, source_target_pairs={{0,12},{1,13},{2,14},{3,15},{4,0},{5,1},{6,2},{7,3},{8,4},{9,5},{1... | collective-permute-start | bytes 1572872 | tf_op jit(solution)/shard_map/ppermute | solution.py:43
  78.7 2.1 %collective-permute-start.12 = (bf16[1024,256]{1,0:T(8,128)(2,1)S(1)}, bf16[1024,256]{1,0:T(8,128)(2,1)}, u32[]{:S(2)}, u32[]{:S(2)}) collective-permute-start(bf16[1024,256]{1,0:T(8,128)(2,1)S(1)} %get-tuple-element.68), channel_id=1, source_target_pairs={{0,16},{16,0},{32,48},{48,32},{64,80},{80,64},{96,112},{112,96},{1... | collective-permute-start | bytes 1572872 | tf_op jit(solution)/shard_map/ppermute | solution.py:52
  78.7 19.1 %collective-permute-start.11 = (bf16[1024,256]{1,0:T(8,128)(2,1)S(1)}, bf16[1024,256]{1,0:T(8,128)(2,1)S(1)}, u32[]{:S(2)}, u32[]{:S(2)}) collective-permute-start(bf16[1024,256]{1,0:T(8,128)(2,1)S(1)} %get-tuple-element.67.kv_ref), channel_id=1, source_target_pairs={{0,32},{16,48},{32,64},{48,80},{64,96},{80,112},{96,0},{112,16},{1... | collective-permute-start | bytes 1572872 | tf_op jit(solution)/shard_map/ppermute | solution.py:48
  80.8 17.0 %collective-permute-start.13 = (bf16[1024,256]{1,0:T(8,128)(2,1)}, bf16[1024,256]{1,0:T(8,128)(2,1)}, u32[]{:S(2)}, u32[]{:S(2)}) collective-permute-start(bf16[1024,256]{1,0:T(8,128)(2,1)} %collective-permute-done.12.kv_other_ref), channel_id=1, source_target_pairs={{0,96},{16,112},{32,0},{48,16},{64,32},{80,48},{96,64},{112,80},{1... | collective-permute-start | bytes 1572872 | tf_op jit(solution)/shard_map/ppermute | solution.py:48
  81.6 7.5 %collective-permute-start.10 = (bf16[1024,128]{1,0:T(8,128)(2,1)}, bf16[1024,128]{1,0:T(8,128)(2,1)S(1)}, u32[]{:S(2)}, u32[]{:S(2)}) collective-permute-start(bf16[1024,128]{1,0:T(8,128)(2,1)} %get-tuple-element.66), channel_id=1, source_target_pairs={{0,16},{16,0},{32,48},{48,32},{64,80},{80,64},{96,112},{112,96},{1... | collective-permute-start | bytes 786440 | tf_op jit(solution)/shard_map/ppermute | solution.py:52
  81.6 2.8 %copy-start = (bf16[3,256,4096]{2,1,0:T(8,128)(2,1)S(1)}, bf16[3,256,4096]{2,1,0:T(8,128)(2,1)}, u32[]{:S(2)}) copy-start(bf16[3,256,4096]{2,1,0:T(8,128)(2,1)} %weight_ref.7) | copy-start | bytes 18874372
  85.4 24.0 %collective-permute-start.15 = (bf16[1024,256]{1,0:T(8,128)(2,1)S(1)}, bf16[1024,256]{1,0:T(8,128)(2,1)}, u32[]{:S(2)}, u32[]{:S(2)}) collective-permute-start(bf16[1024,256]{1,0:T(8,128)(2,1)S(1)} %get-tuple-element.67.kv_ref), channel_id=1, source_target_pairs={{0,96},{16,112},{32,0},{48,16},{64,32},{80,48},{96,64},{112,80},{1... | collective-permute-start | bytes 1572872 | tf_op jit(solution)/shard_map/ppermute | solution.py:48
  86.0 23.4 %collective-permute-start.14 = (bf16[1024,256]{1,0:T(8,128)(2,1)}, bf16[1024,256]{1,0:T(8,128)(2,1)}, u32[]{:S(2)}, u32[]{:S(2)}) collective-permute-start(bf16[1024,256]{1,0:T(8,128)(2,1)} %collective-permute-done.12.kv_other_ref), channel_id=1, source_target_pairs={{0,32},{16,48},{32,64},{48,80},{64,96},{80,112},{96,0},{112,16},{1... | collective-permute-start | bytes 1572872 | tf_op jit(solution)/shard_map/ppermute | solution.py:48
  96.8 1.1 copy-start.6
  97.8 19.7 %collective-permute-start.16 = (bf16[1024,256]{1,0:T(8,128)(2,1)S(1)}, bf16[1024,256]{1,0:T(8,128)(2,1)}, u32[]{:S(2)}, u32[]{:S(2)}) collective-permute-start(bf16[1024,256]{1,0:T(8,128)(2,1)S(1)} %collective-permute-done.11.refs_0_), channel_id=1, source_target_pairs={{0,32},{16,48},{32,64},{48,80},{64,96},{80,112},{96,0},{112,16},{1... | collective-permute-start | bytes 1572872 | tf_op jit(solution)/shard_map/ppermute | solution.py:48
  99.0 19.7 %collective-permute-start.17 = (bf16[1024,256]{1,0:T(8,128)(2,1)}, bf16[1024,256]{1,0:T(8,128)(2,1)}, u32[]{:S(2)}, u32[]{:S(2)}) collective-permute-start(bf16[1024,256]{1,0:T(8,128)(2,1)} %collective-permute-done.13.refs_1_), channel_id=1, source_target_pairs={{0,96},{16,112},{32,0},{48,16},{64,32},{80,48},{96,64},{112,80},{1... | collective-permute-start | bytes 1572872 | tf_op jit(solution)/shard_map/ppermute | solution.py:48
  100.0 1.3 copy-start.7
  127.3 1.6 collective-permute-start.18
  132.8 1.0 copy-start.5
  133.8 19.0 %collective-permute-start.20 = (bf16[2,1024,256]{2,1,0:T(8,128)(2,1)}, bf16[2,1024,256]{2,1,0:T(8,128)(2,1)}, u32[]{:S(2)}, u32[]{:S(2)}) collective-permute-start(bf16[2,1024,256]{2,1,0:T(8,128)(2,1)} %get-tuple-element.78), channel_id=1, source_target_pairs={{0,3},{1,0},{2,1},{3,2},{4,7},{5,4},{6,5},{7,6},{8,11},{9,8},{10,9... | collective-permute-start | bytes 3145736 | tf_op jit(solution)/shard_map/ppermute | solution.py:43
  140.2 16.2 %collective-permute-start.19 = (bf16[2,1024,256]{2,1,0:T(8,128)(2,1)}, bf16[2,1024,256]{2,1,0:T(8,128)(2,1)S(1)}, u32[]{:S(2)}, u32[]{:S(2)}) collective-permute-start(bf16[2,1024,256]{2,1,0:T(8,128)(2,1)} %copy-done.5), channel_id=1, source_target_pairs={{0,1},{1,2},{2,3},{3,0},{4,5},{5,6},{6,7},{7,4},{8,9},{9,10},{10,1... | collective-permute-start | bytes 3145736 | tf_op jit(solution)/shard_map/ppermute | solution.py:43
  140.5 2.8 %copy-start.1 = (bf16[3,256,4096]{2,1,0:T(8,128)(2,1)S(1)}, bf16[3,256,4096]{2,1,0:T(8,128)(2,1)}, u32[]{:S(2)}) copy-start(bf16[3,256,4096]{2,1,0:T(8,128)(2,1)} %weight_ref.7) | copy-start | bytes 18874372
  146.3 21.5 %collective-permute-start.22 = (bf16[2,1024,256]{2,1,0:T(8,128)(2,1)S(1)}, bf16[2,1024,256]{2,1,0:T(8,128)(2,1)}, u32[]{:S(2)}, u32[]{:S(2)}) collective-permute-start(bf16[2,1024,256]{2,1,0:T(8,128)(2,1)S(1)} %get-tuple-element.83), channel_id=1, source_target_pairs={{0,1},{1,2},{2,3},{3,0},{4,5},{5,6},{6,7},{7,4},{8,9},{9,10},{10,1... | collective-permute-start | bytes 3145736 | tf_op jit(solution)/shard_map/ppermute | solution.py:43
  146.4 21.4 %collective-permute-start.23 = (bf16[2,1024,256]{2,1,0:T(8,128)(2,1)S(1)}, bf16[2,1024,256]{2,1,0:T(8,128)(2,1)}, u32[]{:S(2)}, u32[]{:S(2)}) collective-permute-start(bf16[2,1024,256]{2,1,0:T(8,128)(2,1)S(1)} %get-tuple-element.84), channel_id=1, source_target_pairs={{0,3},{1,0},{2,1},{3,2},{4,7},{5,4},{6,5},{7,6},{8,11},{9,8},{10,9... | collective-permute-start | bytes 3145736 | tf_op jit(solution)/shard_map/ppermute | solution.py:43
  157.8 21.3 %collective-permute-start.21 = (bf16[2,1024,256]{2,1,0:T(8,128)(2,1)}, bf16[2,1024,256]{2,1,0:T(8,128)(2,1)}, u32[]{:S(2)}, u32[]{:S(2)}) collective-permute-start(bf16[2,1024,256]{2,1,0:T(8,128)(2,1)} %add_convert_fusion.1), channel_id=1, source_target_pairs={{0,1},{1,2},{2,3},{3,0},{4,5},{5,6},{6,7},{7,4},{8,9},{9,10},{10,1... | collective-permute-start | bytes 3145736 | tf_op jit(solution)/shard_map/ppermute | solution.py:43
  157.8 21.3 %collective-permute-start.24 = (bf16[2,1024,256]{2,1,0:T(8,128)(2,1)}, bf16[2,1024,256]{2,1,0:T(8,128)(2,1)}, u32[]{:S(2)}, u32[]{:S(2)}) collective-permute-start(bf16[2,1024,256]{2,1,0:T(8,128)(2,1)} %add_convert_fusion), channel_id=1, source_target_pairs={{0,3},{1,0},{2,1},{3,2},{4,7},{5,4},{6,5},{7,6},{8,11},{9,8},{10,9... | collective-permute-start | bytes 3145736 | tf_op jit(solution)/shard_map/ppermute | solution.py:43
  161.0 2.8 %copy-start.2 = (bf16[3,256,4096]{2,1,0:T(8,128)(2,1)S(1)}, bf16[3,256,4096]{2,1,0:T(8,128)(2,1)}, u32[]{:S(2)}) copy-start(bf16[3,256,4096]{2,1,0:T(8,128)(2,1)} %weight_ref.7) | copy-start | bytes 18874372
  180.4 16.1 %collective-permute-start.25 = (bf16[1024,256]{1,0:T(8,128)(2,1)S(1)}, bf16[1024,256]{1,0:T(8,128)(2,1)S(1)}, u32[]{:S(2)}, u32[]{:S(2)}) collective-permute-start(bf16[1024,256]{1,0:T(8,128)(2,1)S(1)} %fusion.2), channel_id=1, source_target_pairs={{0,4},{1,5},{2,6},{3,7},{4,8},{5,9},{6,10},{7,11},{8,12},{9,13},{1... | collective-permute-start | bytes 1572872 | tf_op jit(solution)/shard_map/ppermute | solution.py:43
  180.6 18.9 %copy-start.10 = (bf16[1024,256]{1,0:T(8,128)(2,1)S(1)}, bf16[1024,256]{1,0:T(8,128)(2,1)}, u32[]{:S(2)}) copy-start(bf16[1024,256]{1,0:T(8,128)(2,1)} %param.22) | copy-start | bytes 1572868
  182.6 13.9 %collective-permute-start.26 = (bf16[1024,256]{1,0:T(8,128)(2,1)S(1)}, bf16[1024,256]{1,0:T(8,128)(2,1)S(1)}, u32[]{:S(2)}, u32[]{:S(2)}) collective-permute-start(bf16[1024,256]{1,0:T(8,128)(2,1)S(1)} %get-tuple-element.95), channel_id=1, source_target_pairs={{0,8},{1,9},{2,10},{3,11},{4,12},{5,13},{6,14},{7,15},{8,0},{9,1},... | collective-permute-start | bytes 1572872 | tf_op jit(solution)/shard_map/ppermute | solution.py:43
  184.4 15.1 %collective-permute-start.27 = (bf16[1024,256]{1,0:T(8,128)(2,1)S(1)}, bf16[1024,256]{1,0:T(8,128)(2,1)S(1)}, u32[]{:S(2)}, u32[]{:S(2)}) collective-permute-start(bf16[1024,256]{1,0:T(8,128)(2,1)S(1)} %get-tuple-element.96), channel_id=1, source_target_pairs={{0,12},{1,13},{2,14},{3,15},{4,0},{5,1},{6,2},{7,3},{8,4},{9,5},{1... | collective-permute-start | bytes 1572872 | tf_op jit(solution)/shard_map/ppermute | solution.py:43
where the time goes:
time: 203 us; the launch traced here: 202 us
  Pallas kernels  80 us (39%)
  starting transfers between devices  54.5 us (27%)
  waiting for transfers between devices  37.1 us (18%)
  other arithmetic  15.3 us (8%)
  local copies, waits for them, and re-layouts  14.8 us (7%)
    ppermute x19, starting transfers between devices, move(): return lax.ppermute(array, AXES, plane_perm(first, step))  47.2 us
    pallas_call x4, Pallas kernels, project(): pl.pallas_call(kernel, in_specs=in_specs, out_specs=out_specs, scratch_sh...  33.7 us
    ppermute x19, waiting for transfers between devices, move(): return lax.ppermute(array, AXES, plane_perm(first, step))  32.9 us
    pallas_call x3, Pallas kernels, attend_other(): pl.pallas_call(kernel, grid_spec=pltpu.PrefetchScalarGridSpec(num_scalar_...  24.8 us
    unnamed x36, local copies, waits for them, and re-layouts  13.5 us
    pallas_call x4, Pallas kernels, output_part(): pl.pallas_call(kernel, in_specs=[pl.BlockSpec(memory_space=pltpu.SMEM)] *...  12.8 us
    convert_element_type x5, other arithmetic, add(): return sum((array.astype(F32) for array in arrays)).astype(BF)  9.69 us
    pallas_call x1, Pallas kernels, attend_own(): pl.pallas_call(kernel, grid_spec=pltpu.PrefetchScalarGridSpec(num_scalar_...  7.67 us
  transfers between devices with their start and end apart: 28, of which 11 were waited for; matrix products, arithmetic and copies ran while one was open for 6% of the time, Pallas kernels for 30%

commit v1 on v0

--- a/solution.py
+++ b/solution.py
@@ -649,24 +649,30 @@
     plus_high, minus_low = part(w_out, first, seg, (2, 2))
     plus_high = move(plus_high, True, 1)
     minus_low = move(minus_low, True, -1)
-    later = jnp.concatenate([plus[:2], minus[2:]])
-    plus_low, minus_high = part(w_out, later, seg, (2, 2))
-    plus_low = add(plus_low, two_low)
+    later = jnp.concatenate([plus[1:2], plus[:1], minus[2:]])
+    plus_1, plus_0, minus_high = part(w_out, later, seg, (0, 0, 2))
+    plus_1 = add(plus_1, two_low[1])
+    plus_0 = add(plus_0, two_low[0])
     minus_high = add(minus_high, two_high)
-    plus_low, minus_high, own, other = lax.optimization_barrier((plus_low, minus_high, own, other))
+    plus_1, plus_0, minus_high, own, other = lax.optimization_barrier(
+        (plus_1, plus_0, minus_high, own, other)
+    )
     here = output_part(own, other, w_out, here, seg, (0, 0, 0, 0))
-    plus_low = move(plus_low, True, 1)
+    plus_1 = move(plus_1, True, 1)
     minus_high = move(minus_high, True, -1)
-    plus_low, plus_high, minus_low, minus_high = lax.optimization_barrier(
-        (plus_low, plus_high, minus_low, minus_high)
-    )
-    mine, plus, two, minus = (
-        add(here[i], (plus_low, plus_high)[i // 2][i % 2], (minus_low, minus_high)[i // 2][i % 2])
-        for i in range(4)
-    )
-    return add(
-        tokens, mine, move(plus, False, 1), move(two, False, 2), move(minus, False, -1)
-    )
+    plus_0 = move(plus_0, True, 1)
+    plus_1, plus_high, minus_low, minus_high = lax.optimization_barrier(
+        (plus_1, plus_high, minus_low, minus_high)
+    )
+    sums = [
+        add(here[1], plus_1, minus_low[1]),
+        add(here[2], plus_high[0], minus_high[0]),
+        add(here[3], plus_high[1], minus_high[1]),
+    ]
+    after, opposite, before = (move(part, False, step) for part, step in zip(sums, (1, 2, -1)))
+    plus_0, *_ = lax.optimization_barrier((plus_0, *sums))
+    mine = lax.optimization_barrier(add(here[0], plus_0, minus_low[0]))
+    return add(tokens, mine, after, opposite, before)
 
 
 def solution(mesh):

time: 203 us -> 198 us (0.975)
  waiting for transfers between devices: 37.1 us -> 30.3 us
  other arithmetic: 15.3 us -> 17.5 us
    ppermute x19 -> x20, waiting for transfers between devices: 32.9 us -> 26 us  [move(): return lax.ppermute(array, AXES, plane_perm(first, step))]
    ppermute x19 -> x20, starting transfers between devices: 47.2 us -> 46 us  [move(): return lax.ppermute(array, AXES, plane_perm(first, step))]
    unnamed x36 -> x34, local copies, waits for them, and re-layouts: 13.5 us -> 12.5 us
    convert_element_type x5 -> x6, other arithmetic: 9.69 us -> 10.6 us  [add(): return sum((array.astype(F32) for array in arrays)).astype(BF)]
  transfers between devices with their start and end apart: 28 -> 29, of which waited for: 11 -> 11; matrix products, arithmetic and copies ran while one was open for 6% -> 9% of each run, Pallas kernels for 30% -> 30%
where the time goes in v1:
time: 198 us; the launch traced here: 196 us
  Pallas kernels  80.1 us (40%)
  starting transfers between devices  53.3 us (27%)
  waiting for transfers between devices  30.3 us (15%)
  other arithmetic  17.5 us (9%)
  local copies, waits for them, and re-layouts  14.4 us (7%)
    ppermute x20, starting transfers between devices, move(): return lax.ppermute(array, AXES, plane_perm(first, step))  46 us
    pallas_call x4, Pallas kernels, project(): pl.pallas_call(kernel, in_specs=in_specs, out_specs=out_specs, scratch_sh...  33.6 us
    ppermute x20, waiting for transfers between devices, move(): return lax.ppermute(array, AXES, plane_perm(first, step))  26 us
    pallas_call x3, Pallas kernels, attend_other(): pl.pallas_call(kernel, grid_spec=pltpu.PrefetchScalarGridSpec(num_scalar_...  24.8 us
    pallas_call x4, Pallas kernels, output_part(): pl.pallas_call(kernel, in_specs=[pl.BlockSpec(memory_space=pltpu.SMEM)] *...  13.1 us
    unnamed x34, local copies, waits for them, and re-layouts  12.5 us
    convert_element_type x6, other arithmetic, add(): return sum((array.astype(F32) for array in arrays)).astype(BF)  10.6 us
    pallas_call x1, Pallas kernels, attend_own(): pl.pallas_call(kernel, grid_spec=pltpu.PrefetchScalarGridSpec(num_scalar_...  7.67 us
  transfers between devices with their start and end apart: 29, of which 11 were waited for; matrix products, arithmetic and copies ran while one was open for 9% of the time, Pallas kernels for 30%

profile of v1, /device:TPU:6, one launch (start us, length us, event | category | flops | bytes accessed | tf_op | source)
XLA Modules:
  0.0 196.1 jit_solution(14604452444626021598)
XLA Ops:
  0.0 1.6 collective-permute-start
  1.6 1.7 collective-permute-start.2
  3.2 2.0 %collective-permute-start.4 = (bf16[1024,256]{1,0:T(8,128)(2,1)}, bf16[1024,256]{1,0:T(8,128)(2,1)}, u32[]{:S(2)}, u32[]{:S(2)}) collective-permute-start(bf16[1024,256]{1,0:T(8,128)(2,1)} %param.22), channel_id=1, source_target_pairs={{0,2},{1,3},{2,0},{3,1},{4,6},{5,7},{6,4},{7,5},{8,10},{9,11},{10,... | collective-permute-start | bytes 1572872 | tf_op jit(solution)/shard_map/ppermute | solution.py:43
  5.2 5.4 %collective-permute-done = bf16[1024,256]{1,0:T(8,128)(2,1)S(1)} collective-permute-done((bf16[1024,256]{1,0:T(8,128)(2,1)}, bf16[1024,256]{1,0:T(8,128)(2,1)S(1)}, u32[]{:S(2)}, u32[]{:S(2)}) %collective-permute-start) | collective-permute-done | bytes 524320 | tf_op jit(solution)/shard_map/ppermute | solution.py:43
  10.6 0.4 collective-permute-done.2
  11.0 2.5 %pad_maximum_fusion = (bf16[2,1024,256]{2,1,0:T(8,128)(2,1)}, bf16[2,1024,256]{2,1,0:T(8,128)(2,1)S(1)}) fusion(bf16[1,1024,256]{2,1,0:T(8,128)(2,1)} %bitcast.42, bf16[1,1024,256]{2,1,0:T(8,128)(2,1)S(1)} %bitcast.40, bf16[1,1024,256]{2,1,0:T(8,128)(2,1)S(1)} %bitcast.38), kind=kLoop, calls=%fused_computation.1 | loop fusion | flops 1048576 | bytes 3670016 | tf_op jit(solution)/shard_map/stack | solution.py:586
  13.5 1.9 collective-permute-start.1
  15.4 2.1 %collective-permute-start.3 = (bf16[2,1024,256]{2,1,0:T(8,128)(2,1)}, bf16[2,1024,256]{2,1,0:T(8,128)(2,1)S(1)}, u32[]{:S(2)}, u32[]{:S(2)}) collective-permute-start(bf16[2,1024,256]{2,1,0:T(8,128)(2,1)} %get-tuple-element.107), channel_id=1, source_target_pairs={{0,12},{1,13},{2,14},{3,15},{4,0},{5,1},{6,2},{7,3},{8,4},{9,5},{1... | collective-permute-start | bytes 3145736 | tf_op jit(solution)/shard_map/ppermute | solution.py:43
  17.6 2.6 %pad_maximum_fusion.2 = (bf16[2,1024,256]{2,1,0:T(8,128)(2,1)}, bf16[2,1024,256]{2,1,0:T(8,128)(2,1)S(1)}) fusion(bf16[1,1024,256]{2,1,0:T(8,128)(2,1)} %bitcast.6, bf16[1,1024,256]{2,1,0:T(8,128)(2,1)} %bitcast.39, bf16[1,1024,256]{2,1,0:T(8,128)(2,1)} %bitcast.41), kind=kLoop, calls=%fused_computation.3 | loop fusion | flops 1048576 | bytes 3670016 | tf_op jit(solution)/shard_map/stack | solution.py:591
  20.1 4.0 %collective-permute-start.6 = (bf16[2,1024,256]{2,1,0:T(8,128)(2,1)}, bf16[2,1024,256]{2,1,0:T(8,128)(2,1)}, u32[]{:S(2)}, u32[]{:S(2)}) collective-permute-start(bf16[2,1024,256]{2,1,0:T(8,128)(2,1)} %get-tuple-element.105), channel_id=1, source_target_pairs={{0,12},{1,13},{2,14},{3,15},{4,0},{5,1},{6,2},{7,3},{8,4},{9,5},{1... | collective-permute-start | bytes 3145736 | tf_op jit(solution)/shard_map/ppermute | solution.py:43
  24.2 0.2 select_reduce_fusion.1
  24.6 7.6 %shard_map.208 = (f32[1024,1]{1,0:T(8,128)S(1)}, f32[1024,768]{1,0:T(8,128)}) custom-call(s32[4]{0:T(128)S(1)} %get-tuple-element.114.table_ref, s32[7]{0:T(128)S(1)} %pad_add_fusion.seg_ref, bf16[2,1024,256]{2,1,0:T(8,128)(2,1)S(1)} %get-tuple-element.108.refs_0_, bf16[2,1024,256]{2,1,0:T(8,128)(2,1)S(1)} %get-tuple-element.106.refs_1_, ...), custom_call_target="tpu_custom_call" | custom-call | flops 2491416576 | bytes 6815744 | tf_op jit(solution)/shard_map/pallas_call | solution.py:248
  32.2 0.8 copy-done.3
  33.1 15.2 %collective-permute-start.9 = (bf16[1,1024,256]{2,1,0:T(8,128)(2,1)S(1)}, bf16[1,1024,256]{2,1,0:T(8,128)(2,1)S(1)}, u32[]{:S(2)}, u32[]{:S(2)}) collective-permute-start(bf16[1,1024,256]{2,1,0:T(8,128)(2,1)S(1)} %slice.49), channel_id=1, source_target_pairs={{0,12},{1,13},{2,14},{3,15},{4,0},{5,1},{6,2},{7,3},{8,4},{9,5},{1... | collective-permute-start | bytes 1572872 | tf_op jit(solution)/shard_map/ppermute | solution.py:43
  48.3 1.0 copy-done.4
  49.3 8.3 %shard_map.209 = (f32[1024,1]{1,0:T(8,128)S(1)}, f32[1024,768]{1,0:T(8,128)}) custom-call(s32[4]{0:T(128)S(1)} %get-tuple-element.113.table_ref, s32[7]{0:T(128)S(1)} %pad_add_fusion.seg_ref, bf16[2,1024,256]{2,1,0:T(8,128)(2,1)} %collective-permute-done.1.refs_0_, bf16[2,1024,256]{2,1,0:T(8,128)(2,1)S(1)} %collective-permute-done.3.refs_1_, ...), custom_call_target="tpu_custom_call" | custom-call | flops 2491416576 | bytes 6815744 | tf_op jit(solution)/shard_map/pallas_call | solution.py:248
  57.7 1.1 slice.48
  58.7 2.1 %collective-permute-start.7 = (bf16[1,1024,256]{2,1,0:T(8,128)(2,1)S(1)}, bf16[1,1024,256]{2,1,0:T(8,128)(2,1)S(1)}, u32[]{:S(2)}, u32[]{:S(2)}) collective-permute-start(bf16[1,1024,256]{2,1,0:T(8,128)(2,1)S(1)} %slice.48), channel_id=1, source_target_pairs={{0,12},{1,13},{2,14},{3,15},{4,0},{5,1},{6,2},{7,3},{8,4},{9,5},{1... | collective-permute-start | bytes 1572872 | tf_op jit(solution)/shard_map/ppermute | solution.py:43
  60.9 9.8 %shard_map.210 = (f32[1024,1]{1,0:T(8,128)S(1)}, f32[1024,768]{1,0:T(8,128)}) custom-call(s32[5]{0:T(128)S(1)} %broadcast_select_fusion.table_ref, s32[7]{0:T(128)S(1)} %pad_add_fusion.seg_ref, bf16[2,1024,256]{2,1,0:T(8,128)(2,1)} %collective-permute-done.8.refs_0_, bf16[2,1024,256]{2,1,0:T(8,128)(2,1)} %collective-permute-done.6.refs_1_, ...), custom_call_target="tpu_custom_call" | custom-call | flops 3114270720 | bytes 8519680 | tf_op jit(solution)/shard_map/pallas_call | solution.py:248
  70.7 7.8 %shard_map.211 = (bf16[1024,128]{1,0:T(8,128)(2,1)S(1)}, bf16[1024,256]{1,0:T(8,128)(2,1)S(1)}, bf16[1024,128]{1,0:T(8,128)(2,1)}, bf16[1024,256]{1,0:T(8,128)(2,1)S(1)}) custom-call(s32[3]{0:T(128)S(1)} %broadcast_select_fusion.1.table_ref, s32[7]{0:T(128)S(1)} %pad_add_fusion.seg_ref, bf16[2,1024,256]{2,1,0:T(8,128)(2,1)S(1)} %collective-permute-done.5.refs_0_, ...), custom_call_target="tpu_custom_call" | custom-call | flops 1868562432 | bytes 5111808 | tf_op jit(solution)/shard_map/pallas_call | solution.py:248
  78.5 0.1 collective-permute-start.12
  78.6 0.5 collective-permute-start.11
  79.2 1.5 collective-permute-done.12.kv_other_ref
  80.6 0.8 collective-permute-start.13
  81.5 2.8 %copy-done = bf16[3,256,4096]{2,1,0:T(8,128)(2,1)S(1)} copy-done((bf16[3,256,4096]{2,1,0:T(8,128)(2,1)S(1)}, bf16[3,256,4096]{2,1,0:T(8,128)(2,1)}, u32[]{:S(2)}) %copy-start) | copy-done | bytes 6291480
  84.3 1.0 shard_map.213.weight_ref
  85.3 0.6 collective-permute-start.15
  85.9 3.1 %collective-permute-start.14 = (bf16[1024,256]{1,0:T(8,128)(2,1)}, bf16[1024,256]{1,0:T(8,128)(2,1)}, u32[]{:S(2)}, u32[]{:S(2)}) collective-permute-start(bf16[1024,256]{1,0:T(8,128)(2,1)} %collective-permute-done.12.kv_other_ref), channel_id=1, source_target_pairs={{0,32},{16,48},{32,64},{48,80},{64,96},{80,112},{96,0},{112,16},{1... | collective-permute-start | bytes 1572872 | tf_op jit(solution)/shard_map/ppermute | solution.py:48
  89.0 7.7 %shard_map.212.before_ref = f32[4,144,512]{2,1,0:T(8,128)S(1)} custom-call(s32[1]{0:T(128)} %bitcast.core_ref, bf16[1024,128]{1,0:T(8,128)(2,1)S(1)} %get-tuple-element.68.query_ref, bf16[1024,128]{1,0:T(8,128)(2,1)S(1)} %collective-permute-done.10.query_other_ref, bf16[1024,256]{1,0:T(8,128)(2,1)S(1)} %get-tuple-element.70.kv_ref, ...), custom_call_target="tpu_custom_call" | custom-call | flops 1342177280 | bytes 4194304 | tf_op jit(solution)/shard_map/pallas_call | solution.py:353
  96.6 1.1 copy-done.5
  97.7 1.2 collective-permute-start.16
  98.9 0.8 collective-permute-start.17
  99.9 1.3 copy-done.6
  101.2 8.1 %shard_map.214.before_ref = f32[4,144,512]{2,1,0:T(8,128)S(1)} custom-call(s32[2]{0:T(128)S(1)} %add_convert_fusion.3.use_ref, bf16[1024,128]{1,0:T(8,128)(2,1)S(1)} %get-tuple-element.68.query_ref, bf16[1024,128]{1,0:T(8,128)(2,1)S(1)} %collective-permute-done.10.query_other_ref, f32[4,144,512]{2,1,0:T(8,128)S(1)} %copy-done.6, ...), custom_call_target="tpu_custom_call" | custom-call | flops 2147483648 | bytes 6291456 | tf_op jit(solution)/shard_map/pallas_call | solution.py:450
  109.2 8.2 %shard_map.215.before_ref = f32[4,144,512]{2,1,0:T(8,128)S(1)} custom-call(s32[2]{0:T(128)S(1)} %add_convert_fusion.3.use_ref, bf16[1024,128]{1,0:T(8,128)(2,1)S(1)} %get-tuple-element.68.query_ref, bf16[1024,128]{1,0:T(8,128)(2,1)S(1)} %collective-permute-done.10.query_other_ref, f32[4,144,512]{2,1,0:T(8,128)S(1)} %shard_map.214.before_ref, ...), custom_call_target="tpu_custom_call" | custom-call | flops 2147483648 | bytes 6291456 | tf_op jit(solution)/shard_map/pallas_call | solution.py:450
  117.4 1.2 collective-permute-done.17.refs_1_
  118.6 8.5 %shard_map.216 = (bf16[1024,128]{1,0:T(8,128)(2,1)S(1)}, bf16[1024,128]{1,0:T(8,128)(2,1)S(1)}) custom-call(s32[2]{0:T(128)S(1)} %add_convert_fusion.2.use_ref, bf16[1024,128]{1,0:T(8,128)(2,1)S(1)} %get-tuple-element.68.query_ref, bf16[1024,128]{1,0:T(8,128)(2,1)S(1)} %collective-permute-done.10.query_other_ref, f32[4,144,512]{2,1,0:T(8,128)S(1)} %shard_map.215.before_ref, ...), custom_call_target="tpu_custom_call" | custom-call | flops 2147483648 | bytes 6291456 | tf_op jit(solution)/shard_map/pallas_call | solution.py:450
  127.2 0.1 collective-permute-start.18
  127.3 1.5 collective-permute-done.18.other_ref
  128.8 4.0 %shard_map.218 = (bf16[2,1024,256]{2,1,0:T(8,128)(2,1)}, bf16[2,1024,256]{2,1,0:T(8,128)(2,1)}) custom-call(s32[4]{0:T(128)S(1)} %broadcast_select_fusion.2.table_ref, s32[7]{0:T(128)S(1)} %pad_add_fusion.seg_ref, bf16[1024,128]{1,0:T(8,128)(2,1)S(1)} %get-tuple-element.83.own_ref, bf16[1024,128]{1,0:T(8,128)(2,1)S(1)} %collective-permute-done.18.other_ref, ...), custom_call_target="tpu_custom_call" | custom-call | bytes 1024 | tf_op jit(solution)/shard_map/pallas_call | solution.py:554
  132.7 6.5 %collective-permute-start.20 = (bf16[2,1024,256]{2,1,0:T(8,128)(2,1)}, bf16[2,1024,256]{2,1,0:T(8,128)(2,1)}, u32[]{:S(2)}, u32[]{:S(2)}) collective-permute-start(bf16[2,1024,256]{2,1,0:T(8,128)(2,1)} %get-tuple-element.82), channel_id=1, source_target_pairs={{0,3},{1,0},{2,1},{3,2},{4,7},{5,4},{6,5},{7,6},{8,11},{9,8},{10,9... | collective-permute-start | bytes 3145736 | tf_op jit(solution)/shard_map/ppermute | solution.py:43
  139.5 0.6 fusion.14
  140.1 1.4 pad_add_fusion.1.table_ref
  141.4 2.8 %copy-done.1 = bf16[3,256,4096]{2,1,0:T(8,128)(2,1)S(1)} copy-done((bf16[3,256,4096]{2,1,0:T(8,128)(2,1)S(1)}, bf16[3,256,4096]{2,1,0:T(8,128)(2,1)}, u32[]{:S(2)}) %copy-start.1) | copy-done | bytes 6291480
  144.2 3.0 %shard_map.220 = (bf16[2,1024,256]{2,1,0:T(8,128)(2,1)S(1)}, bf16[2,1024,256]{2,1,0:T(8,128)(2,1)S(1)}) custom-call(s32[4]{0:T(128)S(1)} %pad_add_fusion.2.table_ref, s32[7]{0:T(128)S(1)} %pad_add_fusion.seg_ref, bf16[1024,128]{1,0:T(8,128)(2,1)S(1)} %get-tuple-element.83.own_ref, bf16[1024,128]{1,0:T(8,128)(2,1)S(1)} %collective-permute-done.18.other_ref, ...), custom_call_target="tpu_custom_call" | custom-call | bytes 1024 | tf_op jit(solution)/shard_map/pallas_call | solution.py:554
  147.3 3.3 %collective-permute-start.24 = (bf16[2,1024,256]{2,1,0:T(8,128)(2,1)S(1)}, bf16[2,1024,256]{2,1,0:T(8,128)(2,1)}, u32[]{:S(2)}, u32[]{:S(2)}) collective-permute-start(bf16[2,1024,256]{2,1,0:T(8,128)(2,1)S(1)} %get-tuple-element.90), channel_id=1, source_target_pairs={{0,3},{1,0},{2,1},{3,2},{4,7},{5,4},{6,5},{7,6},{8,11},{9,8},{10,9... | collective-permute-start | bytes 3145736 | tf_op jit(solution)/shard_map/ppermute | solution.py:43
  150.6 3.0 %shard_map.217 = (bf16[1024,256]{1,0:T(8,128)(2,1)S(1)}, bf16[1024,256]{1,0:T(8,128)(2,1)S(1)}, bf16[2,1024,256]{2,1,0:T(8,128)(2,1)S(1)}) custom-call(s32[4]{0:T(128)S(1)} %pad_add_fusion.1.table_ref, s32[7]{0:T(128)S(1)} %pad_add_fusion.seg_ref, bf16[1024,128]{1,0:T(8,128)(2,1)S(1)} %get-tuple-element.83.own_ref, ...), custom_call_target="tpu_custom_call" | custom-call | bytes 1024 | tf_op jit(solution)/shard_map/pallas_call | solution.py:554
  153.6 2.5 %add_convert_fusion = bf16[2,1024,256]{2,1,0:T(8,128)(2,1)} fusion(bf16[2,1024,256]{2,1,0:T(8,128)(2,1)} %collective-permute-done.20, bf16[2,1024,256]{2,1,0:T(8,128)(2,1)S(1)} %get-tuple-element.81), kind=kLoop, calls=%fused_computation | loop fusion | flops 2097152 | bytes 3145728 | tf_op jit(solution)/shard_map/convert_element_type | solution.py:575
  156.1 2.3 %fusion.4 = (bf16[1024,256]{1,0:T(8,128)(2,1)S(1)}, bf16[1024,256]{1,0:T(8,128)(2,1)}) fusion(bf16[1024,256]{1,0:T(8,128)(2,1)S(1)} %get-tuple-element.80, bf16[2,1024,256]{2,1,0:T(8,128)(2,1)} %collective-permute-done.19, bf16[1024,256]{1,0:T(8,128)(2,1)S(1)} %get-tuple-element.77), kind=kLoop, calls=%fused_computation.16 | loop fusion | flops 2097152 | bytes 3145728 | tf_op jit(solution)/shard_map/convert_element_type | solution.py:575
  158.3 2.0 %collective-permute-start.25 = (bf16[2,1024,256]{2,1,0:T(8,128)(2,1)}, bf16[2,1024,256]{2,1,0:T(8,128)(2,1)}, u32[]{:S(2)}, u32[]{:S(2)}) collective-permute-start(bf16[2,1024,256]{2,1,0:T(8,128)(2,1)} %add_convert_fusion), channel_id=1, source_target_pairs={{0,3},{1,0},{2,1},{3,2},{4,7},{5,4},{6,5},{7,6},{8,11},{9,8},{10,9... | collective-permute-start | bytes 3145736 | tf_op jit(solution)/shard_map/ppermute | solution.py:43
  160.5 2.8 %copy-done.2 = bf16[3,256,4096]{2,1,0:T(8,128)(2,1)S(1)} copy-done((bf16[3,256,4096]{2,1,0:T(8,128)(2,1)S(1)}, bf16[3,256,4096]{2,1,0:T(8,128)(2,1)}, u32[]{:S(2)}) %copy-start.2) | copy-done | bytes 6291480
  163.3 3.2 %shard_map.219 = (bf16[1024,256]{1,0:T(8,128)(2,1)S(1)}, bf16[1024,256]{1,0:T(8,128)(2,1)S(1)}, bf16[1024,256]{1,0:T(8,128)(2,1)S(1)}, bf16[1024,256]{1,0:T(8,128)(2,1)S(1)}) custom-call(s32[4]{0:T(128)S(1)} %broadcast_select_fusion.7.table_ref, s32[7]{0:T(128)S(1)} %pad_add_fusion.seg_ref, bf16[1024,128]{1,0:T(8,128)(2,1)S(1)} %get-tuple-element.83.own_ref, ...), custom_call_target="tpu_custom_call" | custom-call | bytes 1024 | tf_op jit(solution)/shard_map/pallas_call | solution.py:554
  166.5 0.3 collective-permute-done.23
  166.8 5.6 %collective-permute-done.22 = bf16[1024,256]{1,0:T(8,128)(2,1)} collective-permute-done((bf16[1024,256]{1,0:T(8,128)(2,1)}, bf16[1024,256]{1,0:T(8,128)(2,1)}, u32[]{:S(2)}, u32[]{:S(2)}) %collective-permute-start.22) | collective-permute-done | bytes 524320 | tf_op jit(solution)/shard_map/ppermute | solution.py:43
  172.4 1.9 collective-permute-done.25
  174.3 1.4 fusion.3
  175.7 0.1 collective-permute-start.26
  175.8 2.0 %fusion.2 = (bf16[1024,256]{1,0:T(8,128)(2,1)S(1)}, bf16[1024,256]{1,0:T(8,128)(2,1)S(1)}) fusion(bf16[1024,256]{1,0:T(8,128)(2,1)S(1)} %get-tuple-element.94, bf16[2,1024,256]{2,1,0:T(8,128)(2,1)} %collective-permute-done.25, bf16[2,1024,256]{2,1,0:T(8,128)(2,1)} %collective-permute-done.23, bf16[1024,256]{1,0:T(8,128)(2,1)S(1)} %get-tuple-element.97), kind=kLoop, calls=%fused_computation.11 | loop fusion | flops 3145728 | bytes 4194304 | tf_op jit(solution)/shard_map/convert_element_type | solution.py:575
  177.8 2.0 %collective-permute-start.27 = (bf16[1024,256]{1,0:T(8,128)(2,1)S(1)}, bf16[1024,256]{1,0:T(8,128)(2,1)S(1)}, u32[]{:S(2)}, u32[]{:S(2)}) collective-permute-start(bf16[1024,256]{1,0:T(8,128)(2,1)S(1)} %get-tuple-element.101), channel_id=1, source_target_pairs={{0,8},{1,9},{2,10},{3,11},{4,12},{5,13},{6,14},{7,15},{8,0},{9,1},... | collective-permute-start | bytes 1572872 | tf_op jit(solution)/shard_map/ppermute | solution.py:43
  179.8 1.4 collective-permute-start.28
  181.2 1.3 fusion
  182.5 9.3 %collective-permute-done.26 = bf16[1024,256]{1,0:T(8,128)(2,1)S(1)} collective-permute-done((bf16[1024,256]{1,0:T(8,128)(2,1)S(1)}, bf16[1024,256]{1,0:T(8,128)(2,1)S(1)}, u32[]{:S(2)}, u32[]{:S(2)}) %collective-permute-start.26) | collective-permute-done | bytes 524320 | tf_op jit(solution)/shard_map/ppermute | solution.py:43
  191.8 3.0 %collective-permute-done.28 = bf16[1024,256]{1,0:T(8,128)(2,1)S(1)} collective-permute-done((bf16[1024,256]{1,0:T(8,128)(2,1)S(1)}, bf16[1024,256]{1,0:T(8,128)(2,1)S(1)}, u32[]{:S(2)}, u32[]{:S(2)}) %collective-permute-start.28) | collective-permute-done | bytes 524320 | tf_op jit(solution)/shard_map/ppermute | solution.py:43
  194.8 1.1 add_convert_fusion.1
  (68 shorter events, 1.0 us)
Async XLA Ops:
  0.0 10.6 %collective-permute-start = (bf16[1024,256]{1,0:T(8,128)(2,1)}, bf16[1024,256]{1,0:T(8,128)(2,1)S(1)}, u32[]{:S(2)}, u32[]{:S(2)}) collective-permute-start(bf16[1024,256]{1,0:T(8,128)(2,1)} %param.22), channel_id=1, source_target_pairs={{0,1},{1,2},{2,3},{3,0},{4,5},{5,6},{6,7},{7,4},{8,9},{9,10},{10,1... | collective-permute-start | bytes 1572872 | tf_op jit(solution)/shard_map/ppermute | solution.py:43
  1.6 9.4 %collective-permute-start.2 = (bf16[1024,256]{1,0:T(8,128)(2,1)}, bf16[1024,256]{1,0:T(8,128)(2,1)S(1)}, u32[]{:S(2)}, u32[]{:S(2)}) collective-permute-start(bf16[1024,256]{1,0:T(8,128)(2,1)} %param.22), channel_id=1, source_target_pairs={{0,3},{1,0},{2,1},{3,2},{4,7},{5,4},{6,5},{7,6},{8,11},{9,8},{10,9... | collective-permute-start | bytes 1572872 | tf_op jit(solution)/shard_map/ppermute | solution.py:43
  3.2 14.3 %collective-permute-start.4 = (bf16[1024,256]{1,0:T(8,128)(2,1)}, bf16[1024,256]{1,0:T(8,128)(2,1)}, u32[]{:S(2)}, u32[]{:S(2)}) collective-permute-start(bf16[1024,256]{1,0:T(8,128)(2,1)} %param.22), channel_id=1, source_target_pairs={{0,2},{1,3},{2,0},{3,1},{4,6},{5,7},{6,4},{7,5},{8,10},{9,11},{10,... | collective-permute-start | bytes 1572872 | tf_op jit(solution)/shard_map/ppermute | solution.py:43
  10.6 7.0 %copy-start.7 = (bf16[1024,256]{1,0:T(8,128)(2,1)}, bf16[1024,256]{1,0:T(8,128)(2,1)S(1)}, u32[]{:S(2)}) copy-start(bf16[1024,256]{1,0:T(8,128)(2,1)S(1)} %collective-permute-done) | copy-start | bytes 1572868
  11.0 6.6 %copy-start.8 = (bf16[1024,256]{1,0:T(8,128)(2,1)}, bf16[1024,256]{1,0:T(8,128)(2,1)S(1)}, u32[]{:S(2)}) copy-start(bf16[1024,256]{1,0:T(8,128)(2,1)S(1)} %collective-permute-done.2) | copy-start | bytes 1572868
  11.0 13.2 %copy-start.10 = (s32[1024]{0:T(1024)S(1)}, s32[1024]{0:T(1024)}, u32[]{:S(2)}) copy-start(s32[1024]{0:T(1024)} %param.23) | copy-start | bytes 12292
  11.0 13.4 %copy-start.11 = (s32[4]{0:T(128)S(1)}, s32[4]{0:T(128)}, u32[]{:S(2)}) copy-start(s32[4]{0:T(128)} %constant.221.clone) | copy-start | bytes 52
  11.0 13.4 %copy-start.12 = (s32[4]{0:T(128)S(1)}, s32[4]{0:T(128)}, u32[]{:S(2)}) copy-start(s32[4]{0:T(128)} %constant.223.clone) | copy-start | bytes 52
  11.0 13.4 %copy-start.13 = (s32[4]{0:T(128)S(1)}, s32[4]{0:T(128)}, u32[]{:S(2)}) copy-start(s32[4]{0:T(128)} %constant.224.clone) | copy-start | bytes 52
  13.5 19.5 %collective-permute-start.1 = (bf16[2,1024,256]{2,1,0:T(8,128)(2,1)S(1)}, bf16[2,1024,256]{2,1,0:T(8,128)(2,1)}, u32[]{:S(2)}, u32[]{:S(2)}) collective-permute-start(bf16[2,1024,256]{2,1,0:T(8,128)(2,1)S(1)} %get-tuple-element.108.refs_0_), channel_id=1, source_target_pairs={{0,4},{1,5},{2,6},{3,7},{4,8},{5,9},{6,10},{7,11},{8,12},{9,13},{1... | collective-permute-start | bytes 3145736 | tf_op jit(solution)/shard_map/ppermute | solution.py:43
  15.4 17.6 %collective-permute-start.3 = (bf16[2,1024,256]{2,1,0:T(8,128)(2,1)}, bf16[2,1024,256]{2,1,0:T(8,128)(2,1)S(1)}, u32[]{:S(2)}, u32[]{:S(2)}) collective-permute-start(bf16[2,1024,256]{2,1,0:T(8,128)(2,1)} %get-tuple-element.107), channel_id=1, source_target_pairs={{0,12},{1,13},{2,14},{3,15},{4,0},{5,1},{6,2},{7,3},{8,4},{9,5},{1... | collective-permute-start | bytes 3145736 | tf_op jit(solution)/shard_map/ppermute | solution.py:43
  20.1 37.5 %collective-permute-start.6 = (bf16[2,1024,256]{2,1,0:T(8,128)(2,1)}, bf16[2,1024,256]{2,1,0:T(8,128)(2,1)}, u32[]{:S(2)}, u32[]{:S(2)}) collective-permute-start(bf16[2,1024,256]{2,1,0:T(8,128)(2,1)} %get-tuple-element.105), channel_id=1, source_target_pairs={{0,12},{1,13},{2,14},{3,15},{4,0},{5,1},{6,2},{7,3},{8,4},{9,5},{1... | collective-permute-start | bytes 3145736 | tf_op jit(solution)/shard_map/ppermute | solution.py:43
  24.4 36.5 %collective-permute-start.8 = (bf16[2,1024,256]{2,1,0:T(8,128)(2,1)S(1)}, bf16[2,1024,256]{2,1,0:T(8,128)(2,1)}, u32[]{:S(2)}, u32[]{:S(2)}) collective-permute-start(bf16[2,1024,256]{2,1,0:T(8,128)(2,1)S(1)} %get-tuple-element.106.refs_1_), channel_id=1, source_target_pairs={{0,4},{1,5},{2,6},{3,7},{4,8},{5,9},{6,10},{7,11},{8,12},{9,13},{1... | collective-permute-start | bytes 3145736 | tf_op jit(solution)/shard_map/ppermute | solution.py:43
  32.2 0.8 copy-start.3
  33.0 37.7 %collective-permute-start.5 = (bf16[2,1024,256]{2,1,0:T(8,128)(2,1)}, bf16[2,1024,256]{2,1,0:T(8,128)(2,1)S(1)}, u32[]{:S(2)}, u32[]{:S(2)}) collective-permute-start(bf16[2,1024,256]{2,1,0:T(8,128)(2,1)} %collective-permute-done.1.refs_0_), channel_id=1, source_target_pairs={{0,4},{1,5},{2,6},{3,7},{4,8},{5,9},{6,10},{7,11},{8,12},{9,13},{1... | collective-permute-start | bytes 3145736 | tf_op jit(solution)/shard_map/ppermute | solution.py:43
  33.1 27.8 %collective-permute-start.9 = (bf16[1,1024,256]{2,1,0:T(8,128)(2,1)S(1)}, bf16[1,1024,256]{2,1,0:T(8,128)(2,1)S(1)}, u32[]{:S(2)}, u32[]{:S(2)}) collective-permute-start(bf16[1,1024,256]{2,1,0:T(8,128)(2,1)S(1)} %slice.49), channel_id=1, source_target_pairs={{0,12},{1,13},{2,14},{3,15},{4,0},{5,1},{6,2},{7,3},{8,4},{9,5},{1... | collective-permute-start | bytes 1572872 | tf_op jit(solution)/shard_map/ppermute | solution.py:43
  48.3 1.0 copy-start.4
  49.3 11.5 %copy-start.16 = (s32[3]{0:T(128)S(1)}, s32[3]{0:T(128)}, u32[]{:S(2)}) copy-start(s32[3]{0:T(128)} %constant.227.clone) | copy-start | bytes 40
  49.3 11.5 %copy-start.14 = (s32[5]{0:T(128)S(1)}, s32[5]{0:T(128)}, u32[]{:S(2)}) copy-start(s32[5]{0:T(128)} %constant.225.clone) | copy-start | bytes 64
  49.3 11.5 %copy-start.15 = (s32[5]{0:T(128)S(1)}, s32[5]{0:T(128)}, u32[]{:S(2)}) copy-start(s32[5]{0:T(128)} %constant.226.clone) | copy-start | bytes 64
  58.7 12.0 %collective-permute-start.7 = (bf16[1,1024,256]{2,1,0:T(8,128)(2,1)S(1)}, bf16[1,1024,256]{2,1,0:T(8,128)(2,1)S(1)}, u32[]{:S(2)}, u32[]{:S(2)}) collective-permute-start(bf16[1,1024,256]{2,1,0:T(8,128)(2,1)S(1)} %slice.48), channel_id=1, source_target_pairs={{0,12},{1,13},{2,14},{3,15},{4,0},{5,1},{6,2},{7,3},{8,4},{9,5},{1... | collective-permute-start | bytes 1572872 | tf_op jit(solution)/shard_map/ppermute | solution.py:43
  78.5 2.1 %collective-permute-start.12 = (bf16[1024,256]{1,0:T(8,128)(2,1)S(1)}, bf16[1024,256]{1,0:T(8,128)(2,1)}, u32[]{:S(2)}, u32[]{:S(2)}) collective-permute-start(bf16[1024,256]{1,0:T(8,128)(2,1)S(1)} %get-tuple-element.71), channel_id=1, source_target_pairs={{0,16},{16,0},{32,48},{48,32},{64,80},{80,64},{96,112},{112,96},{1... | collective-permute-start | bytes 1572872 | tf_op jit(solution)/shard_map/ppermute | solution.py:52
  78.6 19.1 %collective-permute-start.11 = (bf16[1024,256]{1,0:T(8,128)(2,1)S(1)}, bf16[1024,256]{1,0:T(8,128)(2,1)S(1)}, u32[]{:S(2)}, u32[]{:S(2)}) collective-permute-start(bf16[1024,256]{1,0:T(8,128)(2,1)S(1)} %get-tuple-element.70.kv_ref), channel_id=1, source_target_pairs={{0,32},{16,48},{32,64},{48,80},{64,96},{80,112},{96,0},{112,16},{1... | collective-permute-start | bytes 1572872 | tf_op jit(solution)/shard_map/ppermute | solution.py:48
  80.6 17.1 %collective-permute-start.13 = (bf16[1024,256]{1,0:T(8,128)(2,1)}, bf16[1024,256]{1,0:T(8,128)(2,1)}, u32[]{:S(2)}, u32[]{:S(2)}) collective-permute-start(bf16[1024,256]{1,0:T(8,128)(2,1)} %collective-permute-done.12.kv_other_ref), channel_id=1, source_target_pairs={{0,96},{16,112},{32,0},{48,16},{64,32},{80,48},{96,64},{112,80},{1... | collective-permute-start | bytes 1572872 | tf_op jit(solution)/shard_map/ppermute | solution.py:48
  81.5 7.5 %collective-permute-start.10 = (bf16[1024,128]{1,0:T(8,128)(2,1)}, bf16[1024,128]{1,0:T(8,128)(2,1)S(1)}, u32[]{:S(2)}, u32[]{:S(2)}) collective-permute-start(bf16[1024,128]{1,0:T(8,128)(2,1)} %get-tuple-element.69), channel_id=1, source_target_pairs={{0,16},{16,0},{32,48},{48,32},{64,80},{80,64},{96,112},{112,96},{1... | collective-permute-start | bytes 786440 | tf_op jit(solution)/shard_map/ppermute | solution.py:52
  81.5 2.8 %copy-start = (bf16[3,256,4096]{2,1,0:T(8,128)(2,1)S(1)}, bf16[3,256,4096]{2,1,0:T(8,128)(2,1)}, u32[]{:S(2)}) copy-start(bf16[3,256,4096]{2,1,0:T(8,128)(2,1)} %weight_ref.7) | copy-start | bytes 18874372
  85.3 24.0 %collective-permute-start.15 = (bf16[1024,256]{1,0:T(8,128)(2,1)S(1)}, bf16[1024,256]{1,0:T(8,128)(2,1)}, u32[]{:S(2)}, u32[]{:S(2)}) collective-permute-start(bf16[1024,256]{1,0:T(8,128)(2,1)S(1)} %get-tuple-element.70.kv_ref), channel_id=1, source_target_pairs={{0,96},{16,112},{32,0},{48,16},{64,32},{80,48},{96,64},{112,80},{1... | collective-permute-start | bytes 1572872 | tf_op jit(solution)/shard_map/ppermute | solution.py:48
  85.9 23.4 %collective-permute-start.14 = (bf16[1024,256]{1,0:T(8,128)(2,1)}, bf16[1024,256]{1,0:T(8,128)(2,1)}, u32[]{:S(2)}, u32[]{:S(2)}) collective-permute-start(bf16[1024,256]{1,0:T(8,128)(2,1)} %collective-permute-done.12.kv_other_ref), channel_id=1, source_target_pairs={{0,32},{16,48},{32,64},{48,80},{64,96},{80,112},{96,0},{112,16},{1... | collective-permute-start | bytes 1572872 | tf_op jit(solution)/shard_map/ppermute | solution.py:48
  96.6 1.1 copy-start.5
  97.7 19.7 %collective-permute-start.16 = (bf16[1024,256]{1,0:T(8,128)(2,1)S(1)}, bf16[1024,256]{1,0:T(8,128)(2,1)}, u32[]{:S(2)}, u32[]{:S(2)}) collective-permute-start(bf16[1024,256]{1,0:T(8,128)(2,1)S(1)} %collective-permute-done.11.refs_0_), channel_id=1, source_target_pairs={{0,32},{16,48},{32,64},{48,80},{64,96},{80,112},{96,0},{112,16},{1... | collective-permute-start | bytes 1572872 | tf_op jit(solution)/shard_map/ppermute | solution.py:48
  98.9 19.7 %collective-permute-start.17 = (bf16[1024,256]{1,0:T(8,128)(2,1)}, bf16[1024,256]{1,0:T(8,128)(2,1)}, u32[]{:S(2)}, u32[]{:S(2)}) collective-permute-start(bf16[1024,256]{1,0:T(8,128)(2,1)} %collective-permute-done.13.refs_1_), channel_id=1, source_target_pairs={{0,96},{16,112},{32,0},{48,16},{64,32},{80,48},{96,64},{112,80},{1... | collective-permute-start | bytes 1572872 | tf_op jit(solution)/shard_map/ppermute | solution.py:48
  99.9 1.3 copy-start.6
  127.2 1.6 collective-permute-start.18
  132.7 20.8 %collective-permute-start.20 = (bf16[2,1024,256]{2,1,0:T(8,128)(2,1)}, bf16[2,1024,256]{2,1,0:T(8,128)(2,1)}, u32[]{:S(2)}, u32[]{:S(2)}) collective-permute-start(bf16[2,1024,256]{2,1,0:T(8,128)(2,1)} %get-tuple-element.82), channel_id=1, source_target_pairs={{0,3},{1,0},{2,1},{3,2},{4,7},{5,4},{6,5},{7,6},{8,11},{9,8},{10,9... | collective-permute-start | bytes 3145736 | tf_op jit(solution)/shard_map/ppermute | solution.py:43
  139.2 16.8 %collective-permute-start.19 = (bf16[2,1024,256]{2,1,0:T(8,128)(2,1)}, bf16[2,1024,256]{2,1,0:T(8,128)(2,1)}, u32[]{:S(2)}, u32[]{:S(2)}) collective-permute-start(bf16[2,1024,256]{2,1,0:T(8,128)(2,1)} %get-tuple-element.79), channel_id=1, source_target_pairs={{0,1},{1,2},{2,3},{3,0},{4,5},{5,6},{6,7},{7,4},{8,9},{9,10},{10,1... | collective-permute-start | bytes 3145736 | tf_op jit(solution)/shard_map/ppermute | solution.py:43
  141.4 2.8 %copy-start.1 = (bf16[3,256,4096]{2,1,0:T(8,128)(2,1)S(1)}, bf16[3,256,4096]{2,1,0:T(8,128)(2,1)}, u32[]{:S(2)}) copy-start(bf16[3,256,4096]{2,1,0:T(8,128)(2,1)} %weight_ref.7) | copy-start | bytes 18874372
  147.2 19.6 %collective-permute-start.23 = (bf16[2,1024,256]{2,1,0:T(8,128)(2,1)S(1)}, bf16[2,1024,256]{2,1,0:T(8,128)(2,1)}, u32[]{:S(2)}, u32[]{:S(2)}) collective-permute-start(bf16[2,1024,256]{2,1,0:T(8,128)(2,1)S(1)} %get-tuple-element.89), channel_id=1, source_target_pairs={{0,1},{1,2},{2,3},{3,0},{4,5},{5,6},{6,7},{7,4},{8,9},{9,10},{10,1... | collective-permute-start | bytes 3145736 | tf_op jit(solution)/shard_map/ppermute | solution.py:43
  147.3 19.5 %collective-permute-start.24 = (bf16[2,1024,256]{2,1,0:T(8,128)(2,1)S(1)}, bf16[2,1024,256]{2,1,0:T(8,128)(2,1)}, u32[]{:S(2)}, u32[]{:S(2)}) collective-permute-start(bf16[2,1024,256]{2,1,0:T(8,128)(2,1)S(1)} %get-tuple-element.90), channel_id=1, source_target_pairs={{0,3},{1,0},{2,1},{3,2},{4,7},{5,4},{6,5},{7,6},{8,11},{9,8},{10,9... | collective-permute-start | bytes 3145736 | tf_op jit(solution)/shard_map/ppermute | solution.py:43
  158.3 16.0 %collective-permute-start.25 = (bf16[2,1024,256]{2,1,0:T(8,128)(2,1)}, bf16[2,1024,256]{2,1,0:T(8,128)(2,1)}, u32[]{:S(2)}, u32[]{:S(2)}) collective-permute-start(bf16[2,1024,256]{2,1,0:T(8,128)(2,1)} %add_convert_fusion), channel_id=1, source_target_pairs={{0,3},{1,0},{2,1},{3,2},{4,7},{5,4},{6,5},{7,6},{8,11},{9,8},{10,9... | collective-permute-start | bytes 3145736 | tf_op jit(solution)/shard_map/ppermute | solution.py:43
  160.3 12.1 %collective-permute-start.22 = (bf16[1024,256]{1,0:T(8,128)(2,1)}, bf16[1024,256]{1,0:T(8,128)(2,1)}, u32[]{:S(2)}, u32[]{:S(2)}) collective-permute-start(bf16[1024,256]{1,0:T(8,128)(2,1)} %get-tuple-element.88), channel_id=1, source_target_pairs={{0,1},{1,2},{2,3},{3,0},{4,5},{5,6},{6,7},{7,4},{8,9},{9,10},{10,1... | collective-permute-start | bytes 1572872 | tf_op jit(solution)/shard_map/ppermute | solution.py:43
  160.4 20.8 %collective-permute-start.21 = (bf16[1024,256]{1,0:T(8,128)(2,1)S(1)}, bf16[1024,256]{1,0:T(8,128)(2,1)S(1)}, u32[]{:S(2)}, u32[]{:S(2)}) collective-permute-start(bf16[1024,256]{1,0:T(8,128)(2,1)S(1)} %get-tuple-element.86), channel_id=1, source_target_pairs={{0,1},{1,2},{2,3},{3,0},{4,5},{5,6},{6,7},{7,4},{8,9},{9,10},{10,1... | collective-permute-start | bytes 1572872 | tf_op jit(solution)/shard_map/ppermute | solution.py:43
  160.5 2.8 %copy-start.2 = (bf16[3,256,4096]{2,1,0:T(8,128)(2,1)S(1)}, bf16[3,256,4096]{2,1,0:T(8,128)(2,1)}, u32[]{:S(2)}) copy-start(bf16[3,256,4096]{2,1,0:T(8,128)(2,1)} %weight_ref.7) | copy-start | bytes 18874372
  175.7 16.1 %collective-permute-start.26 = (bf16[1024,256]{1,0:T(8,128)(2,1)S(1)}, bf16[1024,256]{1,0:T(8,128)(2,1)S(1)}, u32[]{:S(2)}, u32[]{:S(2)}) collective-permute-start(bf16[1024,256]{1,0:T(8,128)(2,1)S(1)} %fusion.3), channel_id=1, source_target_pairs={{0,4},{1,5},{2,6},{3,7},{4,8},{5,9},{6,10},{7,11},{8,12},{9,13},{1... | collective-permute-start | bytes 1572872 | tf_op jit(solution)/shard_map/ppermute | solution.py:43
  175.8 19.0 %copy-start.9 = (bf16[1024,256]{1,0:T(8,128)(2,1)S(1)}, bf16[1024,256]{1,0:T(8,128)(2,1)}, u32[]{:S(2)}) copy-start(bf16[1024,256]{1,0:T(8,128)(2,1)} %param.22) | copy-start | bytes 1572868
  177.8 14.0 %collective-permute-start.27 = (bf16[1024,256]{1,0:T(8,128)(2,1)S(1)}, bf16[1024,256]{1,0:T(8,128)(2,1)S(1)}, u32[]{:S(2)}, u32[]{:S(2)}) collective-permute-start(bf16[1024,256]{1,0:T(8,128)(2,1)S(1)} %get-tuple-element.101), channel_id=1, source_target_pairs={{0,8},{1,9},{2,10},{3,11},{4,12},{5,13},{6,14},{7,15},{8,0},{9,1},... | collective-permute-start | bytes 1572872 | tf_op jit(solution)/shard_map/ppermute | solution.py:43
  179.8 15.0 %collective-permute-start.28 = (bf16[1024,256]{1,0:T(8,128)(2,1)S(1)}, bf16[1024,256]{1,0:T(8,128)(2,1)S(1)}, u32[]{:S(2)}, u32[]{:S(2)}) collective-permute-start(bf16[1024,256]{1,0:T(8,128)(2,1)S(1)} %get-tuple-element.102), channel_id=1, source_target_pairs={{0,12},{1,13},{2,14},{3,15},{4,0},{5,1},{6,2},{7,3},{8,4},{9,5},{1... | collective-permute-start | bytes 1572872 | tf_op jit(solution)/shard_map/ppermute | solution.py:43

commit v2 on v1

--- a/solution.py
+++ b/solution.py
@@ -474,24 +474,44 @@
     )(use, query, query_other, state, *sources)
 
 
-def pick_weights(w_out, table):
+def pick_weights(w_out, tables):
     depth, width = w_out.shape[1], 2 * HD
-
-    def kernel(table_ref, weight_ref, out_ref):
-        out_ref[0] = weight_ref[...]
+    groups = len(tables)
+
+    def kernel(*refs):
+        weight_ref, *out_refs = refs[groups:]
+        for i, out_ref in enumerate(out_refs):
+
+            @pl.when(pl.program_id(0) // 4 == i)
+            def _(out_ref=out_ref):
+                out_ref[0] = weight_ref[...]
+
+    def column(k, *table_refs):
+        place = table_refs[0][k % 4]
+        for i in range(1, groups):
+            place = jnp.where(k // 4 == i, table_refs[i][k % 4], place)
+        return (0, 0, place)
 
     return pl.pallas_call(
         kernel,
         grid_spec=pltpu.PrefetchScalarGridSpec(
-            num_scalar_prefetch=1,
-            grid=(4,),
-            in_specs=[pl.BlockSpec((MODALITIES, depth, width), lambda k, t: (0, 0, t[k]))],
-            out_specs=pl.BlockSpec((1, MODALITIES, depth, width), lambda k, t: (k, 0, 0, 0)),
+            num_scalar_prefetch=groups,
+            grid=(4 * groups,),
+            in_specs=[pl.BlockSpec((MODALITIES, depth, width), column)],
+            out_specs=tuple(
+                pl.BlockSpec(
+                    (1, MODALITIES, depth, width),
+                    lambda k, *t, i=i: (jnp.clip(k - 4 * i, 0, 3), 0, 0, 0),
+                )
+                for i in range(groups)
+            ),
         ),
-        out_shape=jax.ShapeDtypeStruct((4, MODALITIES, depth, width), BF),
+        out_shape=(jax.ShapeDtypeStruct((4, MODALITIES, depth, width), BF),) * groups,
         compiler_params=pltpu.CompilerParams(vmem_limit_bytes=VMEM_BYTES),
-        cost_estimate=pl.CostEstimate(flops=0, bytes_accessed=3 << 20, transcendentals=0),
-    )(table, w_out)
+        cost_estimate=pl.CostEstimate(
+            flops=0, bytes_accessed=groups * (3 << 20), transcendentals=0
+        ),
+    )(*tables, w_out)
 
 
 def output_part(own, other, weights, table, seg, sizes):
@@ -630,10 +650,18 @@
     far_use = jnp.stack([chip >= 2, chip >= 2]).astype(jnp.int32)
     queries = (query, query_other)
     state = attend_own(*queries, kv, kv_other, core)
-    here, plus, two, minus = (shard_table(np.full(4, offset), np.arange(4)) for offset in range(4))
-    kv_before, kv_other_after, state, w_two = lax.optimization_barrier(
-        (kv_before, kv_other_after, state, pick_weights(w_out, two))
-    )
+    order = [
+        [(2, 0), (2, 2), (2, 1), (2, 3)],
+        [(1, 1), (1, 3), (3, 0), (3, 2)],
+        [(1, 2), (1, 0), (3, 1), (3, 3)],
+        [(0, 0), (0, 2), (0, 1), (0, 3)],
+    ]
+    t_two, t_first, t_later, t_here = (shard_table(*zip(*blocks)) for blocks in order)
+    picked = pick_weights(w_out, [t_two, t_first, t_later])
+    kv_before, kv_other_after, state, *picked = lax.optimization_barrier(
+        (kv_before, kv_other_after, state, *picked)
+    )
+    w_two, w_first, w_later = picked
     kv_far = move_x(kv_before, 1)
     kv_other_far = move_x(kv_other_after, -1)
     state = attend_other(*queries, state, [kv_before, kv_other_after], near_use)
@@ -642,34 +670,30 @@
     other = swap_core(own_send)
 
     part = functools.partial(output_part, own, other)
-    two_low, two_high = part(w_two, two, seg, (2, 2))
+    two_low, two_high = part(w_two, t_two, seg, (2, 2))
     two_low = move(two_low, True, 1)
     two_high = move(two_high, True, -1)
-    first = jnp.concatenate([plus[2:], minus[:2]])
-    plus_high, minus_low = part(w_out, first, seg, (2, 2))
+    plus_high, minus_low = part(w_first, t_first, seg, (2, 2))
     plus_high = move(plus_high, True, 1)
     minus_low = move(minus_low, True, -1)
-    later = jnp.concatenate([plus[1:2], plus[:1], minus[2:]])
-    plus_1, plus_0, minus_high = part(w_out, later, seg, (0, 0, 2))
-    plus_1 = add(plus_1, two_low[1])
+    plus_2, plus_0, minus_high = part(w_later, t_later, seg, (0, 0, 2))
+    plus_2 = add(plus_2, two_low[1])
     plus_0 = add(plus_0, two_low[0])
     minus_high = add(minus_high, two_high)
-    plus_1, plus_0, minus_high, own, other = lax.optimization_barrier(
-        (plus_1, plus_0, minus_high, own, other)
-    )
-    here = output_part(own, other, w_out, here, seg, (0, 0, 0, 0))
-    plus_1 = move(plus_1, True, 1)
+    plus_2, plus_0, minus_high, own, other = lax.optimization_barrier(
+        (plus_2, plus_0, minus_high, own, other)
+    )
+    here = output_part(own, other, w_out, t_here, seg, (0, 0, 0, 0))
+    plus_2 = move(plus_2, True, 1)
     minus_high = move(minus_high, True, -1)
     plus_0 = move(plus_0, True, 1)
-    plus_1, plus_high, minus_low, minus_high = lax.optimization_barrier(
-        (plus_1, plus_high, minus_low, minus_high)
-    )
+    plus_2, plus_high, minus_low = lax.optimization_barrier((plus_2, plus_high, minus_low))
     sums = [
-        add(here[1], plus_1, minus_low[1]),
+        add(here[1], plus_2, minus_low[1]),
         add(here[2], plus_high[0], minus_high[0]),
         add(here[3], plus_high[1], minus_high[1]),
     ]
-    after, opposite, before = (move(part, False, step) for part, step in zip(sums, (1, 2, -1)))
+    opposite, after, before = (move(part, False, step) for part, step in zip(sums, (2, 1, -1)))
     plus_0, *_ = lax.optimization_barrier((plus_0, *sums))
     mine = lax.optimization_barrier(add(here[0], plus_0, minus_low[0]))
     return add(tokens, mine, after, opposite, before)

time: 198 us -> 195 us (0.985)
  other arithmetic: 17.5 us -> 12.3 us
  waiting for transfers between devices: 30.3 us -> 34.6 us
  local copies, waits for them, and re-layouts: 14.4 us -> 10.9 us
    ppermute x20, waiting for transfers between devices: 26 us -> 31.4 us  [move(): return lax.ppermute(array, AXES, plane_perm(first, step))]
    convert_element_type x6, other arithmetic: 10.6 us -> 6.78 us  [add(): return sum((array.astype(F32) for array in arrays)).astype(BF)]
    unnamed x34 -> x48, local copies, waits for them, and re-layouts: 12.5 us -> 9.74 us
  transfers between devices with their start and end apart: 29 -> 29, of which waited for: 11 -> 12; matrix products, arithmetic and copies ran while one was open for 9% -> 6% of each run, Pallas kernels for 30% -> 31%
where the time goes in v2:
time: 195 us; the launch traced here: 192 us
  Pallas kernels  79.8 us (41%)
  starting transfers between devices  54 us (28%)
  waiting for transfers between devices  34.6 us (18%)
  other arithmetic  12.3 us (6%)
  local copies, waits for them, and re-layouts  10.9 us (6%)
    ppermute x20, starting transfers between devices, move(): return lax.ppermute(array, AXES, plane_perm(first, step))  46.3 us
    pallas_call x4, Pallas kernels, project(): pl.pallas_call(kernel, in_specs=in_specs, out_specs=out_specs, scratch_sh...  33.6 us
    ppermute x20, waiting for transfers between devices, move(): return lax.ppermute(array, AXES, plane_perm(first, step))  31.4 us
    pallas_call x3, Pallas kernels, attend_other(): pl.pallas_call(kernel, grid_spec=pltpu.PrefetchScalarGridSpec(num_scalar_...  24.8 us
    pallas_call x4, Pallas kernels, output_part(): pl.pallas_call(kernel, in_specs=[pl.BlockSpec(memory_space=pltpu.SMEM)] *...  12.6 us
    unnamed x48, local copies, waits for them, and re-layouts  9.74 us
    ppermute x6, starting transfers between devices, move_x(): return lax.ppermute(array, 'ctx', pairs)  7.01 us
    convert_element_type x6, other arithmetic, add(): return sum((array.astype(F32) for array in arrays)).astype(BF)  6.78 us
  transfers between devices with their start and end apart: 29, of which 12 were waited for; matrix products, arithmetic and copies ran while one was open for 6% of the time, Pallas kernels for 31%

profile of v2, /device:TPU:6, one launch (start us, length us, event | category | flops | bytes accessed | tf_op | source)
XLA Modules:
  0.0 192.3 jit_solution(16746021104632095772)
XLA Ops:
  0.0 1.6 collective-permute-start
  1.6 1.7 collective-permute-start.2
  3.2 2.0 %collective-permute-start.4 = (bf16[1024,256]{1,0:T(8,128)(2,1)}, bf16[1024,256]{1,0:T(8,128)(2,1)}, u32[]{:S(2)}, u32[]{:S(2)}) collective-permute-start(bf16[1024,256]{1,0:T(8,128)(2,1)} %param.22), channel_id=1, source_target_pairs={{0,2},{1,3},{2,0},{3,1},{4,6},{5,7},{6,4},{7,5},{8,10},{9,11},{10,... | collective-permute-start | bytes 1572872 | tf_op jit(solution)/shard_map/ppermute | solution.py:43
  5.2 5.4 %collective-permute-done = bf16[1024,256]{1,0:T(8,128)(2,1)S(1)} collective-permute-done((bf16[1024,256]{1,0:T(8,128)(2,1)}, bf16[1024,256]{1,0:T(8,128)(2,1)S(1)}, u32[]{:S(2)}, u32[]{:S(2)}) %collective-permute-start) | collective-permute-done | bytes 524320 | tf_op jit(solution)/shard_map/ppermute | solution.py:43
  10.6 0.4 collective-permute-done.2
  11.0 2.4 %pad_maximum_fusion = (bf16[2,1024,256]{2,1,0:T(8,128)(2,1)}, bf16[2,1024,256]{2,1,0:T(8,128)(2,1)S(1)}) fusion(bf16[1,1024,256]{2,1,0:T(8,128)(2,1)} %bitcast.46, bf16[1,1024,256]{2,1,0:T(8,128)(2,1)S(1)} %bitcast.44, bf16[1,1024,256]{2,1,0:T(8,128)(2,1)S(1)} %bitcast.42), kind=kLoop, calls=%fused_computation.1 | loop fusion | flops 1048576 | bytes 3670016 | tf_op jit(solution)/shard_map/stack | solution.py:606
  13.4 2.0 %collective-permute-start.1 = (bf16[2,1024,256]{2,1,0:T(8,128)(2,1)S(1)}, bf16[2,1024,256]{2,1,0:T(8,128)(2,1)}, u32[]{:S(2)}, u32[]{:S(2)}) collective-permute-start(bf16[2,1024,256]{2,1,0:T(8,128)(2,1)S(1)} %get-tuple-element.120.refs_0_), channel_id=1, source_target_pairs={{0,4},{1,5},{2,6},{3,7},{4,8},{5,9},{6,10},{7,11},{8,12},{9,13},{1... | collective-permute-start | bytes 3145736 | tf_op jit(solution)/shard_map/ppermute | solution.py:43
  15.4 2.2 %collective-permute-start.3 = (bf16[2,1024,256]{2,1,0:T(8,128)(2,1)}, bf16[2,1024,256]{2,1,0:T(8,128)(2,1)S(1)}, u32[]{:S(2)}, u32[]{:S(2)}) collective-permute-start(bf16[2,1024,256]{2,1,0:T(8,128)(2,1)} %get-tuple-element.119), channel_id=1, source_target_pairs={{0,12},{1,13},{2,14},{3,15},{4,0},{5,1},{6,2},{7,3},{8,4},{9,5},{1... | collective-permute-start | bytes 3145736 | tf_op jit(solution)/shard_map/ppermute | solution.py:43
  17.6 2.6 %pad_maximum_fusion.2 = (bf16[2,1024,256]{2,1,0:T(8,128)(2,1)}, bf16[2,1024,256]{2,1,0:T(8,128)(2,1)S(1)}) fusion(bf16[1,1024,256]{2,1,0:T(8,128)(2,1)} %bitcast.6, bf16[1,1024,256]{2,1,0:T(8,128)(2,1)} %bitcast.43, bf16[1,1024,256]{2,1,0:T(8,128)(2,1)} %bitcast.45), kind=kLoop, calls=%fused_computation.3 | loop fusion | flops 1048576 | bytes 3670016 | tf_op jit(solution)/shard_map/stack | solution.py:611
  20.2 4.0 %collective-permute-start.6 = (bf16[2,1024,256]{2,1,0:T(8,128)(2,1)}, bf16[2,1024,256]{2,1,0:T(8,128)(2,1)}, u32[]{:S(2)}, u32[]{:S(2)}) collective-permute-start(bf16[2,1024,256]{2,1,0:T(8,128)(2,1)} %get-tuple-element.117), channel_id=1, source_target_pairs={{0,12},{1,13},{2,14},{3,15},{4,0},{5,1},{6,2},{7,3},{8,4},{9,5},{1... | collective-permute-start | bytes 3145736 | tf_op jit(solution)/shard_map/ppermute | solution.py:43
  24.2 0.2 select_reduce_fusion.1
  24.6 7.6 %shard_map.208 = (f32[1024,1]{1,0:T(8,128)S(1)}, f32[1024,768]{1,0:T(8,128)}) custom-call(s32[4]{0:T(128)S(1)} %get-tuple-element.124.table_ref, s32[7]{0:T(128)S(1)} %pad_add_fusion.seg_ref, bf16[2,1024,256]{2,1,0:T(8,128)(2,1)S(1)} %get-tuple-element.120.refs_0_, bf16[2,1024,256]{2,1,0:T(8,128)(2,1)S(1)} %get-tuple-element.118.refs_1_, ...), custom_call_target="tpu_custom_call" | custom-call | flops 2491416576 | bytes 6815744 | tf_op jit(solution)/shard_map/pallas_call | solution.py:248
  32.2 0.8 copy-done.6
  33.1 15.3 %collective-permute-start.9 = (bf16[1,1024,256]{2,1,0:T(8,128)(2,1)S(1)}, bf16[1,1024,256]{2,1,0:T(8,128)(2,1)S(1)}, u32[]{:S(2)}, u32[]{:S(2)}) collective-permute-start(bf16[1,1024,256]{2,1,0:T(8,128)(2,1)S(1)} %slice.31), channel_id=1, source_target_pairs={{0,12},{1,13},{2,14},{3,15},{4,0},{5,1},{6,2},{7,3},{8,4},{9,5},{1... | collective-permute-start | bytes 1572872 | tf_op jit(solution)/shard_map/ppermute | solution.py:43
  48.4 1.0 copy-done.7
  49.4 8.3 %shard_map.209 = (f32[1024,1]{1,0:T(8,128)S(1)}, f32[1024,768]{1,0:T(8,128)}) custom-call(s32[4]{0:T(128)S(1)} %get-tuple-element.123.table_ref, s32[7]{0:T(128)S(1)} %pad_add_fusion.seg_ref, bf16[2,1024,256]{2,1,0:T(8,128)(2,1)} %collective-permute-done.1.refs_0_, bf16[2,1024,256]{2,1,0:T(8,128)(2,1)S(1)} %collective-permute-done.3.refs_1_, ...), custom_call_target="tpu_custom_call" | custom-call | flops 2491416576 | bytes 6815744 | tf_op jit(solution)/shard_map/pallas_call | solution.py:248
  57.7 1.1 slice.30
  58.8 2.1 %collective-permute-start.7 = (bf16[1,1024,256]{2,1,0:T(8,128)(2,1)S(1)}, bf16[1,1024,256]{2,1,0:T(8,128)(2,1)S(1)}, u32[]{:S(2)}, u32[]{:S(2)}) collective-permute-start(bf16[1,1024,256]{2,1,0:T(8,128)(2,1)S(1)} %slice.30), channel_id=1, source_target_pairs={{0,12},{1,13},{2,14},{3,15},{4,0},{5,1},{6,2},{7,3},{8,4},{9,5},{1... | collective-permute-start | bytes 1572872 | tf_op jit(solution)/shard_map/ppermute | solution.py:43
  61.0 9.8 %shard_map.210 = (f32[1024,1]{1,0:T(8,128)S(1)}, f32[1024,768]{1,0:T(8,128)}) custom-call(s32[5]{0:T(128)S(1)} %broadcast_select_fusion.table_ref, s32[7]{0:T(128)S(1)} %pad_add_fusion.seg_ref, bf16[2,1024,256]{2,1,0:T(8,128)(2,1)} %collective-permute-done.8.refs_0_, bf16[2,1024,256]{2,1,0:T(8,128)(2,1)} %collective-permute-done.6.refs_1_, ...), custom_call_target="tpu_custom_call" | custom-call | flops 3114270720 | bytes 8519680 | tf_op jit(solution)/shard_map/pallas_call | solution.py:248
  70.9 7.8 %shard_map.211 = (bf16[1024,128]{1,0:T(8,128)(2,1)S(1)}, bf16[1024,256]{1,0:T(8,128)(2,1)S(1)}, bf16[1024,128]{1,0:T(8,128)(2,1)}, bf16[1024,256]{1,0:T(8,128)(2,1)S(1)}) custom-call(s32[3]{0:T(128)S(1)} %broadcast_select_fusion.1.table_ref, s32[7]{0:T(128)S(1)} %pad_add_fusion.seg_ref, bf16[2,1024,256]{2,1,0:T(8,128)(2,1)S(1)} %collective-permute-done.5.refs_0_, ...), custom_call_target="tpu_custom_call" | custom-call | flops 1868562432 | bytes 5111808 | tf_op jit(solution)/shard_map/pallas_call | solution.py:248
  78.7 0.1 collective-permute-start.12
  78.8 0.5 collective-permute-start.10
  79.3 0.5 collective-permute-start.11
  79.7 0.9 collective-permute-done.12.kv_other_ref
  80.7 0.8 collective-permute-start.13
  81.6 2.8 %copy-done = bf16[3,256,4096]{2,1,0:T(8,128)(2,1)S(1)} copy-done((bf16[3,256,4096]{2,1,0:T(8,128)(2,1)S(1)}, bf16[3,256,4096]{2,1,0:T(8,128)(2,1)}, u32[]{:S(2)}) %copy-start) | copy-done | bytes 6291480
  84.3 2.2 %shard_map.213 = (bf16[4,3,256,256]{3,2,1,0:T(8,128)(2,1)S(1)}, bf16[4,3,256,256]{3,2,1,0:T(8,128)(2,1)S(1)}, bf16[4,3,256,256]{3,2,1,0:T(8,128)(2,1)S(1)}) custom-call(s32[4]{0:T(128)S(1)} %get-tuple-element.121.refs_0_.table_ref, s32[4]{0:T(128)S(1)} %get-tuple-element.109.refs_1_.table_ref, s32[4]{0:T(128)S(1)} %broadcast_select_fusion.6.refs_2_.table_ref, ...), custom_call_target="tpu_custom_call" | custom-call | bytes 9437184 | tf_op jit(solution)/shard_map/pallas_call | solution.py:495
  86.5 0.7 collective-permute-start.15
  87.2 3.0 %collective-permute-start.14 = (bf16[1024,256]{1,0:T(8,128)(2,1)S(1)}, bf16[1024,256]{1,0:T(8,128)(2,1)}, u32[]{:S(2)}, u32[]{:S(2)}) collective-permute-start(bf16[1024,256]{1,0:T(8,128)(2,1)S(1)} %collective-permute-done.12.kv_other_ref), channel_id=1, source_target_pairs={{0,32},{16,48},{32,64},{48,80},{64,96},{80,112},{96,0},{112,16},{1... | collective-permute-start | bytes 1572872 | tf_op jit(solution)/shard_map/ppermute | solution.py:48
  90.2 6.6 %shard_map.212.before_ref = f32[4,144,512]{2,1,0:T(8,128)S(1)} custom-call(s32[1]{0:T(128)} %bitcast.core_ref, bf16[1024,128]{1,0:T(8,128)(2,1)S(1)} %get-tuple-element.72.query_ref, bf16[1024,128]{1,0:T(8,128)(2,1)S(1)} %collective-permute-done.10.query_other_ref, bf16[1024,256]{1,0:T(8,128)(2,1)S(1)} %get-tuple-element.74.kv_ref, ...), custom_call_target="tpu_custom_call" | custom-call | flops 1342177280 | bytes 4194304 | tf_op jit(solution)/shard_map/pallas_call | solution.py:353
  96.9 1.0 copy-done.8
  97.9 1.2 collective-permute-start.16
  99.1 0.8 collective-permute-start.17
  100.0 1.3 copy-done.9
  101.3 8.2 %shard_map.214.before_ref = f32[4,144,512]{2,1,0:T(8,128)S(1)} custom-call(s32[2]{0:T(128)S(1)} %add_convert_fusion.3.use_ref, bf16[1024,128]{1,0:T(8,128)(2,1)S(1)} %get-tuple-element.72.query_ref, bf16[1024,128]{1,0:T(8,128)(2,1)S(1)} %collective-permute-done.10.query_other_ref, f32[4,144,512]{2,1,0:T(8,128)S(1)} %copy-done.9, ...), custom_call_target="tpu_custom_call" | custom-call | flops 2147483648 | bytes 6291456 | tf_op jit(solution)/shard_map/pallas_call | solution.py:450
  109.5 8.1 %shard_map.215.before_ref = f32[4,144,512]{2,1,0:T(8,128)S(1)} custom-call(s32[2]{0:T(128)S(1)} %add_convert_fusion.3.use_ref, bf16[1024,128]{1,0:T(8,128)(2,1)S(1)} %get-tuple-element.72.query_ref, bf16[1024,128]{1,0:T(8,128)(2,1)S(1)} %collective-permute-done.10.query_other_ref, f32[4,144,512]{2,1,0:T(8,128)S(1)} %shard_map.214.before_ref, ...), custom_call_target="tpu_custom_call" | custom-call | flops 2147483648 | bytes 6291456 | tf_op jit(solution)/shard_map/pallas_call | solution.py:450
  117.7 0.7 collective-permute-done.17.refs_1_
  118.4 8.5 %shard_map.216 = (bf16[1024,128]{1,0:T(8,128)(2,1)S(1)}, bf16[1024,128]{1,0:T(8,128)(2,1)S(1)}) custom-call(s32[2]{0:T(128)S(1)} %add_convert_fusion.2.use_ref, bf16[1024,128]{1,0:T(8,128)(2,1)S(1)} %get-tuple-element.72.query_ref, bf16[1024,128]{1,0:T(8,128)(2,1)S(1)} %collective-permute-done.10.query_other_ref, f32[4,144,512]{2,1,0:T(8,128)S(1)} %shard_map.215.before_ref, ...), custom_call_target="tpu_custom_call" | custom-call | flops 2147483648 | bytes 6291456 | tf_op jit(solution)/shard_map/pallas_call | solution.py:450
  127.0 0.1 collective-permute-start.18
  127.1 1.5 collective-permute-done.18.other_ref
  128.6 3.0 %shard_map.218 = (bf16[2,1024,256]{2,1,0:T(8,128)(2,1)S(1)}, bf16[2,1024,256]{2,1,0:T(8,128)(2,1)S(1)}) custom-call(s32[4]{0:T(128)S(1)} %get-tuple-element.121.refs_0_.table_ref, s32[7]{0:T(128)S(1)} %pad_add_fusion.seg_ref, bf16[1024,128]{1,0:T(8,128)(2,1)S(1)} %get-tuple-element.91.own_ref, bf16[1024,128]{1,0:T(8,128)(2,1)S(1)} %collective-permute-done.18.other_ref, ...), custom_call_target="tpu_custom_call" | custom-call | bytes 1024 | tf_op jit(solution)/shard_map/pallas_call | solution.py:574
  131.6 6.5 %collective-permute-start.20 = (bf16[2,1024,256]{2,1,0:T(8,128)(2,1)S(1)}, bf16[2,1024,256]{2,1,0:T(8,128)(2,1)S(1)}, u32[]{:S(2)}, u32[]{:S(2)}) collective-permute-start(bf16[2,1024,256]{2,1,0:T(8,128)(2,1)S(1)} %get-tuple-element.90), channel_id=1, source_target_pairs={{0,3},{1,0},{2,1},{3,2},{4,7},{5,4},{6,5},{7,6},{8,11},{9,8},{10,9... | collective-permute-start | bytes 3145736 | tf_op jit(solution)/shard_map/ppermute | solution.py:43
  138.1 3.8 %shard_map.220 = (bf16[2,1024,256]{2,1,0:T(8,128)(2,1)}, bf16[2,1024,256]{2,1,0:T(8,128)(2,1)}) custom-call(s32[4]{0:T(128)S(1)} %get-tuple-element.109.refs_1_.table_ref, s32[7]{0:T(128)S(1)} %pad_add_fusion.seg_ref, bf16[1024,128]{1,0:T(8,128)(2,1)S(1)} %get-tuple-element.91.own_ref, bf16[1024,128]{1,0:T(8,128)(2,1)S(1)} %collective-permute-done.18.other_ref, ...), custom_call_target="tpu_custom_call" | custom-call | bytes 1024 | tf_op jit(solution)/shard_map/pallas_call | solution.py:574
  142.0 3.3 %collective-permute-start.24 = (bf16[2,1024,256]{2,1,0:T(8,128)(2,1)}, bf16[2,1024,256]{2,1,0:T(8,128)(2,1)}, u32[]{:S(2)}, u32[]{:S(2)}) collective-permute-start(bf16[2,1024,256]{2,1,0:T(8,128)(2,1)} %get-tuple-element.99), channel_id=1, source_target_pairs={{0,3},{1,0},{2,1},{3,2},{4,7},{5,4},{6,5},{7,6},{8,11},{9,8},{10,9... | collective-permute-start | bytes 3145736 | tf_op jit(solution)/shard_map/ppermute | solution.py:43
  145.3 2.9 %shard_map.217 = (bf16[1024,256]{1,0:T(8,128)(2,1)S(1)}, bf16[1024,256]{1,0:T(8,128)(2,1)S(1)}, bf16[2,1024,256]{2,1,0:T(8,128)(2,1)S(1)}) custom-call(s32[4]{0:T(128)S(1)} %broadcast_select_fusion.6.refs_2_.table_ref, s32[7]{0:T(128)S(1)} %pad_add_fusion.seg_ref, bf16[1024,128]{1,0:T(8,128)(2,1)S(1)} %get-tuple-element.91.own_ref, ...), custom_call_target="tpu_custom_call" | custom-call | bytes 1024 | tf_op jit(solution)/shard_map/pallas_call | solution.py:574
  148.2 2.3 %collective-permute-done.20 = bf16[2,1024,256]{2,1,0:T(8,128)(2,1)S(1)} collective-permute-done((bf16[2,1024,256]{2,1,0:T(8,128)(2,1)S(1)}, bf16[2,1024,256]{2,1,0:T(8,128)(2,1)S(1)}, u32[]{:S(2)}, u32[]{:S(2)}) %collective-permute-start.20) | collective-permute-done | bytes 1048608 | tf_op jit(solution)/shard_map/ppermute | solution.py:43
  150.4 0.3 add_convert_fusion
  150.7 3.4 %collective-permute-done.19 = bf16[2,1024,256]{2,1,0:T(8,128)(2,1)S(1)} collective-permute-done((bf16[2,1024,256]{2,1,0:T(8,128)(2,1)S(1)}, bf16[2,1024,256]{2,1,0:T(8,128)(2,1)S(1)}, u32[]{:S(2)}, u32[]{:S(2)}) %collective-permute-start.19) | collective-permute-done | bytes 1048608 | tf_op jit(solution)/shard_map/ppermute | solution.py:43
  154.1 1.1 fusion.4
  155.2 0.3 collective-permute-start.25
  155.5 1.7 collective-permute-start.22
  157.3 2.8 %copy-done.1 = bf16[3,256,4096]{2,1,0:T(8,128)(2,1)S(1)} copy-done((bf16[3,256,4096]{2,1,0:T(8,128)(2,1)S(1)}, bf16[3,256,4096]{2,1,0:T(8,128)(2,1)}, u32[]{:S(2)}) %copy-start.1) | copy-done | bytes 6291480
  160.1 3.0 %shard_map.219 = (bf16[1024,256]{1,0:T(8,128)(2,1)S(1)}, bf16[1024,256]{1,0:T(8,128)(2,1)S(1)}, bf16[1024,256]{1,0:T(8,128)(2,1)S(1)}, bf16[1024,256]{1,0:T(8,128)(2,1)S(1)}) custom-call(s32[4]{0:T(128)S(1)} %broadcast_select_fusion.7.table_ref, s32[7]{0:T(128)S(1)} %pad_add_fusion.seg_ref, bf16[1024,128]{1,0:T(8,128)(2,1)S(1)} %get-tuple-element.91.own_ref, ...), custom_call_target="tpu_custom_call" | custom-call | bytes 1024 | tf_op jit(solution)/shard_map/pallas_call | solution.py:574
  163.1 2.4 %collective-permute-done.23 = bf16[2,1024,256]{2,1,0:T(8,128)(2,1)} collective-permute-done((bf16[2,1024,256]{2,1,0:T(8,128)(2,1)}, bf16[2,1024,256]{2,1,0:T(8,128)(2,1)}, u32[]{:S(2)}, u32[]{:S(2)}) %collective-permute-start.23) | collective-permute-done | bytes 1048608 | tf_op jit(solution)/shard_map/ppermute | solution.py:43
  165.5 5.6 %collective-permute-done.22 = bf16[1024,256]{1,0:T(8,128)(2,1)} collective-permute-done((bf16[1024,256]{1,0:T(8,128)(2,1)}, bf16[1024,256]{1,0:T(8,128)(2,1)}, u32[]{:S(2)}, u32[]{:S(2)}) %collective-permute-start.22) | collective-permute-done | bytes 524320 | tf_op jit(solution)/shard_map/ppermute | solution.py:43
  171.1 1.4 fusion.3
  172.5 0.3 collective-permute-start.27
  172.8 6.1 %collective-permute-done.25 = bf16[2,1024,256]{2,1,0:T(8,128)(2,1)S(1)} collective-permute-done((bf16[2,1024,256]{2,1,0:T(8,128)(2,1)S(1)}, bf16[2,1024,256]{2,1,0:T(8,128)(2,1)S(1)}, u32[]{:S(2)}, u32[]{:S(2)}) %collective-permute-start.25) | collective-permute-done | bytes 1048608 | tf_op jit(solution)/shard_map/ppermute | solution.py:43
  178.8 1.6 fusion.2
  180.6 3.2 %collective-permute-start.28 = (bf16[1024,256]{1,0:T(8,128)(2,1)S(1)}, bf16[1024,256]{1,0:T(8,128)(2,1)S(1)}, u32[]{:S(2)}, u32[]{:S(2)}) collective-permute-start(bf16[1024,256]{1,0:T(8,128)(2,1)S(1)} %get-tuple-element.114), channel_id=1, source_target_pairs={{0,12},{1,13},{2,14},{3,15},{4,0},{5,1},{6,2},{7,3},{8,4},{9,5},{1... | collective-permute-start | bytes 1572872 | tf_op jit(solution)/shard_map/ppermute | solution.py:43
  183.8 0.1 collective-permute-done.21
  183.9 1.3 fusion
  185.2 5.8 %collective-permute-done.26 = bf16[1024,256]{1,0:T(8,128)(2,1)S(1)} collective-permute-done((bf16[1024,256]{1,0:T(8,128)(2,1)S(1)}, bf16[1024,256]{1,0:T(8,128)(2,1)S(1)}, u32[]{:S(2)}, u32[]{:S(2)}) %collective-permute-start.26) | collective-permute-done | bytes 524320 | tf_op jit(solution)/shard_map/ppermute | solution.py:43
  191.0 1.1 add_convert_fusion.1
  (77 shorter events, 0.8 us)
Async XLA Ops:
  0.0 10.6 %collective-permute-start = (bf16[1024,256]{1,0:T(8,128)(2,1)}, bf16[1024,256]{1,0:T(8,128)(2,1)S(1)}, u32[]{:S(2)}, u32[]{:S(2)}) collective-permute-start(bf16[1024,256]{1,0:T(8,128)(2,1)} %param.22), channel_id=1, source_target_pairs={{0,1},{1,2},{2,3},{3,0},{4,5},{5,6},{6,7},{7,4},{8,9},{9,10},{10,1... | collective-permute-start | bytes 1572872 | tf_op jit(solution)/shard_map/ppermute | solution.py:43
  1.6 9.4 %collective-permute-start.2 = (bf16[1024,256]{1,0:T(8,128)(2,1)}, bf16[1024,256]{1,0:T(8,128)(2,1)S(1)}, u32[]{:S(2)}, u32[]{:S(2)}) collective-permute-start(bf16[1024,256]{1,0:T(8,128)(2,1)} %param.22), channel_id=1, source_target_pairs={{0,3},{1,0},{2,1},{3,2},{4,7},{5,4},{6,5},{7,6},{8,11},{9,8},{10,9... | collective-permute-start | bytes 1572872 | tf_op jit(solution)/shard_map/ppermute | solution.py:43
  3.2 14.4 %collective-permute-start.4 = (bf16[1024,256]{1,0:T(8,128)(2,1)}, bf16[1024,256]{1,0:T(8,128)(2,1)}, u32[]{:S(2)}, u32[]{:S(2)}) collective-permute-start(bf16[1024,256]{1,0:T(8,128)(2,1)} %param.22), channel_id=1, source_target_pairs={{0,2},{1,3},{2,0},{3,1},{4,6},{5,7},{6,4},{7,5},{8,10},{9,11},{10,... | collective-permute-start | bytes 1572872 | tf_op jit(solution)/shard_map/ppermute | solution.py:43
  10.6 7.0 %copy-start.10 = (bf16[1024,256]{1,0:T(8,128)(2,1)}, bf16[1024,256]{1,0:T(8,128)(2,1)S(1)}, u32[]{:S(2)}) copy-start(bf16[1024,256]{1,0:T(8,128)(2,1)S(1)} %collective-permute-done) | copy-start | bytes 1572868
  11.0 6.6 %copy-start.11 = (bf16[1024,256]{1,0:T(8,128)(2,1)}, bf16[1024,256]{1,0:T(8,128)(2,1)S(1)}, u32[]{:S(2)}) copy-start(bf16[1024,256]{1,0:T(8,128)(2,1)S(1)} %collective-permute-done.2) | copy-start | bytes 1572868
  13.4 10.8 %copy-start.13 = (s32[1024]{0:T(1024)S(1)}, s32[1024]{0:T(1024)}, u32[]{:S(2)}) copy-start(s32[1024]{0:T(1024)} %param.23) | copy-start | bytes 12292
  13.4 11.0 %copy-start.18 = (s32[4]{0:T(128)S(1)}, s32[4]{0:T(128)}, u32[]{:S(2)}) copy-start(s32[4]{0:T(128)} %constant.223.clone) | copy-start | bytes 52
  13.4 11.0 %copy-start.19 = (s32[4]{0:T(128)S(1)}, s32[4]{0:T(128)}, u32[]{:S(2)}) copy-start(s32[4]{0:T(128)} %constant.225.clone) | copy-start | bytes 52
  13.4 11.0 %copy-start.20 = (s32[4]{0:T(128)S(1)}, s32[4]{0:T(128)}, u32[]{:S(2)}) copy-start(s32[4]{0:T(128)} %constant.226.clone) | copy-start | bytes 52
  13.4 19.6 %collective-permute-start.1 = (bf16[2,1024,256]{2,1,0:T(8,128)(2,1)S(1)}, bf16[2,1024,256]{2,1,0:T(8,128)(2,1)}, u32[]{:S(2)}, u32[]{:S(2)}) collective-permute-start(bf16[2,1024,256]{2,1,0:T(8,128)(2,1)S(1)} %get-tuple-element.120.refs_0_), channel_id=1, source_target_pairs={{0,4},{1,5},{2,6},{3,7},{4,8},{5,9},{6,10},{7,11},{8,12},{9,13},{1... | collective-permute-start | bytes 3145736 | tf_op jit(solution)/shard_map/ppermute | solution.py:43
  15.4 17.6 %collective-permute-start.3 = (bf16[2,1024,256]{2,1,0:T(8,128)(2,1)}, bf16[2,1024,256]{2,1,0:T(8,128)(2,1)S(1)}, u32[]{:S(2)}, u32[]{:S(2)}) collective-permute-start(bf16[2,1024,256]{2,1,0:T(8,128)(2,1)} %get-tuple-element.119), channel_id=1, source_target_pairs={{0,12},{1,13},{2,14},{3,15},{4,0},{5,1},{6,2},{7,3},{8,4},{9,5},{1... | collective-permute-start | bytes 3145736 | tf_op jit(solution)/shard_map/ppermute | solution.py:43
  20.2 37.5 %collective-permute-start.6 = (bf16[2,1024,256]{2,1,0:T(8,128)(2,1)}, bf16[2,1024,256]{2,1,0:T(8,128)(2,1)}, u32[]{:S(2)}, u32[]{:S(2)}) collective-permute-start(bf16[2,1024,256]{2,1,0:T(8,128)(2,1)} %get-tuple-element.117), channel_id=1, source_target_pairs={{0,12},{1,13},{2,14},{3,15},{4,0},{5,1},{6,2},{7,3},{8,4},{9,5},{1... | collective-permute-start | bytes 3145736 | tf_op jit(solution)/shard_map/ppermute | solution.py:43
  24.4 36.5 %collective-permute-start.8 = (bf16[2,1024,256]{2,1,0:T(8,128)(2,1)S(1)}, bf16[2,1024,256]{2,1,0:T(8,128)(2,1)}, u32[]{:S(2)}, u32[]{:S(2)}) collective-permute-start(bf16[2,1024,256]{2,1,0:T(8,128)(2,1)S(1)} %get-tuple-element.118.refs_1_), channel_id=1, source_target_pairs={{0,4},{1,5},{2,6},{3,7},{4,8},{5,9},{6,10},{7,11},{8,12},{9,13},{1... | collective-permute-start | bytes 3145736 | tf_op jit(solution)/shard_map/ppermute | solution.py:43
  32.2 0.8 copy-start.6
  33.0 37.8 %collective-permute-start.5 = (bf16[2,1024,256]{2,1,0:T(8,128)(2,1)}, bf16[2,1024,256]{2,1,0:T(8,128)(2,1)S(1)}, u32[]{:S(2)}, u32[]{:S(2)}) collective-permute-start(bf16[2,1024,256]{2,1,0:T(8,128)(2,1)} %collective-permute-done.1.refs_0_), channel_id=1, source_target_pairs={{0,4},{1,5},{2,6},{3,7},{4,8},{5,9},{6,10},{7,11},{8,12},{9,13},{1... | collective-permute-start | bytes 3145736 | tf_op jit(solution)/shard_map/ppermute | solution.py:43
  33.1 27.9 %collective-permute-start.9 = (bf16[1,1024,256]{2,1,0:T(8,128)(2,1)S(1)}, bf16[1,1024,256]{2,1,0:T(8,128)(2,1)S(1)}, u32[]{:S(2)}, u32[]{:S(2)}) collective-permute-start(bf16[1,1024,256]{2,1,0:T(8,128)(2,1)S(1)} %slice.31), channel_id=1, source_target_pairs={{0,12},{1,13},{2,14},{3,15},{4,0},{5,1},{6,2},{7,3},{8,4},{9,5},{1... | collective-permute-start | bytes 1572872 | tf_op jit(solution)/shard_map/ppermute | solution.py:43
  48.3 1.0 copy-start.7
  49.4 11.5 %copy-start.23 = (s32[3]{0:T(128)S(1)}, s32[3]{0:T(128)}, u32[]{:S(2)}) copy-start(s32[3]{0:T(128)} %constant.229.clone) | copy-start | bytes 40
  49.4 11.5 %copy-start.21 = (s32[5]{0:T(128)S(1)}, s32[5]{0:T(128)}, u32[]{:S(2)}) copy-start(s32[5]{0:T(128)} %constant.227.clone) | copy-start | bytes 64
  49.4 11.5 %copy-start.22 = (s32[5]{0:T(128)S(1)}, s32[5]{0:T(128)}, u32[]{:S(2)}) copy-start(s32[5]{0:T(128)} %constant.228.clone) | copy-start | bytes 64
  58.8 12.0 %collective-permute-start.7 = (bf16[1,1024,256]{2,1,0:T(8,128)(2,1)S(1)}, bf16[1,1024,256]{2,1,0:T(8,128)(2,1)S(1)}, u32[]{:S(2)}, u32[]{:S(2)}) collective-permute-start(bf16[1,1024,256]{2,1,0:T(8,128)(2,1)S(1)} %slice.30), channel_id=1, source_target_pairs={{0,12},{1,13},{2,14},{3,15},{4,0},{5,1},{6,2},{7,3},{8,4},{9,5},{1... | collective-permute-start | bytes 1572872 | tf_op jit(solution)/shard_map/ppermute | solution.py:43
  70.8 10.6 %copy-start.15 = (s32[4]{0:T(128)S(1)}, s32[4]{0:T(128)}, u32[]{:S(2)}) copy-start(s32[4]{0:T(128)} %constant.231.clone) | copy-start | bytes 52
  70.9 10.6 %copy-start.16 = (s32[4]{0:T(128)S(1)}, s32[4]{0:T(128)}, u32[]{:S(2)}) copy-start(s32[4]{0:T(128)} %constant.232.clone) | copy-start | bytes 52
  70.9 10.6 %copy-start.17 = (s32[4]{0:T(128)S(1)}, s32[4]{0:T(128)}, u32[]{:S(2)}) copy-start(s32[4]{0:T(128)} %constant.233.clone) | copy-start | bytes 52
  70.9 10.7 %copy-start.14 = (s32[4]{0:T(128)S(1)}, s32[4]{0:T(128)}, u32[]{:S(2)}) copy-start(s32[4]{0:T(128)} %constant.234.clone) | copy-start | bytes 52
  78.7 2.0 %collective-permute-start.12 = (bf16[1024,256]{1,0:T(8,128)(2,1)S(1)}, bf16[1024,256]{1,0:T(8,128)(2,1)S(1)}, u32[]{:S(2)}, u32[]{:S(2)}) collective-permute-start(bf16[1024,256]{1,0:T(8,128)(2,1)S(1)} %get-tuple-element.75), channel_id=1, source_target_pairs={{0,16},{16,0},{32,48},{48,32},{64,80},{80,64},{96,112},{112,96},{1... | collective-permute-start | bytes 1572872 | tf_op jit(solution)/shard_map/ppermute | solution.py:52
  78.8 11.5 %collective-permute-start.10 = (bf16[1024,128]{1,0:T(8,128)(2,1)}, bf16[1024,128]{1,0:T(8,128)(2,1)S(1)}, u32[]{:S(2)}, u32[]{:S(2)}) collective-permute-start(bf16[1024,128]{1,0:T(8,128)(2,1)} %get-tuple-element.73), channel_id=1, source_target_pairs={{0,16},{16,0},{32,48},{48,32},{64,80},{80,64},{96,112},{112,96},{1... | collective-permute-start | bytes 786440 | tf_op jit(solution)/shard_map/ppermute | solution.py:52
  79.3 18.6 %collective-permute-start.11 = (bf16[1024,256]{1,0:T(8,128)(2,1)S(1)}, bf16[1024,256]{1,0:T(8,128)(2,1)}, u32[]{:S(2)}, u32[]{:S(2)}) collective-permute-start(bf16[1024,256]{1,0:T(8,128)(2,1)S(1)} %get-tuple-element.74.kv_ref), channel_id=1, source_target_pairs={{0,32},{16,48},{32,64},{48,80},{64,96},{80,112},{96,0},{112,16},{1... | collective-permute-start | bytes 1572872 | tf_op jit(solution)/shard_map/ppermute | solution.py:48
  80.7 17.2 %collective-permute-start.13 = (bf16[1024,256]{1,0:T(8,128)(2,1)S(1)}, bf16[1024,256]{1,0:T(8,128)(2,1)}, u32[]{:S(2)}, u32[]{:S(2)}) collective-permute-start(bf16[1024,256]{1,0:T(8,128)(2,1)S(1)} %collective-permute-done.12.kv_other_ref), channel_id=1, source_target_pairs={{0,96},{16,112},{32,0},{48,16},{64,32},{80,48},{96,64},{112,80},{1... | collective-permute-start | bytes 1572872 | tf_op jit(solution)/shard_map/ppermute | solution.py:48
  81.6 2.8 %copy-start = (bf16[3,256,4096]{2,1,0:T(8,128)(2,1)S(1)}, bf16[3,256,4096]{2,1,0:T(8,128)(2,1)}, u32[]{:S(2)}) copy-start(bf16[3,256,4096]{2,1,0:T(8,128)(2,1)} %weight_ref.1) | copy-start | bytes 18874372
  86.5 10.3 %copy-start.2 = (bf16[4,3,256,256]{3,2,1,0:T(8,128)(2,1)}, bf16[4,3,256,256]{3,2,1,0:T(8,128)(2,1)S(1)}, u32[]{:S(2)}) copy-start(bf16[4,3,256,256]{3,2,1,0:T(8,128)(2,1)S(1)} %get-tuple-element.97.weight_ref) | copy-start | bytes 4718596
  86.5 10.3 %copy-start.4 = (bf16[4,3,256,256]{3,2,1,0:T(8,128)(2,1)}, bf16[4,3,256,256]{3,2,1,0:T(8,128)(2,1)S(1)}, u32[]{:S(2)}) copy-start(bf16[4,3,256,256]{3,2,1,0:T(8,128)(2,1)S(1)} %get-tuple-element.86.weight_ref) | copy-start | bytes 4718596
  86.5 22.9 %collective-permute-start.15 = (bf16[1024,256]{1,0:T(8,128)(2,1)S(1)}, bf16[1024,256]{1,0:T(8,128)(2,1)}, u32[]{:S(2)}, u32[]{:S(2)}) collective-permute-start(bf16[1024,256]{1,0:T(8,128)(2,1)S(1)} %get-tuple-element.74.kv_ref), channel_id=1, source_target_pairs={{0,96},{16,112},{32,0},{48,16},{64,32},{80,48},{96,64},{112,80},{1... | collective-permute-start | bytes 1572872 | tf_op jit(solution)/shard_map/ppermute | solution.py:48
  87.2 22.2 %collective-permute-start.14 = (bf16[1024,256]{1,0:T(8,128)(2,1)S(1)}, bf16[1024,256]{1,0:T(8,128)(2,1)}, u32[]{:S(2)}, u32[]{:S(2)}) collective-permute-start(bf16[1024,256]{1,0:T(8,128)(2,1)S(1)} %collective-permute-done.12.kv_other_ref), channel_id=1, source_target_pairs={{0,32},{16,48},{32,64},{48,80},{64,96},{80,112},{96,0},{112,16},{1... | collective-permute-start | bytes 1572872 | tf_op jit(solution)/shard_map/ppermute | solution.py:48
  96.9 1.0 copy-start.8
  97.9 19.8 %collective-permute-start.16 = (bf16[1024,256]{1,0:T(8,128)(2,1)}, bf16[1024,256]{1,0:T(8,128)(2,1)}, u32[]{:S(2)}, u32[]{:S(2)}) collective-permute-start(bf16[1024,256]{1,0:T(8,128)(2,1)} %collective-permute-done.11.refs_0_), channel_id=1, source_target_pairs={{0,32},{16,48},{32,64},{48,80},{64,96},{80,112},{96,0},{112,16},{1... | collective-permute-start | bytes 1572872 | tf_op jit(solution)/shard_map/ppermute | solution.py:48
  99.1 19.3 %collective-permute-start.17 = (bf16[1024,256]{1,0:T(8,128)(2,1)}, bf16[1024,256]{1,0:T(8,128)(2,1)}, u32[]{:S(2)}, u32[]{:S(2)}) collective-permute-start(bf16[1024,256]{1,0:T(8,128)(2,1)} %collective-permute-done.13.refs_1_), channel_id=1, source_target_pairs={{0,96},{16,112},{32,0},{48,16},{64,32},{80,48},{96,64},{112,80},{1... | collective-permute-start | bytes 1572872 | tf_op jit(solution)/shard_map/ppermute | solution.py:48
  100.0 1.3 copy-start.9
  117.6 10.9 %copy-start.5 = (bf16[4,3,256,256]{3,2,1,0:T(8,128)(2,1)S(1)}, bf16[4,3,256,256]{3,2,1,0:T(8,128)(2,1)}, u32[]{:S(2)}) copy-start(bf16[4,3,256,256]{3,2,1,0:T(8,128)(2,1)} %copy-done.4) | copy-start | bytes 4718596
  127.0 11.2 %copy-start.3 = (bf16[4,3,256,256]{3,2,1,0:T(8,128)(2,1)S(1)}, bf16[4,3,256,256]{3,2,1,0:T(8,128)(2,1)}, u32[]{:S(2)}) copy-start(bf16[4,3,256,256]{3,2,1,0:T(8,128)(2,1)} %copy-done.2) | copy-start | bytes 4718596
  127.0 1.6 collective-permute-start.18
  131.6 18.8 %collective-permute-start.20 = (bf16[2,1024,256]{2,1,0:T(8,128)(2,1)S(1)}, bf16[2,1024,256]{2,1,0:T(8,128)(2,1)S(1)}, u32[]{:S(2)}, u32[]{:S(2)}) collective-permute-start(bf16[2,1024,256]{2,1,0:T(8,128)(2,1)S(1)} %get-tuple-element.90), channel_id=1, source_target_pairs={{0,3},{1,0},{2,1},{3,2},{4,7},{5,4},{6,5},{7,6},{8,11},{9,8},{10,9... | collective-permute-start | bytes 3145736 | tf_op jit(solution)/shard_map/ppermute | solution.py:43
  138.1 16.0 %collective-permute-start.19 = (bf16[2,1024,256]{2,1,0:T(8,128)(2,1)S(1)}, bf16[2,1024,256]{2,1,0:T(8,128)(2,1)S(1)}, u32[]{:S(2)}, u32[]{:S(2)}) collective-permute-start(bf16[2,1024,256]{2,1,0:T(8,128)(2,1)S(1)} %get-tuple-element.87), channel_id=1, source_target_pairs={{0,1},{1,2},{2,3},{3,0},{4,5},{5,6},{6,7},{7,4},{8,9},{9,10},{10,1... | collective-permute-start | bytes 3145736 | tf_op jit(solution)/shard_map/ppermute | solution.py:43
  141.9 23.6 %collective-permute-start.23 = (bf16[2,1024,256]{2,1,0:T(8,128)(2,1)}, bf16[2,1024,256]{2,1,0:T(8,128)(2,1)}, u32[]{:S(2)}, u32[]{:S(2)}) collective-permute-start(bf16[2,1024,256]{2,1,0:T(8,128)(2,1)} %get-tuple-element.98), channel_id=1, source_target_pairs={{0,1},{1,2},{2,3},{3,0},{4,5},{5,6},{6,7},{7,4},{8,9},{9,10},{10,1... | collective-permute-start | bytes 3145736 | tf_op jit(solution)/shard_map/ppermute | solution.py:43
  142.0 23.5 %collective-permute-start.24 = (bf16[2,1024,256]{2,1,0:T(8,128)(2,1)}, bf16[2,1024,256]{2,1,0:T(8,128)(2,1)}, u32[]{:S(2)}, u32[]{:S(2)}) collective-permute-start(bf16[2,1024,256]{2,1,0:T(8,128)(2,1)} %get-tuple-element.99), channel_id=1, source_target_pairs={{0,3},{1,0},{2,1},{3,2},{4,7},{5,4},{6,5},{7,6},{8,11},{9,8},{10,9... | collective-permute-start | bytes 3145736 | tf_op jit(solution)/shard_map/ppermute | solution.py:43
  155.2 23.6 %collective-permute-start.25 = (bf16[2,1024,256]{2,1,0:T(8,128)(2,1)S(1)}, bf16[2,1024,256]{2,1,0:T(8,128)(2,1)S(1)}, u32[]{:S(2)}, u32[]{:S(2)}) collective-permute-start(bf16[2,1024,256]{2,1,0:T(8,128)(2,1)S(1)} %add_convert_fusion), channel_id=1, source_target_pairs={{0,3},{1,0},{2,1},{3,2},{4,7},{5,4},{6,5},{7,6},{8,11},{9,8},{10,9... | collective-permute-start | bytes 3145736 | tf_op jit(solution)/shard_map/ppermute | solution.py:43
  155.5 15.6 %collective-permute-start.22 = (bf16[1024,256]{1,0:T(8,128)(2,1)}, bf16[1024,256]{1,0:T(8,128)(2,1)}, u32[]{:S(2)}, u32[]{:S(2)}) collective-permute-start(bf16[1024,256]{1,0:T(8,128)(2,1)} %get-tuple-element.96), channel_id=1, source_target_pairs={{0,1},{1,2},{2,3},{3,0},{4,5},{5,6},{6,7},{7,4},{8,9},{9,10},{10,1... | collective-permute-start | bytes 1572872 | tf_op jit(solution)/shard_map/ppermute | solution.py:43
  157.3 26.6 %collective-permute-start.21 = (bf16[1024,256]{1,0:T(8,128)(2,1)S(1)}, bf16[1024,256]{1,0:T(8,128)(2,1)S(1)}, u32[]{:S(2)}, u32[]{:S(2)}) collective-permute-start(bf16[1024,256]{1,0:T(8,128)(2,1)S(1)} %get-tuple-element.94), channel_id=1, source_target_pairs={{0,1},{1,2},{2,3},{3,0},{4,5},{5,6},{6,7},{7,4},{8,9},{9,10},{10,1... | collective-permute-start | bytes 1572872 | tf_op jit(solution)/shard_map/ppermute | solution.py:43
  157.3 2.8 %copy-start.1 = (bf16[3,256,4096]{2,1,0:T(8,128)(2,1)S(1)}, bf16[3,256,4096]{2,1,0:T(8,128)(2,1)}, u32[]{:S(2)}) copy-start(bf16[3,256,4096]{2,1,0:T(8,128)(2,1)} %weight_ref.1) | copy-start | bytes 18874372
  172.5 12.7 %collective-permute-start.27 = (bf16[1024,256]{1,0:T(8,128)(2,1)S(1)}, bf16[1024,256]{1,0:T(8,128)(2,1)S(1)}, u32[]{:S(2)}, u32[]{:S(2)}) collective-permute-start(bf16[1024,256]{1,0:T(8,128)(2,1)S(1)} %fusion.3), channel_id=1, source_target_pairs={{0,8},{1,9},{2,10},{3,11},{4,12},{5,13},{6,14},{7,15},{8,0},{9,1},... | collective-permute-start | bytes 1572872 | tf_op jit(solution)/shard_map/ppermute | solution.py:43
  180.5 10.5 %copy-start.12 = (bf16[1024,256]{1,0:T(8,128)(2,1)S(1)}, bf16[1024,256]{1,0:T(8,128)(2,1)}, u32[]{:S(2)}) copy-start(bf16[1024,256]{1,0:T(8,128)(2,1)} %param.22) | copy-start | bytes 1572868
  180.5 10.5 %collective-permute-start.26 = (bf16[1024,256]{1,0:T(8,128)(2,1)S(1)}, bf16[1024,256]{1,0:T(8,128)(2,1)S(1)}, u32[]{:S(2)}, u32[]{:S(2)}) collective-permute-start(bf16[1024,256]{1,0:T(8,128)(2,1)S(1)} %get-tuple-element.113), channel_id=1, source_target_pairs={{0,4},{1,5},{2,6},{3,7},{4,8},{5,9},{6,10},{7,11},{8,12},{9,13},{1... | collective-permute-start | bytes 1572872 | tf_op jit(solution)/shard_map/ppermute | solution.py:43
  180.6 10.4 %collective-permute-start.28 = (bf16[1024,256]{1,0:T(8,128)(2,1)S(1)}, bf16[1024,256]{1,0:T(8,128)(2,1)S(1)}, u32[]{:S(2)}, u32[]{:S(2)}) collective-permute-start(bf16[1024,256]{1,0:T(8,128)(2,1)S(1)} %get-tuple-element.114), channel_id=1, source_target_pairs={{0,12},{1,13},{2,14},{3,15},{4,0},{5,1},{6,2},{7,3},{8,4},{9,5},{1... | collective-permute-start | bytes 1572872 | tf_op jit(solution)/shard_map/ppermute | solution.py:43

commit v3 on v2

--- a/solution.py
+++ b/solution.py
@@ -108,7 +108,7 @@
             query_ref, kv_ref, query_send_ref, kv_send_ref, *refs = refs
         else:
             squares_ref, out_ref, *refs = refs
-        held, normed, left, right, total, shrink, piece_sem, weight_sem, total_sem = refs
+        held, normed, left, right, total, passed, shrink, piece_sem, weight_sem, total_sem = refs
 
         spans = [pl.ds(row, SPAN) for row in range(0, rows, SPAN)]
         piece_copies = [
@@ -141,14 +141,14 @@
                     before_copies[g].append(
                         pltpu.make_async_copy(
                             before_ref.at[span, columns],
-                            total.at[span, columns],
+                            passed.at[span, columns],
                             total_sem.at[0, g, k],
                         )
                     )
                 if not last:
                     out_copies.append(
                         pltpu.make_async_copy(
-                            total.at[span, columns],
+                            passed.at[span, columns],
                             out_ref.at[span, columns],
                             total_sem.at[1, g, k],
                         )
@@ -191,7 +191,7 @@
             for copy in weight_copies[g] + before_copies[g]:
                 copy.wait()
             if has_before:
-                total[:, low:high] *= shrink[...]
+                total[:, low:high] = passed[:, low:high].astype(F32) * shrink[...]
             else:
                 total[:, low:high] = jnp.zeros((rows, high - low), F32)
 
@@ -202,6 +202,7 @@
 
             for_runs(seg_ref, rows, run)
             if not last:
+                passed[:, low:high] = total[:, low:high].astype(BF)
                 for copy in out_copies[g * len(spans) : (g + 1) * len(spans)]:
                     copy.start()
         for copy in out_copies:
@@ -242,7 +243,7 @@
     else:
         out_shape = (
             jax.ShapeDtypeStruct((rows, 1), F32),
-            jax.ShapeDtypeStruct((rows, 3 * width), F32),
+            jax.ShapeDtypeStruct((rows, out_width), BF),
         )
         out_specs = (vmem, pl.BlockSpec(memory_space=pl.ANY))
     return pl.pallas_call(
@@ -255,6 +256,7 @@
             pltpu.VMEM((MODALITIES, WINDOW, depth * width), BF),
             pltpu.VMEM((MODALITIES, depth * width, 3 * width), BF),
             pltpu.VMEM((rows, out_width), F32),
+            pltpu.VMEM((rows, out_width), BF),
             pltpu.VMEM((rows, 1), F32),
             pltpu.SemaphoreType.DMA((rows // SPAN, count)),
             pltpu.SemaphoreType.DMA((3, depth)),

time: 195 us -> 195 us (level)
  starting transfers between devices: 54 us -> 58.6 us
  waiting for transfers between devices: 34.6 us -> 31.2 us
    ppermute x20, starting transfers between devices: 46.3 us -> 50.4 us  [move(): return lax.ppermute(array, AXES, plane_perm(first, step))]
    ppermute x20, waiting for transfers between devices: 31.4 us -> 27.7 us  [move(): return lax.ppermute(array, AXES, plane_perm(first, step))]
    unnamed x48 -> x50, local copies, waits for them, and re-layouts: 9.74 us -> 10.5 us
  transfers between devices with their start and end apart: 29 -> 29, of which waited for: 12 -> 13; matrix products, arithmetic and copies ran while one was open for 6% -> 6% of each run, Pallas kernels for 31% -> 31%
where the time goes in v3:
time: 195 us; the launch traced here: 193 us
  Pallas kernels  78.7 us (40%)
  starting transfers between devices  58.6 us (30%)
  waiting for transfers between devices  31.2 us (16%)
  other arithmetic  12.2 us (6%)
  local copies, waits for them, and re-layouts  11.6 us (6%)
    ppermute x20, starting transfers between devices, move(): return lax.ppermute(array, AXES, plane_perm(first, step))  50.4 us
    pallas_call x4, Pallas kernels, project(): pl.pallas_call(kernel, in_specs=in_specs, out_specs=out_specs, scratch_sh...  32.5 us
    ppermute x20, waiting for transfers between devices, move(): return lax.ppermute(array, AXES, plane_perm(first, step))  27.7 us
    pallas_call x3, Pallas kernels, attend_other(): pl.pallas_call(kernel, grid_spec=pltpu.PrefetchScalarGridSpec(num_scalar_...  24.8 us
    pallas_call x4, Pallas kernels, output_part(): pl.pallas_call(kernel, in_specs=[pl.BlockSpec(memory_space=pltpu.SMEM)] *...  12.6 us
    unnamed x50, local copies, waits for them, and re-layouts  10.5 us
    ppermute x6, starting transfers between devices, move_x(): return lax.ppermute(array, 'ctx', pairs)  7.04 us
    convert_element_type x6, other arithmetic, add(): return sum((array.astype(F32) for array in arrays)).astype(BF)  6.78 us
  transfers between devices with their start and end apart: 29, of which 13 were waited for; matrix products, arithmetic and copies ran while one was open for 6% of the time, Pallas kernels for 31%

profile of v3, /device:TPU:6, one launch (start us, length us, event | category | flops | bytes accessed | tf_op | source)
XLA Modules:
  0.0 193.1 jit_solution(15215821050639296781)
XLA Ops:
  0.0 1.6 collective-permute-start
  1.6 1.7 collective-permute-start.2
  3.2 2.0 %collective-permute-start.4 = (bf16[1024,256]{1,0:T(8,128)(2,1)}, bf16[1024,256]{1,0:T(8,128)(2,1)S(1)}, u32[]{:S(2)}, u32[]{:S(2)}) collective-permute-start(bf16[1024,256]{1,0:T(8,128)(2,1)} %param.22), channel_id=1, source_target_pairs={{0,2},{1,3},{2,0},{3,1},{4,6},{5,7},{6,4},{7,5},{8,10},{9,11},{10,... | collective-permute-start | bytes 1572872 | tf_op jit(solution)/shard_map/ppermute | solution.py:43
  5.2 5.4 %collective-permute-done = bf16[1024,256]{1,0:T(8,128)(2,1)S(1)} collective-permute-done((bf16[1024,256]{1,0:T(8,128)(2,1)}, bf16[1024,256]{1,0:T(8,128)(2,1)S(1)}, u32[]{:S(2)}, u32[]{:S(2)}) %collective-permute-start) | collective-permute-done | bytes 524320 | tf_op jit(solution)/shard_map/ppermute | solution.py:43
  10.6 0.4 collective-permute-done.2
  11.0 2.4 %pad_maximum_fusion = (bf16[2,1024,256]{2,1,0:T(8,128)(2,1)}, bf16[2,1024,256]{2,1,0:T(8,128)(2,1)S(1)}) fusion(bf16[1,1024,256]{2,1,0:T(8,128)(2,1)} %bitcast.46, bf16[1,1024,256]{2,1,0:T(8,128)(2,1)S(1)} %bitcast.44, bf16[1,1024,256]{2,1,0:T(8,128)(2,1)S(1)} %bitcast.42), kind=kLoop, calls=%fused_computation.1 | loop fusion | flops 1048576 | bytes 3670016 | tf_op jit(solution)/shard_map/stack | solution.py:608
  13.4 4.0 %collective-permute-start.3 = (bf16[2,1024,256]{2,1,0:T(8,128)(2,1)}, bf16[2,1024,256]{2,1,0:T(8,128)(2,1)S(1)}, u32[]{:S(2)}, u32[]{:S(2)}) collective-permute-start(bf16[2,1024,256]{2,1,0:T(8,128)(2,1)} %get-tuple-element.119), channel_id=1, source_target_pairs={{0,12},{1,13},{2,14},{3,15},{4,0},{5,1},{6,2},{7,3},{8,4},{9,5},{1... | collective-permute-start | bytes 3145736 | tf_op jit(solution)/shard_map/ppermute | solution.py:43
  17.5 0.8 copy-done.13
  18.3 2.6 %pad_maximum_fusion.2 = (bf16[2,1024,256]{2,1,0:T(8,128)(2,1)}, bf16[2,1024,256]{2,1,0:T(8,128)(2,1)S(1)}) fusion(bf16[1,1024,256]{2,1,0:T(8,128)(2,1)} %bitcast.47, bf16[1,1024,256]{2,1,0:T(8,128)(2,1)} %bitcast.43, bf16[1,1024,256]{2,1,0:T(8,128)(2,1)} %bitcast.45), kind=kLoop, calls=%fused_computation.3 | loop fusion | flops 1048576 | bytes 3670016 | tf_op jit(solution)/shard_map/stack | solution.py:613
  20.8 4.0 %collective-permute-start.6 = (bf16[2,1024,256]{2,1,0:T(8,128)(2,1)}, bf16[2,1024,256]{2,1,0:T(8,128)(2,1)}, u32[]{:S(2)}, u32[]{:S(2)}) collective-permute-start(bf16[2,1024,256]{2,1,0:T(8,128)(2,1)} %get-tuple-element.117), channel_id=1, source_target_pairs={{0,12},{1,13},{2,14},{3,15},{4,0},{5,1},{6,2},{7,3},{8,4},{9,5},{1... | collective-permute-start | bytes 3145736 | tf_op jit(solution)/shard_map/ppermute | solution.py:43
  24.9 0.2 select_reduce_fusion.1
  25.3 7.6 %shard_map.208 = (f32[1024,1]{1,0:T(8,128)S(1)}, bf16[1024,768]{1,0:T(8,128)(2,1)}) custom-call(s32[4]{0:T(128)S(1)} %get-tuple-element.124.table_ref, s32[7]{0:T(128)S(1)} %pad_add_fusion.seg_ref, bf16[2,1024,256]{2,1,0:T(8,128)(2,1)S(1)} %get-tuple-element.120.refs_0_, bf16[2,1024,256]{2,1,0:T(8,128)(2,1)S(1)} %get-tuple-element.118.refs_1_, ...), custom_call_target="tpu_custom_call" | custom-call | flops 2491416576 | bytes 6815744 | tf_op jit(solution)/shard_map/pallas_call | solution.py:249
  32.9 0.8 copy-done.6
  33.7 15.2 %collective-permute-start.9 = (bf16[1,1024,256]{2,1,0:T(8,128)(2,1)S(1)}, bf16[1,1024,256]{2,1,0:T(8,128)(2,1)S(1)}, u32[]{:S(2)}, u32[]{:S(2)}) collective-permute-start(bf16[1,1024,256]{2,1,0:T(8,128)(2,1)S(1)} %slice.31), channel_id=1, source_target_pairs={{0,12},{1,13},{2,14},{3,15},{4,0},{5,1},{6,2},{7,3},{8,4},{9,5},{1... | collective-permute-start | bytes 1572872 | tf_op jit(solution)/shard_map/ppermute | solution.py:43
  49.0 1.0 copy-done.7
  50.0 8.0 %shard_map.209 = (f32[1024,1]{1,0:T(8,128)S(1)}, bf16[1024,768]{1,0:T(8,128)(2,1)}) custom-call(s32[4]{0:T(128)S(1)} %get-tuple-element.123.table_ref, s32[7]{0:T(128)S(1)} %pad_add_fusion.seg_ref, bf16[2,1024,256]{2,1,0:T(8,128)(2,1)} %collective-permute-done.1.refs_0_, bf16[2,1024,256]{2,1,0:T(8,128)(2,1)S(1)} %collective-permute-done.3.refs_1_, ...), custom_call_target="tpu_custom_call" | custom-call | flops 2491416576 | bytes 6815744 | tf_op jit(solution)/shard_map/pallas_call | solution.py:249
  58.0 1.1 slice.30
  59.1 2.1 %collective-permute-start.7 = (bf16[1,1024,256]{2,1,0:T(8,128)(2,1)S(1)}, bf16[1,1024,256]{2,1,0:T(8,128)(2,1)S(1)}, u32[]{:S(2)}, u32[]{:S(2)}) collective-permute-start(bf16[1,1024,256]{2,1,0:T(8,128)(2,1)S(1)} %slice.30), channel_id=1, source_target_pairs={{0,12},{1,13},{2,14},{3,15},{4,0},{5,1},{6,2},{7,3},{8,4},{9,5},{1... | collective-permute-start | bytes 1572872 | tf_op jit(solution)/shard_map/ppermute | solution.py:43
  61.3 9.5 %shard_map.210 = (f32[1024,1]{1,0:T(8,128)S(1)}, bf16[1024,768]{1,0:T(8,128)(2,1)}) custom-call(s32[5]{0:T(128)S(1)} %broadcast_select_fusion.table_ref, s32[7]{0:T(128)S(1)} %pad_add_fusion.seg_ref, bf16[2,1024,256]{2,1,0:T(8,128)(2,1)} %collective-permute-done.8.refs_0_, bf16[2,1024,256]{2,1,0:T(8,128)(2,1)} %collective-permute-done.6.refs_1_, ...), custom_call_target="tpu_custom_call" | custom-call | flops 3114270720 | bytes 8519680 | tf_op jit(solution)/shard_map/pallas_call | solution.py:249
  70.8 7.5 %shard_map.211 = (bf16[1024,128]{1,0:T(8,128)(2,1)S(1)}, bf16[1024,256]{1,0:T(8,128)(2,1)S(1)}, bf16[1024,128]{1,0:T(8,128)(2,1)}, bf16[1024,256]{1,0:T(8,128)(2,1)S(1)}) custom-call(s32[3]{0:T(128)S(1)} %broadcast_select_fusion.1.table_ref, s32[7]{0:T(128)S(1)} %pad_add_fusion.seg_ref, bf16[2,1024,256]{2,1,0:T(8,128)(2,1)S(1)} %collective-permute-done.5.refs_0_, ...), custom_call_target="tpu_custom_call" | custom-call | flops 1868562432 | bytes 5111808 | tf_op jit(solution)/shard_map/pallas_call | solution.py:249
  78.3 1.0 collective-permute-start.12
  79.3 0.1 collective-permute-start.10
  79.4 0.5 collective-permute-start.11
  79.9 0.9 collective-permute-done.12.kv_other_ref
  80.8 0.8 collective-permute-start.13
  81.8 2.8 %copy-done = bf16[3,256,4096]{2,1,0:T(8,128)(2,1)S(1)} copy-done((bf16[3,256,4096]{2,1,0:T(8,128)(2,1)S(1)}, bf16[3,256,4096]{2,1,0:T(8,128)(2,1)}, u32[]{:S(2)}) %copy-start) | copy-done | bytes 6291480
  84.5 2.2 %shard_map.213 = (bf16[4,3,256,256]{3,2,1,0:T(8,128)(2,1)S(1)}, bf16[4,3,256,256]{3,2,1,0:T(8,128)(2,1)S(1)}, bf16[4,3,256,256]{3,2,1,0:T(8,128)(2,1)S(1)}) custom-call(s32[4]{0:T(128)S(1)} %get-tuple-element.121.refs_0_.table_ref, s32[4]{0:T(128)S(1)} %get-tuple-element.109.refs_1_.table_ref, s32[4]{0:T(128)S(1)} %broadcast_select_fusion.6.refs_2_.table_ref, ...), custom_call_target="tpu_custom_call" | custom-call | bytes 9437184 | tf_op jit(solution)/shard_map/pallas_call | solution.py:497
  86.7 1.1 collective-permute-start.15
  87.8 2.6 %collective-permute-start.14 = (bf16[1024,256]{1,0:T(8,128)(2,1)S(1)}, bf16[1024,256]{1,0:T(8,128)(2,1)}, u32[]{:S(2)}, u32[]{:S(2)}) collective-permute-start(bf16[1024,256]{1,0:T(8,128)(2,1)S(1)} %collective-permute-done.12.kv_other_ref), channel_id=1, source_target_pairs={{0,32},{16,48},{32,64},{48,80},{64,96},{80,112},{96,0},{112,16},{1... | collective-permute-start | bytes 1572872 | tf_op jit(solution)/shard_map/ppermute | solution.py:48
  90.4 6.6 %shard_map.212.before_ref = f32[4,144,512]{2,1,0:T(8,128)S(1)} custom-call(s32[1]{0:T(128)} %bitcast.core_ref, bf16[1024,128]{1,0:T(8,128)(2,1)S(1)} %get-tuple-element.72.query_ref, bf16[1024,128]{1,0:T(8,128)(2,1)S(1)} %collective-permute-done.10.query_other_ref, bf16[1024,256]{1,0:T(8,128)(2,1)S(1)} %get-tuple-element.74.kv_ref, ...), custom_call_target="tpu_custom_call" | custom-call | flops 1342177280 | bytes 4194304 | tf_op jit(solution)/shard_map/pallas_call | solution.py:355
  97.1 1.0 copy-done.8
  98.1 1.2 collective-permute-start.16
  99.3 0.8 collective-permute-start.17
  100.2 1.3 copy-done.9
  101.5 8.1 %shard_map.214.before_ref = f32[4,144,512]{2,1,0:T(8,128)S(1)} custom-call(s32[2]{0:T(128)S(1)} %add_convert_fusion.3.use_ref, bf16[1024,128]{1,0:T(8,128)(2,1)S(1)} %get-tuple-element.72.query_ref, bf16[1024,128]{1,0:T(8,128)(2,1)S(1)} %collective-permute-done.10.query_other_ref, f32[4,144,512]{2,1,0:T(8,128)S(1)} %copy-done.9, ...), custom_call_target="tpu_custom_call" | custom-call | flops 2147483648 | bytes 6291456 | tf_op jit(solution)/shard_map/pallas_call | solution.py:452
  109.7 8.1 %shard_map.215.before_ref = f32[4,144,512]{2,1,0:T(8,128)S(1)} custom-call(s32[2]{0:T(128)S(1)} %add_convert_fusion.3.use_ref, bf16[1024,128]{1,0:T(8,128)(2,1)S(1)} %get-tuple-element.72.query_ref, bf16[1024,128]{1,0:T(8,128)(2,1)S(1)} %collective-permute-done.10.query_other_ref, f32[4,144,512]{2,1,0:T(8,128)S(1)} %shard_map.214.before_ref, ...), custom_call_target="tpu_custom_call" | custom-call | flops 2147483648 | bytes 6291456 | tf_op jit(solution)/shard_map/pallas_call | solution.py:452
  117.9 1.0 collective-permute-done.17.refs_1_
  118.8 8.5 %shard_map.216 = (bf16[1024,128]{1,0:T(8,128)(2,1)S(1)}, bf16[1024,128]{1,0:T(8,128)(2,1)S(1)}) custom-call(s32[2]{0:T(128)S(1)} %add_convert_fusion.2.use_ref, bf16[1024,128]{1,0:T(8,128)(2,1)S(1)} %get-tuple-element.72.query_ref, bf16[1024,128]{1,0:T(8,128)(2,1)S(1)} %collective-permute-done.10.query_other_ref, f32[4,144,512]{2,1,0:T(8,128)S(1)} %shard_map.215.before_ref, ...), custom_call_target="tpu_custom_call" | custom-call | flops 2147483648 | bytes 6291456 | tf_op jit(solution)/shard_map/pallas_call | solution.py:452
  127.5 1.5 collective-permute-done.18.other_ref
  129.0 3.0 %shard_map.218 = (bf16[2,1024,256]{2,1,0:T(8,128)(2,1)S(1)}, bf16[2,1024,256]{2,1,0:T(8,128)(2,1)S(1)}) custom-call(s32[4]{0:T(128)S(1)} %get-tuple-element.121.refs_0_.table_ref, s32[7]{0:T(128)S(1)} %pad_add_fusion.seg_ref, bf16[1024,128]{1,0:T(8,128)(2,1)S(1)} %get-tuple-element.91.own_ref, bf16[1024,128]{1,0:T(8,128)(2,1)S(1)} %collective-permute-done.18.other_ref, ...), custom_call_target="tpu_custom_call" | custom-call | bytes 1024 | tf_op jit(solution)/shard_map/pallas_call | solution.py:576
  132.0 7.0 %collective-permute-start.20 = (bf16[2,1024,256]{2,1,0:T(8,128)(2,1)S(1)}, bf16[2,1024,256]{2,1,0:T(8,128)(2,1)S(1)}, u32[]{:S(2)}, u32[]{:S(2)}) collective-permute-start(bf16[2,1024,256]{2,1,0:T(8,128)(2,1)S(1)} %get-tuple-element.90), channel_id=1, source_target_pairs={{0,3},{1,0},{2,1},{3,2},{4,7},{5,4},{6,5},{7,6},{8,11},{9,8},{10,9... | collective-permute-start | bytes 3145736 | tf_op jit(solution)/shard_map/ppermute | solution.py:43
  139.0 3.8 %shard_map.220 = (bf16[2,1024,256]{2,1,0:T(8,128)(2,1)}, bf16[2,1024,256]{2,1,0:T(8,128)(2,1)}) custom-call(s32[4]{0:T(128)S(1)} %get-tuple-element.109.refs_1_.table_ref, s32[7]{0:T(128)S(1)} %pad_add_fusion.seg_ref, bf16[1024,128]{1,0:T(8,128)(2,1)S(1)} %get-tuple-element.91.own_ref, bf16[1024,128]{1,0:T(8,128)(2,1)S(1)} %collective-permute-done.18.other_ref, ...), custom_call_target="tpu_custom_call" | custom-call | bytes 1024 | tf_op jit(solution)/shard_map/pallas_call | solution.py:576
  142.9 3.3 %collective-permute-start.24 = (bf16[2,1024,256]{2,1,0:T(8,128)(2,1)}, bf16[2,1024,256]{2,1,0:T(8,128)(2,1)}, u32[]{:S(2)}, u32[]{:S(2)}) collective-permute-start(bf16[2,1024,256]{2,1,0:T(8,128)(2,1)} %get-tuple-element.99), channel_id=1, source_target_pairs={{0,3},{1,0},{2,1},{3,2},{4,7},{5,4},{6,5},{7,6},{8,11},{9,8},{10,9... | collective-permute-start | bytes 3145736 | tf_op jit(solution)/shard_map/ppermute | solution.py:43
  146.2 2.9 %shard_map.217 = (bf16[1024,256]{1,0:T(8,128)(2,1)S(1)}, bf16[1024,256]{1,0:T(8,128)(2,1)S(1)}, bf16[2,1024,256]{2,1,0:T(8,128)(2,1)S(1)}) custom-call(s32[4]{0:T(128)S(1)} %broadcast_select_fusion.6.refs_2_.table_ref, s32[7]{0:T(128)S(1)} %pad_add_fusion.seg_ref, bf16[1024,128]{1,0:T(8,128)(2,1)S(1)} %get-tuple-element.91.own_ref, ...), custom_call_target="tpu_custom_call" | custom-call | bytes 1024 | tf_op jit(solution)/shard_map/pallas_call | solution.py:576
  149.0 2.3 %collective-permute-done.20 = bf16[2,1024,256]{2,1,0:T(8,128)(2,1)S(1)} collective-permute-done((bf16[2,1024,256]{2,1,0:T(8,128)(2,1)S(1)}, bf16[2,1024,256]{2,1,0:T(8,128)(2,1)S(1)}, u32[]{:S(2)}, u32[]{:S(2)}) %collective-permute-start.20) | collective-permute-done | bytes 1048608 | tf_op jit(solution)/shard_map/ppermute | solution.py:43
  151.3 0.3 add_convert_fusion
  151.6 3.4 %collective-permute-done.19 = bf16[2,1024,256]{2,1,0:T(8,128)(2,1)S(1)} collective-permute-done((bf16[2,1024,256]{2,1,0:T(8,128)(2,1)S(1)}, bf16[2,1024,256]{2,1,0:T(8,128)(2,1)S(1)}, u32[]{:S(2)}, u32[]{:S(2)}) %collective-permute-start.19) | collective-permute-done | bytes 1048608 | tf_op jit(solution)/shard_map/ppermute | solution.py:43
  155.0 1.1 fusion.4
  156.1 0.3 collective-permute-start.25
  156.4 1.7 collective-permute-start.22
  158.2 2.8 %copy-done.1 = bf16[3,256,4096]{2,1,0:T(8,128)(2,1)S(1)} copy-done((bf16[3,256,4096]{2,1,0:T(8,128)(2,1)S(1)}, bf16[3,256,4096]{2,1,0:T(8,128)(2,1)}, u32[]{:S(2)}) %copy-start.1) | copy-done | bytes 6291480
  160.9 3.0 %shard_map.219 = (bf16[1024,256]{1,0:T(8,128)(2,1)S(1)}, bf16[1024,256]{1,0:T(8,128)(2,1)S(1)}, bf16[1024,256]{1,0:T(8,128)(2,1)S(1)}, bf16[1024,256]{1,0:T(8,128)(2,1)S(1)}) custom-call(s32[4]{0:T(128)S(1)} %broadcast_select_fusion.7.table_ref, s32[7]{0:T(128)S(1)} %pad_add_fusion.seg_ref, bf16[1024,128]{1,0:T(8,128)(2,1)S(1)} %get-tuple-element.91.own_ref, ...), custom_call_target="tpu_custom_call" | custom-call | bytes 1024 | tf_op jit(solution)/shard_map/pallas_call | solution.py:576
  163.9 2.4 %collective-permute-done.23 = bf16[2,1024,256]{2,1,0:T(8,128)(2,1)} collective-permute-done((bf16[2,1024,256]{2,1,0:T(8,128)(2,1)}, bf16[2,1024,256]{2,1,0:T(8,128)(2,1)}, u32[]{:S(2)}, u32[]{:S(2)}) %collective-permute-start.23) | collective-permute-done | bytes 1048608 | tf_op jit(solution)/shard_map/ppermute | solution.py:43
  166.4 5.6 %collective-permute-done.22 = bf16[1024,256]{1,0:T(8,128)(2,1)} collective-permute-done((bf16[1024,256]{1,0:T(8,128)(2,1)}, bf16[1024,256]{1,0:T(8,128)(2,1)}, u32[]{:S(2)}, u32[]{:S(2)}) %collective-permute-start.22) | collective-permute-done | bytes 524320 | tf_op jit(solution)/shard_map/ppermute | solution.py:43
  172.0 1.4 fusion.3
  173.4 0.1 collective-permute-start.27
  173.5 0.4 collective-permute-done.25
  173.8 1.6 fusion.2
  175.5 7.1 %collective-permute-start.26 = (bf16[1024,256]{1,0:T(8,128)(2,1)S(1)}, bf16[1024,256]{1,0:T(8,128)(2,1)S(1)}, u32[]{:S(2)}, u32[]{:S(2)}) collective-permute-start(bf16[1024,256]{1,0:T(8,128)(2,1)S(1)} %get-tuple-element.113), channel_id=1, source_target_pairs={{0,4},{1,5},{2,6},{3,7},{4,8},{5,9},{6,10},{7,11},{8,12},{9,13},{1... | collective-permute-start | bytes 1572872 | tf_op jit(solution)/shard_map/ppermute | solution.py:43
  182.7 2.2 %collective-permute-done.21 = bf16[1024,256]{1,0:T(8,128)(2,1)S(1)} collective-permute-done((bf16[1024,256]{1,0:T(8,128)(2,1)S(1)}, bf16[1024,256]{1,0:T(8,128)(2,1)S(1)}, u32[]{:S(2)}, u32[]{:S(2)}) %collective-permute-start.21) | collective-permute-done | bytes 524320 | tf_op jit(solution)/shard_map/ppermute | solution.py:43
  184.8 1.3 fusion
  186.1 3.6 %collective-permute-done.26 = bf16[1024,256]{1,0:T(8,128)(2,1)S(1)} collective-permute-done((bf16[1024,256]{1,0:T(8,128)(2,1)S(1)}, bf16[1024,256]{1,0:T(8,128)(2,1)S(1)}, u32[]{:S(2)}, u32[]{:S(2)}) %collective-permute-start.26) | collective-permute-done | bytes 524320 | tf_op jit(solution)/shard_map/ppermute | solution.py:43
  189.7 2.1 %collective-permute-done.28 = bf16[1024,256]{1,0:T(8,128)(2,1)S(1)} collective-permute-done((bf16[1024,256]{1,0:T(8,128)(2,1)S(1)}, bf16[1024,256]{1,0:T(8,128)(2,1)S(1)}, u32[]{:S(2)}, u32[]{:S(2)}) %collective-permute-start.28) | collective-permute-done | bytes 524320 | tf_op jit(solution)/shard_map/ppermute | solution.py:43
  191.8 1.1 add_convert_fusion.1
  (79 shorter events, 0.8 us)
Async XLA Ops:
  0.0 10.6 %collective-permute-start = (bf16[1024,256]{1,0:T(8,128)(2,1)}, bf16[1024,256]{1,0:T(8,128)(2,1)S(1)}, u32[]{:S(2)}, u32[]{:S(2)}) collective-permute-start(bf16[1024,256]{1,0:T(8,128)(2,1)} %param.22), channel_id=1, source_target_pairs={{0,1},{1,2},{2,3},{3,0},{4,5},{5,6},{6,7},{7,4},{8,9},{9,10},{10,1... | collective-permute-start | bytes 1572872 | tf_op jit(solution)/shard_map/ppermute | solution.py:43
  1.6 9.4 %collective-permute-start.2 = (bf16[1024,256]{1,0:T(8,128)(2,1)}, bf16[1024,256]{1,0:T(8,128)(2,1)S(1)}, u32[]{:S(2)}, u32[]{:S(2)}) collective-permute-start(bf16[1024,256]{1,0:T(8,128)(2,1)} %param.22), channel_id=1, source_target_pairs={{0,3},{1,0},{2,1},{3,2},{4,7},{5,4},{6,5},{7,6},{8,11},{9,8},{10,9... | collective-permute-start | bytes 1572872 | tf_op jit(solution)/shard_map/ppermute | solution.py:43
  3.2 14.2 %collective-permute-start.4 = (bf16[1024,256]{1,0:T(8,128)(2,1)}, bf16[1024,256]{1,0:T(8,128)(2,1)S(1)}, u32[]{:S(2)}, u32[]{:S(2)}) collective-permute-start(bf16[1024,256]{1,0:T(8,128)(2,1)} %param.22), channel_id=1, source_target_pairs={{0,2},{1,3},{2,0},{3,1},{4,6},{5,7},{6,4},{7,5},{8,10},{9,11},{10,... | collective-permute-start | bytes 1572872 | tf_op jit(solution)/shard_map/ppermute | solution.py:43
  10.6 2.8 %copy-start.10 = (bf16[1024,256]{1,0:T(8,128)(2,1)}, bf16[1024,256]{1,0:T(8,128)(2,1)S(1)}, u32[]{:S(2)}) copy-start(bf16[1024,256]{1,0:T(8,128)(2,1)S(1)} %collective-permute-done) | copy-start | bytes 1572868
  11.0 2.4 %copy-start.11 = (bf16[1024,256]{1,0:T(8,128)(2,1)}, bf16[1024,256]{1,0:T(8,128)(2,1)S(1)}, u32[]{:S(2)}) copy-start(bf16[1024,256]{1,0:T(8,128)(2,1)S(1)} %collective-permute-done.2) | copy-start | bytes 1572868
  13.4 20.3 %collective-permute-start.3 = (bf16[2,1024,256]{2,1,0:T(8,128)(2,1)}, bf16[2,1024,256]{2,1,0:T(8,128)(2,1)S(1)}, u32[]{:S(2)}, u32[]{:S(2)}) collective-permute-start(bf16[2,1024,256]{2,1,0:T(8,128)(2,1)} %get-tuple-element.119), channel_id=1, source_target_pairs={{0,12},{1,13},{2,14},{3,15},{4,0},{5,1},{6,2},{7,3},{8,4},{9,5},{1... | collective-permute-start | bytes 3145736 | tf_op jit(solution)/shard_map/ppermute | solution.py:43
  17.4 16.2 %collective-permute-start.1 = (bf16[2,1024,256]{2,1,0:T(8,128)(2,1)S(1)}, bf16[2,1024,256]{2,1,0:T(8,128)(2,1)}, u32[]{:S(2)}, u32[]{:S(2)}) collective-permute-start(bf16[2,1024,256]{2,1,0:T(8,128)(2,1)S(1)} %get-tuple-element.120.refs_0_), channel_id=1, source_target_pairs={{0,4},{1,5},{2,6},{3,7},{4,8},{5,9},{6,10},{7,11},{8,12},{9,13},{1... | collective-permute-start | bytes 3145736 | tf_op jit(solution)/shard_map/ppermute | solution.py:43
  17.5 0.8 copy-start.13
  18.3 6.6 %copy-start.14 = (s32[1024]{0:T(1024)S(1)}, s32[1024]{0:T(1024)}, u32[]{:S(2)}) copy-start(s32[1024]{0:T(1024)} %param.23) | copy-start | bytes 12292
  18.3 6.8 %copy-start.19 = (s32[4]{0:T(128)S(1)}, s32[4]{0:T(128)}, u32[]{:S(2)}) copy-start(s32[4]{0:T(128)} %constant.226.clone) | copy-start | bytes 52
  18.3 6.8 %copy-start.20 = (s32[4]{0:T(128)S(1)}, s32[4]{0:T(128)}, u32[]{:S(2)}) copy-start(s32[4]{0:T(128)} %constant.225.clone) | copy-start | bytes 52
  18.3 6.8 %copy-start.21 = (s32[4]{0:T(128)S(1)}, s32[4]{0:T(128)}, u32[]{:S(2)}) copy-start(s32[4]{0:T(128)} %constant.223.clone) | copy-start | bytes 52
  20.8 37.2 %collective-permute-start.6 = (bf16[2,1024,256]{2,1,0:T(8,128)(2,1)}, bf16[2,1024,256]{2,1,0:T(8,128)(2,1)}, u32[]{:S(2)}, u32[]{:S(2)}) collective-permute-start(bf16[2,1024,256]{2,1,0:T(8,128)(2,1)} %get-tuple-element.117), channel_id=1, source_target_pairs={{0,12},{1,13},{2,14},{3,15},{4,0},{5,1},{6,2},{7,3},{8,4},{9,5},{1... | collective-permute-start | bytes 3145736 | tf_op jit(solution)/shard_map/ppermute | solution.py:43
  25.1 36.1 %collective-permute-start.8 = (bf16[2,1024,256]{2,1,0:T(8,128)(2,1)S(1)}, bf16[2,1024,256]{2,1,0:T(8,128)(2,1)}, u32[]{:S(2)}, u32[]{:S(2)}) collective-permute-start(bf16[2,1024,256]{2,1,0:T(8,128)(2,1)S(1)} %get-tuple-element.118.refs_1_), channel_id=1, source_target_pairs={{0,4},{1,5},{2,6},{3,7},{4,8},{5,9},{6,10},{7,11},{8,12},{9,13},{1... | collective-permute-start | bytes 3145736 | tf_op jit(solution)/shard_map/ppermute | solution.py:43
  32.9 0.8 copy-start.6
  33.7 37.1 %collective-permute-start.5 = (bf16[2,1024,256]{2,1,0:T(8,128)(2,1)}, bf16[2,1024,256]{2,1,0:T(8,128)(2,1)S(1)}, u32[]{:S(2)}, u32[]{:S(2)}) collective-permute-start(bf16[2,1024,256]{2,1,0:T(8,128)(2,1)} %collective-permute-done.1.refs_0_), channel_id=1, source_target_pairs={{0,4},{1,5},{2,6},{3,7},{4,8},{5,9},{6,10},{7,11},{8,12},{9,13},{1... | collective-permute-start | bytes 3145736 | tf_op jit(solution)/shard_map/ppermute | solution.py:43
  33.7 27.5 %collective-permute-start.9 = (bf16[1,1024,256]{2,1,0:T(8,128)(2,1)S(1)}, bf16[1,1024,256]{2,1,0:T(8,128)(2,1)S(1)}, u32[]{:S(2)}, u32[]{:S(2)}) collective-permute-start(bf16[1,1024,256]{2,1,0:T(8,128)(2,1)S(1)} %slice.31), channel_id=1, source_target_pairs={{0,12},{1,13},{2,14},{3,15},{4,0},{5,1},{6,2},{7,3},{8,4},{9,5},{1... | collective-permute-start | bytes 1572872 | tf_op jit(solution)/shard_map/ppermute | solution.py:43
  49.0 1.0 copy-start.7
  50.0 11.1 %copy-start.24 = (s32[3]{0:T(128)S(1)}, s32[3]{0:T(128)}, u32[]{:S(2)}) copy-start(s32[3]{0:T(128)} %constant.229.clone) | copy-start | bytes 40
  50.0 11.2 %copy-start.22 = (s32[5]{0:T(128)S(1)}, s32[5]{0:T(128)}, u32[]{:S(2)}) copy-start(s32[5]{0:T(128)} %constant.228.clone) | copy-start | bytes 64
  50.0 11.2 %copy-start.23 = (s32[5]{0:T(128)S(1)}, s32[5]{0:T(128)}, u32[]{:S(2)}) copy-start(s32[5]{0:T(128)} %constant.227.clone) | copy-start | bytes 64
  59.1 11.6 %collective-permute-start.7 = (bf16[1,1024,256]{2,1,0:T(8,128)(2,1)S(1)}, bf16[1,1024,256]{2,1,0:T(8,128)(2,1)S(1)}, u32[]{:S(2)}, u32[]{:S(2)}) collective-permute-start(bf16[1,1024,256]{2,1,0:T(8,128)(2,1)S(1)} %slice.30), channel_id=1, source_target_pairs={{0,12},{1,13},{2,14},{3,15},{4,0},{5,1},{6,2},{7,3},{8,4},{9,5},{1... | collective-permute-start | bytes 1572872 | tf_op jit(solution)/shard_map/ppermute | solution.py:43
  70.8 10.9 %copy-start.16 = (s32[4]{0:T(128)S(1)}, s32[4]{0:T(128)}, u32[]{:S(2)}) copy-start(s32[4]{0:T(128)} %constant.233.clone) | copy-start | bytes 52
  70.8 10.9 %copy-start.17 = (s32[4]{0:T(128)S(1)}, s32[4]{0:T(128)}, u32[]{:S(2)}) copy-start(s32[4]{0:T(128)} %constant.232.clone) | copy-start | bytes 52
  70.8 10.9 %copy-start.18 = (s32[4]{0:T(128)S(1)}, s32[4]{0:T(128)}, u32[]{:S(2)}) copy-start(s32[4]{0:T(128)} %constant.231.clone) | copy-start | bytes 52
  70.8 10.9 %copy-start.15 = (s32[4]{0:T(128)S(1)}, s32[4]{0:T(128)}, u32[]{:S(2)}) copy-start(s32[4]{0:T(128)} %constant.234.clone) | copy-start | bytes 52
  78.3 2.5 %collective-permute-start.12 = (bf16[1024,256]{1,0:T(8,128)(2,1)S(1)}, bf16[1024,256]{1,0:T(8,128)(2,1)S(1)}, u32[]{:S(2)}, u32[]{:S(2)}) collective-permute-start(bf16[1024,256]{1,0:T(8,128)(2,1)S(1)} %get-tuple-element.75), channel_id=1, source_target_pairs={{0,16},{16,0},{32,48},{48,32},{64,80},{80,64},{96,112},{112,96},{1... | collective-permute-start | bytes 1572872 | tf_op jit(solution)/shard_map/ppermute | solution.py:52
  79.3 11.1 %collective-permute-start.10 = (bf16[1024,128]{1,0:T(8,128)(2,1)}, bf16[1024,128]{1,0:T(8,128)(2,1)S(1)}, u32[]{:S(2)}, u32[]{:S(2)}) collective-permute-start(bf16[1024,128]{1,0:T(8,128)(2,1)} %get-tuple-element.73), channel_id=1, source_target_pairs={{0,16},{16,0},{32,48},{48,32},{64,80},{80,64},{96,112},{112,96},{1... | collective-permute-start | bytes 786440 | tf_op jit(solution)/shard_map/ppermute | solution.py:52
  79.4 18.6 %collective-permute-start.11 = (bf16[1024,256]{1,0:T(8,128)(2,1)S(1)}, bf16[1024,256]{1,0:T(8,128)(2,1)}, u32[]{:S(2)}, u32[]{:S(2)}) collective-permute-start(bf16[1024,256]{1,0:T(8,128)(2,1)S(1)} %get-tuple-element.74.kv_ref), channel_id=1, source_target_pairs={{0,32},{16,48},{32,64},{48,80},{64,96},{80,112},{96,0},{112,16},{1... | collective-permute-start | bytes 1572872 | tf_op jit(solution)/shard_map/ppermute | solution.py:48
  80.8 17.2 %collective-permute-start.13 = (bf16[1024,256]{1,0:T(8,128)(2,1)S(1)}, bf16[1024,256]{1,0:T(8,128)(2,1)}, u32[]{:S(2)}, u32[]{:S(2)}) collective-permute-start(bf16[1024,256]{1,0:T(8,128)(2,1)S(1)} %collective-permute-done.12.kv_other_ref), channel_id=1, source_target_pairs={{0,96},{16,112},{32,0},{48,16},{64,32},{80,48},{96,64},{112,80},{1... | collective-permute-start | bytes 1572872 | tf_op jit(solution)/shard_map/ppermute | solution.py:48
  81.7 2.8 %copy-start = (bf16[3,256,4096]{2,1,0:T(8,128)(2,1)S(1)}, bf16[3,256,4096]{2,1,0:T(8,128)(2,1)}, u32[]{:S(2)}) copy-start(bf16[3,256,4096]{2,1,0:T(8,128)(2,1)} %weight_ref.1) | copy-start | bytes 18874372
  86.7 10.3 %copy-start.2 = (bf16[4,3,256,256]{3,2,1,0:T(8,128)(2,1)}, bf16[4,3,256,256]{3,2,1,0:T(8,128)(2,1)S(1)}, u32[]{:S(2)}) copy-start(bf16[4,3,256,256]{3,2,1,0:T(8,128)(2,1)S(1)} %get-tuple-element.97.weight_ref) | copy-start | bytes 4718596
  86.7 10.3 %copy-start.4 = (bf16[4,3,256,256]{3,2,1,0:T(8,128)(2,1)}, bf16[4,3,256,256]{3,2,1,0:T(8,128)(2,1)S(1)}, u32[]{:S(2)}) copy-start(bf16[4,3,256,256]{3,2,1,0:T(8,128)(2,1)S(1)} %get-tuple-element.86.weight_ref) | copy-start | bytes 4718596
  86.7 22.9 %collective-permute-start.15 = (bf16[1024,256]{1,0:T(8,128)(2,1)S(1)}, bf16[1024,256]{1,0:T(8,128)(2,1)}, u32[]{:S(2)}, u32[]{:S(2)}) collective-permute-start(bf16[1024,256]{1,0:T(8,128)(2,1)S(1)} %get-tuple-element.74.kv_ref), channel_id=1, source_target_pairs={{0,96},{16,112},{32,0},{48,16},{64,32},{80,48},{96,64},{112,80},{1... | collective-permute-start | bytes 1572872 | tf_op jit(solution)/shard_map/ppermute | solution.py:48
  87.8 21.9 %collective-permute-start.14 = (bf16[1024,256]{1,0:T(8,128)(2,1)S(1)}, bf16[1024,256]{1,0:T(8,128)(2,1)}, u32[]{:S(2)}, u32[]{:S(2)}) collective-permute-start(bf16[1024,256]{1,0:T(8,128)(2,1)S(1)} %collective-permute-done.12.kv_other_ref), channel_id=1, source_target_pairs={{0,32},{16,48},{32,64},{48,80},{64,96},{80,112},{96,0},{112,16},{1... | collective-permute-start | bytes 1572872 | tf_op jit(solution)/shard_map/ppermute | solution.py:48
  97.1 1.0 copy-start.8
  98.1 19.8 %collective-permute-start.16 = (bf16[1024,256]{1,0:T(8,128)(2,1)}, bf16[1024,256]{1,0:T(8,128)(2,1)}, u32[]{:S(2)}, u32[]{:S(2)}) collective-permute-start(bf16[1024,256]{1,0:T(8,128)(2,1)} %collective-permute-done.11.refs_0_), channel_id=1, source_target_pairs={{0,32},{16,48},{32,64},{48,80},{64,96},{80,112},{96,0},{112,16},{1... | collective-permute-start | bytes 1572872 | tf_op jit(solution)/shard_map/ppermute | solution.py:48
  99.3 19.5 %collective-permute-start.17 = (bf16[1024,256]{1,0:T(8,128)(2,1)}, bf16[1024,256]{1,0:T(8,128)(2,1)}, u32[]{:S(2)}, u32[]{:S(2)}) collective-permute-start(bf16[1024,256]{1,0:T(8,128)(2,1)} %collective-permute-done.13.refs_1_), channel_id=1, source_target_pairs={{0,96},{16,112},{32,0},{48,16},{64,32},{80,48},{96,64},{112,80},{1... | collective-permute-start | bytes 1572872 | tf_op jit(solution)/shard_map/ppermute | solution.py:48
  100.2 1.3 copy-start.9
  117.8 11.1 %copy-start.5 = (bf16[4,3,256,256]{3,2,1,0:T(8,128)(2,1)S(1)}, bf16[4,3,256,256]{3,2,1,0:T(8,128)(2,1)}, u32[]{:S(2)}) copy-start(bf16[4,3,256,256]{3,2,1,0:T(8,128)(2,1)} %copy-done.4) | copy-start | bytes 4718596
  127.4 11.6 %copy-start.3 = (bf16[4,3,256,256]{3,2,1,0:T(8,128)(2,1)S(1)}, bf16[4,3,256,256]{3,2,1,0:T(8,128)(2,1)}, u32[]{:S(2)}) copy-start(bf16[4,3,256,256]{3,2,1,0:T(8,128)(2,1)} %copy-done.2) | copy-start | bytes 4718596
  127.4 1.6 collective-permute-start.18
  132.0 19.3 %collective-permute-start.20 = (bf16[2,1024,256]{2,1,0:T(8,128)(2,1)S(1)}, bf16[2,1024,256]{2,1,0:T(8,128)(2,1)S(1)}, u32[]{:S(2)}, u32[]{:S(2)}) collective-permute-start(bf16[2,1024,256]{2,1,0:T(8,128)(2,1)S(1)} %get-tuple-element.90), channel_id=1, source_target_pairs={{0,3},{1,0},{2,1},{3,2},{4,7},{5,4},{6,5},{7,6},{8,11},{9,8},{10,9... | collective-permute-start | bytes 3145736 | tf_op jit(solution)/shard_map/ppermute | solution.py:43
  139.0 16.0 %collective-permute-start.19 = (bf16[2,1024,256]{2,1,0:T(8,128)(2,1)S(1)}, bf16[2,1024,256]{2,1,0:T(8,128)(2,1)S(1)}, u32[]{:S(2)}, u32[]{:S(2)}) collective-permute-start(bf16[2,1024,256]{2,1,0:T(8,128)(2,1)S(1)} %get-tuple-element.87), channel_id=1, source_target_pairs={{0,1},{1,2},{2,3},{3,0},{4,5},{5,6},{6,7},{7,4},{8,9},{9,10},{10,1... | collective-permute-start | bytes 3145736 | tf_op jit(solution)/shard_map/ppermute | solution.py:43
  142.8 23.6 %collective-permute-start.23 = (bf16[2,1024,256]{2,1,0:T(8,128)(2,1)}, bf16[2,1024,256]{2,1,0:T(8,128)(2,1)}, u32[]{:S(2)}, u32[]{:S(2)}) collective-permute-start(bf16[2,1024,256]{2,1,0:T(8,128)(2,1)} %get-tuple-element.98), channel_id=1, source_target_pairs={{0,1},{1,2},{2,3},{3,0},{4,5},{5,6},{6,7},{7,4},{8,9},{9,10},{10,1... | collective-permute-start | bytes 3145736 | tf_op jit(solution)/shard_map/ppermute | solution.py:43
  142.9 23.5 %collective-permute-start.24 = (bf16[2,1024,256]{2,1,0:T(8,128)(2,1)}, bf16[2,1024,256]{2,1,0:T(8,128)(2,1)}, u32[]{:S(2)}, u32[]{:S(2)}) collective-permute-start(bf16[2,1024,256]{2,1,0:T(8,128)(2,1)} %get-tuple-element.99), channel_id=1, source_target_pairs={{0,3},{1,0},{2,1},{3,2},{4,7},{5,4},{6,5},{7,6},{8,11},{9,8},{10,9... | collective-permute-start | bytes 3145736 | tf_op jit(solution)/shard_map/ppermute | solution.py:43
  156.1 17.7 %collective-permute-start.25 = (bf16[2,1024,256]{2,1,0:T(8,128)(2,1)S(1)}, bf16[2,1024,256]{2,1,0:T(8,128)(2,1)S(1)}, u32[]{:S(2)}, u32[]{:S(2)}) collective-permute-start(bf16[2,1024,256]{2,1,0:T(8,128)(2,1)S(1)} %add_convert_fusion), channel_id=1, source_target_pairs={{0,3},{1,0},{2,1},{3,2},{4,7},{5,4},{6,5},{7,6},{8,11},{9,8},{10,9... | collective-permute-start | bytes 3145736 | tf_op jit(solution)/shard_map/ppermute | solution.py:43
  156.4 15.6 %collective-permute-start.22 = (bf16[1024,256]{1,0:T(8,128)(2,1)}, bf16[1024,256]{1,0:T(8,128)(2,1)}, u32[]{:S(2)}, u32[]{:S(2)}) collective-permute-start(bf16[1024,256]{1,0:T(8,128)(2,1)} %get-tuple-element.96), channel_id=1, source_target_pairs={{0,1},{1,2},{2,3},{3,0},{4,5},{5,6},{6,7},{7,4},{8,9},{9,10},{10,1... | collective-permute-start | bytes 1572872 | tf_op jit(solution)/shard_map/ppermute | solution.py:43
  158.1 26.7 %collective-permute-start.21 = (bf16[1024,256]{1,0:T(8,128)(2,1)S(1)}, bf16[1024,256]{1,0:T(8,128)(2,1)S(1)}, u32[]{:S(2)}, u32[]{:S(2)}) collective-permute-start(bf16[1024,256]{1,0:T(8,128)(2,1)S(1)} %get-tuple-element.94), channel_id=1, source_target_pairs={{0,1},{1,2},{2,3},{3,0},{4,5},{5,6},{6,7},{7,4},{8,9},{9,10},{10,1... | collective-permute-start | bytes 1572872 | tf_op jit(solution)/shard_map/ppermute | solution.py:43
  158.2 2.8 %copy-start.1 = (bf16[3,256,4096]{2,1,0:T(8,128)(2,1)S(1)}, bf16[3,256,4096]{2,1,0:T(8,128)(2,1)}, u32[]{:S(2)}) copy-start(bf16[3,256,4096]{2,1,0:T(8,128)(2,1)} %weight_ref.1) | copy-start | bytes 18874372
  173.4 12.7 %collective-permute-start.27 = (bf16[1024,256]{1,0:T(8,128)(2,1)S(1)}, bf16[1024,256]{1,0:T(8,128)(2,1)S(1)}, u32[]{:S(2)}, u32[]{:S(2)}) collective-permute-start(bf16[1024,256]{1,0:T(8,128)(2,1)S(1)} %fusion.3), channel_id=1, source_target_pairs={{0,8},{1,9},{2,10},{3,11},{4,12},{5,13},{6,14},{7,15},{8,0},{9,1},... | collective-permute-start | bytes 1572872 | tf_op jit(solution)/shard_map/ppermute | solution.py:43
  175.5 16.3 %copy-start.12 = (bf16[1024,256]{1,0:T(8,128)(2,1)S(1)}, bf16[1024,256]{1,0:T(8,128)(2,1)}, u32[]{:S(2)}) copy-start(bf16[1024,256]{1,0:T(8,128)(2,1)} %param.22) | copy-start | bytes 1572868
  175.5 14.3 %collective-permute-start.26 = (bf16[1024,256]{1,0:T(8,128)(2,1)S(1)}, bf16[1024,256]{1,0:T(8,128)(2,1)S(1)}, u32[]{:S(2)}, u32[]{:S(2)}) collective-permute-start(bf16[1024,256]{1,0:T(8,128)(2,1)S(1)} %get-tuple-element.113), channel_id=1, source_target_pairs={{0,4},{1,5},{2,6},{3,7},{4,8},{5,9},{6,10},{7,11},{8,12},{9,13},{1... | collective-permute-start | bytes 1572872 | tf_op jit(solution)/shard_map/ppermute | solution.py:43
  182.6 9.2 %collective-permute-start.28 = (bf16[1024,256]{1,0:T(8,128)(2,1)S(1)}, bf16[1024,256]{1,0:T(8,128)(2,1)S(1)}, u32[]{:S(2)}, u32[]{:S(2)}) collective-permute-start(bf16[1024,256]{1,0:T(8,128)(2,1)S(1)} %get-tuple-element.114), channel_id=1, source_target_pairs={{0,12},{1,13},{2,14},{3,15},{4,0},{5,1},{6,2},{7,3},{8,4},{9,5},{1... | collective-permute-start | bytes 1572872 | tf_op jit(solution)/shard_map/ppermute | solution.py:43
